TPU v7x, 768 devices: a whole 4x8x12 slice. The times are simulated.
768 devices in a mesh: slab: 64 (over y, x, core), sub: 12 (over z).
Axes of the slice: x: 4, y: 8, z: 12, core: 2. Of those that a mesh axis runs over, the one named last changes fastest.
Arguments:
- fine_old: float32 [4, 192, 98304], P(None, 'sub', 'slab'), may hold values from -1 to 1
- coarse: float32 [4, 96, 98304], P(None, 'sub', 'slab'), may hold values from -1 to 1
- box_pos: int32 [1536], replicated, may hold values from 0 to 3071, as said below
- old_owner: int32 [1536], replicated, may hold values from 0 to 63, as said below
- new_counts: int32 [64], replicated, may hold values from 1 to 48, 1536 in all
Outputs:
- fine_new: float32 [4, 192, 196608], P(None, 'sub', 'slab')
Inputs may be any that keep to these rules, and one draw needn't show every extreme that they name: `box_pos`: strictly increasing; the first box sits at 0 and the last at 3071. `old_owner`: any 64 consecutive boxes of the list have different old owners, so each old owner holds exactly 24 boxes and at most 1 boxes pass from one old owner to one new owner, a bound that is reached. `new_counts`: sums to 1536; some owner receives exactly 48 boxes.
All inputs are finite; a program needn't handle non-finite values.
Results may differ from a plain program's by a relative error of at most 0.00002.
Values sent between devices are 32-bit elements; how exact they have to be, the bound alone decides.
No kernel may reach another device: no remote copies, remote signals or barrier semaphores. Data moves between devices by JAX's collectives and lax.ppermute only.
A program may use at most 128 MiB of HBM per device.

v0:
```python
import jax
import jax.numpy as jnp
from jax import lax
from jax.sharding import PartitionSpec as P

BX = 64
BOX_DEV = 24
MOST = 48


ANISOTROPY = 0.3
TIME_STEP = 0.1
COUPLING = 1.5
SOLUTE_ONE = 0.6
SOLUTE_TWO = -0.4
DIFF_HEAT = 2.0
DIFF_ONE = 0.5
DIFF_TWO = 0.25
LATENT = 0.5
REJECT_ONE = 0.5
REJECT_TWO = -0.3


def extended(block, sides, width):
    for axis, dim in sides:
        count = lax.axis_size(axis)
        forward = [(i, i + 1) for i in range(count - 1)]
        backward = [(target, source) for source, target in forward]
        low = lax.ppermute(
            lax.slice_in_dim(block, block.shape[dim] - width, None, axis=dim), axis, forward
        )
        high = lax.ppermute(lax.slice_in_dim(block, 0, width, axis=dim), axis, backward)
        block = jnp.concatenate([low, block, high], axis=dim)
    return block


def advance(center, west_cells, east_cells, south_cells, north_cells):
    laplace = west_cells + east_cells + south_cells + north_cells - 4.0 * center
    phase = center[0]
    grad_x = 0.5 * (east_cells[0] - west_cells[0])
    grad_y = 0.5 * (north_cells[0] - south_cells[0])
    sq_x = grad_x * grad_x
    sq_y = grad_y * grad_y
    spread_sum = sq_x + sq_y + 1.0
    anisotropy = 1.0 + ANISOTROPY * (sq_x * sq_x - 6.0 * sq_x * sq_y + sq_y * sq_y) / (
        spread_sum * spread_sum
    )
    couple = center[1] + SOLUTE_ONE * center[2] + SOLUTE_TWO * center[3]
    wall_term = 1.0 - phase * phase
    phase_step = TIME_STEP * (
        anisotropy * anisotropy * laplace[0]
        + phase
        - phase * phase * phase
        - COUPLING * wall_term * wall_term * couple
    )
    heat_new = center[1] + TIME_STEP * DIFF_HEAT * laplace[1] + LATENT * phase_step
    first_solute = (
        center[2] + TIME_STEP * DIFF_ONE * laplace[2] + REJECT_ONE * center[2] * phase_step
    )
    second_solute = (
        center[3] + TIME_STEP * DIFF_TWO * laplace[3] + REJECT_TWO * center[3] * phase_step
    )
    return jnp.stack([phase + phase_step, heat_new, first_solute, second_solute])


def stored_block(position, per_device, device_count):
    total = per_device * device_count
    wrapped = position % total
    block = wrapped // per_device
    target = jnp.where(block % 2 == 1, block - 1, (block + device_count // 2 + 1) % device_count)
    return target * per_device + wrapped % per_device


def settle_rows(padded):
    at_bottom = lax.axis_index("sub") == 0
    at_top = lax.axis_index("sub") == lax.axis_size("sub") - 1
    lower_row = jnp.where(at_bottom, padded[:, 1:2], padded[:, :1])
    upper_row = jnp.where(at_top, padded[:, -2:-1], padded[:, -1:])
    return jnp.concatenate([lower_row, padded[:, 1:-1], upper_row], axis=1)


def pick_cols(shard_piece, targets):
    length = shard_piece.shape[2]
    inside = (targets >= 0) & (targets < length)
    taken = jnp.take(shard_piece, jnp.clip(targets, 0, length - 1), axis=2)
    return jnp.where(inside, taken, 0.0)


def body(fine_old, coarse, box_pos, old_owner, new_counts):
    slab_size = lax.axis_size("slab")
    my_index = lax.axis_index("slab")
    box_total = box_pos.shape[0]
    per_peer = (MOST + slab_size - 1) // slab_size
    half_width = BX // 2
    per_device = coarse.shape[2] // half_width
    positions = per_device * slab_size
    coarse_rows = coarse.shape[1]
    owners = jnp.arange(slab_size, dtype=jnp.int32)
    box_ids = jnp.arange(box_total, dtype=jnp.int32)
    starts = jnp.cumsum(new_counts) - new_counts
    new_owner = jnp.sum((box_ids[:, None] >= starts[None, :]).astype(jnp.int32), axis=1) - 1
    onehot = (old_owner[:, None] == owners[None, :]).astype(jnp.int32)
    earlier = jnp.cumsum(onehot, axis=0) - onehot
    old_slot = jnp.sum(earlier * onehot, axis=1)
    at_start = jnp.take(earlier, jnp.take(starts, new_owner), axis=0)
    pair_rank = old_slot - jnp.sum(at_start * onehot, axis=1)
    bucket = new_owner * per_peer + pair_rank
    cell_ids = jnp.arange(BX, dtype=jnp.int32)
    slot_old = jnp.arange(BOX_DEV, dtype=jnp.int32)
    mine_mask = (old_owner[None, :] == my_index) & (old_slot[None, :] == slot_old[:, None])
    my_bucket = jnp.sum(mine_mask.astype(jnp.int32) * bucket[None, :], axis=1)
    bucket_ids = jnp.arange(slab_size * per_peer, dtype=jnp.int32)
    matches = my_bucket[None, :] == bucket_ids[:, None]
    source_slot = jnp.sum(matches.astype(jnp.int32) * slot_old[None, :], axis=1)
    filled = jnp.any(matches, axis=1)
    send_cols = (source_slot[:, None] * BX + cell_ids[None, :]).reshape(-1)
    send_live = jnp.repeat(filled, BX)
    outgoing = jnp.where(send_live, jnp.take(fine_old, send_cols, axis=2), 0.0)
    incoming = lax.all_to_all(outgoing, "slab", split_axis=2, concat_axis=2, tiled=True)
    box_count = new_counts[my_index]
    first_box = starts[my_index]
    slot_ids = jnp.arange(MOST, dtype=jnp.int32)
    live_slots = slot_ids < box_count
    my_boxes = jnp.clip(first_box + slot_ids, 0, box_total - 1)
    from_bucket = jnp.take(old_owner, my_boxes) * per_peer + jnp.take(pair_rank, my_boxes)
    recv_cols = (from_bucket[:, None] * BX + cell_ids[None, :]).reshape(-1)
    live_cols = jnp.repeat(live_slots, BX)
    new_strip = jnp.where(live_cols, jnp.take(incoming, recv_cols, axis=2), 0.0)
    padded = settle_rows(extended(new_strip, (("sub", 1),), 1))
    center = padded[:, 1:-1]
    south_cells = padded[:, :-2]
    north_cells = padded[:, 2:]
    first_cols = center[:, :, 0::BX]
    last_cols = center[:, :, BX - 1 :: BX]
    pos_mine = jnp.take(box_pos, my_boxes)
    left_target = stored_block(pos_mine - 1, per_device, slab_size)
    right_target = stored_block(pos_mine + 1, per_device, slab_size)
    coarse_first = coarse[:, :, 0::half_width]
    coarse_last = coarse[:, :, half_width - 1 :: half_width]
    coarse_edges = jnp.concatenate([coarse_first, coarse_last], axis=1)
    shard_piece = lax.all_gather(coarse_edges, "slab", axis=2, tiled=True)
    left_coarse = pick_cols(shard_piece[:, coarse_rows:], left_target)
    right_coarse = pick_cols(shard_piece[:, :coarse_rows], right_target)
    last_live = lax.dynamic_slice_in_dim(last_cols, box_count - 1, 1, axis=2)
    own_edges = jnp.concatenate([first_cols[:, :, :1], last_live], axis=2)
    received = extended(own_edges, (("slab", 2),), 1)
    from_prev = received[:, :, :1]
    from_next = received[:, :, 3:]
    left_coarse = jnp.repeat(left_coarse, 2, axis=1)
    right_coarse = jnp.repeat(right_coarse, 2, axis=1)
    prev_pos = jnp.take(box_pos, jnp.clip(my_boxes - 1, 0, box_total - 1))
    next_pos = jnp.take(box_pos, jnp.clip(my_boxes + 1, 0, box_total - 1))
    fine_left = (my_boxes > 0) & (prev_pos == pos_mine - 1)
    fine_right = (my_boxes < box_total - 1) & (next_pos == pos_mine + 1)
    zero_col = jnp.zeros_like(from_prev)
    prev_last = jnp.concatenate([from_prev, last_cols[:, :, :-1]], axis=2)
    next_first = jnp.concatenate([first_cols[:, :, 1:], zero_col], axis=2)
    next_first = jnp.where(slot_ids == box_count - 1, from_next, next_first)
    left_val = jnp.where(fine_left, prev_last, jnp.where(pos_mine > 0, left_coarse, first_cols))
    right_val = jnp.where(
        fine_right, next_first, jnp.where(pos_mine < positions - 1, right_coarse, last_cols)
    )
    col_ids = jnp.arange(MOST * BX, dtype=jnp.int32) % BX
    shifted_west = jnp.concatenate([zero_col, center[:, :, :-1]], axis=2)
    shifted_east = jnp.concatenate([center[:, :, 1:], zero_col], axis=2)
    west_cells = jnp.where(col_ids == 0, jnp.repeat(left_val, BX, axis=2), shifted_west)
    east_cells = jnp.where(col_ids == BX - 1, jnp.repeat(right_val, BX, axis=2), shifted_east)
    stepped = advance(center, west_cells, east_cells, south_cells, north_cells)
    return jnp.where(live_cols, stepped, 0.0)


def solution(mesh):
    placed = (P(None, "sub", "slab"), P(None, "sub", "slab"), P(), P(), P())
    return jax.shard_map(
        body, mesh=mesh, in_specs=placed, out_specs=P(None, "sub", "slab"), check_vma=False
    )
```

profile of v0, /device:TPU:224, one launch (start us, length us, event | category | flops | bytes accessed | tf_op | source)
XLA Modules:
  0.0 311.3 jit_solution(7113876541220575427)
XLA Ops:
  0.0 0.8 copy.152
  1.0 0.7 sub.91
  1.8 0.7 fusion.44
  2.4 0.7 fusion.43
  3.2 0.7 fusion.42
  3.9 0.7 broadcast_compare_fusion
  4.6 0.7 fusion.3
  5.3 18.1 %reduce-window.20 = s32[64,12,128]{2,1,0:T(8,128)S(1)} reduce-window(s32[64,12,128]{2,1,0:T(8,128)S(1)} %fusion.3, s32[]{:T(128)} %constant.198.clone.1), window={size=1x1x128 pad=0_0x0_0x127_0}, to_apply=%region_1.3 | reduce-window | flops 12484608 | bytes 786436 | tf_op jit(solution)/shard_map/reduce-window.1
  23.5 0.2 slice.212
  23.7 0.3 copy.153
  24.1 0.2 broadcast_add_fusion
  24.3 0.3 copy.165
  24.6 1.0 bitcast_subtract_fusion
  25.6 4.3 %fusion.25 = (s32[1536]{0:T(1024)S(1)}, s32[1536,1]{0,1:T(1,128)S(1)}) fusion(s32[]{:T(128)} %bitcast.64, s32[]{:T(128)} %bitcast.65, s32[]{:T(128)} %bitcast.66, s32[]{:T(128)} %bitcast.67, s32[]{:T(128)} %bitcast.68, s32[]{:T(128)} %bitcast.70, s32[]{:T(128)} %bitcast.69, s32[1536]{0:T(1024)S(1)} %get-tuple-element.99, s32[1536]{0:T(1024)S(1)} %get-tuple-element.98), kind=kLoop, calls=%fused_computation.153 | loop fusion | flops 21504 | bytes 24604 | tf_op jit(solution)/shard_map/jit(_take)/gather | solution.py:105
  29.9 1.1 compare_reduce_fusion.56
  31.0 0.7 fusion.41
  31.7 35.6 %compare_and_fusion.2 = (pred[1536]{0:T(1024)(128)(4,1)S(1)}, s32[1536]{0:T(1024)S(1)}) fusion(s32[1536]{0:T(1024)S(1)} %convert_reduce_fusion, pred[1536]{0:T(1024)(128)(4,1)S(1)} %get-tuple-element.65, pred[1536]{0:T(1024)(128)(4,1)S(1)} %get-tuple-element.63, pred[1536]{0:T(1024)(128)(4,1)S(1)} %get-tuple-element.64, ...), kind=kLoop, calls=%fused_computation.152 | loop fusion | flops 109056 | bytes 107748 | tf_op jit(solution)/shard_map/jit(_take)/and | solution.py:105
  67.4 2.6 gather_fusion
  70.0 1.5 select_reduce_fusion
  72.1 2.8 copy.156
  75.1 32.0 %gather_fusion.1 = f32[4096,4,16]{2,1,0:T(4,128)} fusion(f32[4,16,1536]{1,0,2:T(4,128)} %copy.156, s32[4096]{0:T(1024)S(1)} %broadcast_clamp_fusion), kind=kCustom, calls=%fused_computation.8 | custom fusion | bytes 2113536 | tf_op jit(solution)/shard_map/jit(_take)/gather | solution.py:118
  107.2 21.8 %fusion.45 = f32[4096,4,16]{2,1,0:T(4,128)} fusion(f32[4096,4,16]{2,1,0:T(4,128)} %gather_fusion.1, pred[4096]{0:T(1024)(128)(4,1)S(1)} %compare_and_fusion, pred[4096]{0:T(1024)(128)(4,1)S(1)} %reshape.232), kind=kLoop, calls=%fused_computation.222 | loop fusion | flops 524288 | bytes 2105344
  129.0 8.9 %reshape.611 = f32[64,1,4096]{2,1,0:T(1,128)} reshape(f32[4096,4,16]{2,1,0:T(4,128)} %fusion.45) | data formatting | bytes 2097152
  137.9 10.3 %all-to-all-start = ((f32[64,1,4096]{2,1,0:T(1,128)}), f32[64,1,4096]{2,1,0:T(1,128)S(1)}, u32[]{:S(2)}, u32[]{:S(2)}) async-start(f32[64,1,4096]{2,1,0:T(1,128)} %reshape.611), calls=%async_computation | async-start | bytes 2097152 | tf_op jit(solution)/shard_map/all_to_all | solution.py:119
  148.3 0.6 dynamic_slice.9
  148.9 0.6 compare_select_fusion.18
  149.5 0.8 gather_fusion.3
  150.2 0.8 gather_fusion.4
  151.0 0.6 fusion.33
  151.8 1.2 slice.105
  153.0 1.2 slice.104
  154.2 0.6 compare_select_fusion.15
  154.8 0.7 iota_compare_fusion.6
  155.8 64.4 %all_gather.3 = f32[4,16,3072]{1,0,2:T(4,128)S(1)} all-gather(f32[4,16,48]{1,0,2:T(4,128)S(1)} %copy.158), channel_id=1, replica_groups=mesh['slab'=64,'sub'=12] {'slab'}, dimensions={2}, use_global_device_ids=true | all-gather | bytes 798720 | tf_op jit(solution)/shard_map/all_gather | solution.py:141
  220.2 6.4 %fusion.38 = (f32[4,8,3072]{1,0,2:T(4,128)}, f32[4,8,3072]{1,0,2:T(4,128)}) fusion(f32[4,16,3072]{1,0,2:T(4,128)S(1)} %all_gather.3), kind=kLoop, calls=%fused_computation.215 | loop fusion | bytes 1572864 | tf_op jit(solution)/shard_map/slice | solution.py:142
  226.6 0.8 gather_fusion.6
  227.4 0.8 gather_fusion.5
  228.2 0.8 gather_fusion.8
  228.9 0.6 compare_and_fusion.9
  229.5 0.6 compare_and_fusion.6
  230.2 3.4 %gather_fusion.7 = f32[48,4,8]{2,1,0:T(4,128)S(1)} fusion(f32[4,8,3072]{1,0,2:T(4,128)} %get-tuple-element.88, s32[1024]{0:T(1024)S(1)} %pad_clamp_fusion.3), kind=kCustom, calls=%fused_computation.1.clone | custom fusion | bytes 12480 | tf_op jit(solution)/shard_map/jit(_take)/gather | solution.py:85
  233.6 0.2 bitcast_select_fusion.1
  235.2 3.4 %gather_fusion.9 = f32[48,4,8]{2,1,0:T(4,128)S(1)} fusion(f32[4,8,3072]{1,0,2:T(4,128)} %get-tuple-element.87, s32[1024]{0:T(1024)S(1)} %pad_clamp_fusion.1), kind=kCustom, calls=%fused_computation.6.clone | custom fusion | bytes 12480 | tf_op jit(solution)/shard_map/jit(_take)/gather | solution.py:85
  238.6 0.2 bitcast_select_fusion
  238.9 0.5 broadcast.942
  239.5 3.3 %reduce.120 = f32[64,4096]{1,0:T(8,128)S(1)} reduce(f32[64,1,4096]{2,1,0:T(1,128)S(1)} %all-to-all-done, f32[]{:T(128)} %broadcast.942), dimensions={1}, to_apply=%all_to_all.3.reduce_sub_computation | reduce | bytes 2097156 | tf_op jit(solution)/shard_map/all_to_all | solution.py:119
  242.7 7.2 %reshape.612 = f32[4096,4,16]{2,1,0:T(4,128)} reshape(f32[64,4096]{1,0:T(8,128)S(1)} %reduce.120) | data formatting | bytes 2097152
  250.0 26.1 %gather_fusion.2 = f32[3072,4,16]{2,1,0:T(4,128)} fusion(f32[4,16,4096]{1,0,2:T(4,128)} %bitcast.100, s32[3072]{0:T(1024)S(1)} %broadcast_clamp_fusion.1), kind=kCustom, calls=%fused_computation.9 | custom fusion | bytes 1585152 | tf_op jit(solution)/shard_map/jit(_take)/gather | solution.py:128
  276.1 5.1 %copy.157 = f32[3072,4,16]{0,2,1:T(8,128)S(1)} copy(f32[3072,4,16]{2,1,0:T(4,128)} %gather_fusion.2) | data formatting | bytes 1572864 | tf_op jit(solution)/shard_map/jit(_take)/gather | solution.py:128
  281.4 0.5 slice.107
  281.9 0.5 slice.101
  282.3 1.2 fusion.39
  283.5 5.5 %collective-permute-start.3 = (f32[4,1,3072]{2,0,1:T(4,128)S(1)}, f32[4,1,3072]{2,0,1:T(4,128)S(1)}, u32[]{:S(2)}, u32[]{:S(2)}) collective-permute-start(f32[4,1,3072]{2,0,1:T(4,128)S(1)} %copy.163), channel_id=1, source_target_pairs={{0,1},{1,2},{2,3},{3,4},{4,5},{5,6},{6,7},{7,8},{8,9},{9,10},{10,1... | collective-permute-start | bytes 147464 | tf_op jit(solution)/shard_map/ppermute | solution.py:29
  289.1 1.9 collective-permute-start.2
  291.1 4.3 %collective-permute-start = (f32[4,16,1]{2,1,0:T(8,128)S(1)}, f32[4,16,1]{2,1,0:T(8,128)S(1)}, u32[]{:S(2)}, u32[]{:S(2)}) collective-permute-start(f32[4,16,1]{2,1,0:T(8,128)S(1)} %bitcast.102), channel_id=1, source_target_pairs={{12,0},{24,12},{36,24},{48,36},{60,48},{72,60},{84,72},{96,84},{10... | collective-permute-start | bytes 776 | tf_op jit(solution)/shard_map/ppermute | solution.py:32
  295.4 2.1 collective-permute-start.1
  297.7 6.2 %collective-permute-done.1 = f32[4,16,1]{2,1,0:T(8,128)S(1)} collective-permute-done((f32[4,16,1]{2,1,0:T(8,128)S(1)}, f32[4,16,1]{2,1,0:T(8,128)S(1)}, u32[]{:S(2)}, u32[]{:S(2)}) %collective-permute-start.1) | collective-permute-done | bytes 288 | tf_op jit(solution)/shard_map/ppermute | solution.py:29
  304.0 0.5 broadcast_in_dim.174
  304.5 1.3 reshape.234
  305.8 0.5 broadcast_in_dim.180
  306.3 1.3 reshape.236
  307.8 2.1 fusion.1
  310.0 0.3 slice_add_fusion
  310.4 0.9 maximum_select_fusion
  (67 shorter events, 2.9 us)
Async XLA Ops:
  0.0 226.6 %copy-start = (s32[1536]{0:T(1024)S(1)}, s32[1536]{0:T(1024)}, u32[]{:S(2)}) copy-start(s32[1536]{0:T(1024)} %param.11) | copy-start | bytes 18436
  23.7 46.3 %copy-start.1 = (s32[1536]{0:T(1024)S(1)}, s32[1536]{0:T(1024)}, u32[]{:S(2)}) copy-start(s32[1536]{0:T(1024)} %param.12) | copy-start | bytes 18436
  24.3 47.8 %copy-start.2 = (f32[4,16,1536]{2,1,0:T(8,128)S(1)}, f32[4,16,1536]{2,1,0:T(8,128)}, u32[]{:S(2)}) copy-start(f32[4,16,1536]{2,1,0:T(8,128)} %param.9) | copy-start | bytes 1179652
  129.0 19.3 %copy-start.3 = (s32[64]{0:T(128)S(1)}, s32[64]{0:T(128)}, u32[]{:S(2)}) copy-start(s32[64]{0:T(128)} %param.13) | copy-start | bytes 772
  137.9 101.0 %all-to-all-start = ((f32[64,1,4096]{2,1,0:T(1,128)}), f32[64,1,4096]{2,1,0:T(1,128)S(1)}, u32[]{:S(2)}, u32[]{:S(2)}) async-start(f32[64,1,4096]{2,1,0:T(1,128)} %reshape.611), calls=%async_computation | async-start | bytes 2097152 | tf_op jit(solution)/shard_map/all_to_all | solution.py:119
  283.5 24.1 %collective-permute-start.3 = (f32[4,1,3072]{2,0,1:T(4,128)S(1)}, f32[4,1,3072]{2,0,1:T(4,128)S(1)}, u32[]{:S(2)}, u32[]{:S(2)}) collective-permute-start(f32[4,1,3072]{2,0,1:T(4,128)S(1)} %copy.163), channel_id=1, source_target_pairs={{0,1},{1,2},{2,3},{3,4},{4,5},{5,6},{6,7},{7,8},{8,9},{9,10},{10,1... | collective-permute-start | bytes 147464 | tf_op jit(solution)/shard_map/ppermute | solution.py:29
  289.1 18.6 %collective-permute-start.2 = (f32[4,1,3072]{2,0,1:T(4,128)S(1)}, f32[4,1,3072]{2,0,1:T(4,128)S(1)}, u32[]{:S(2)}, u32[]{:S(2)}) collective-permute-start(f32[4,1,3072]{2,0,1:T(4,128)S(1)} %copy.161), channel_id=1, source_target_pairs={{1,0},{2,1},{3,2},{4,3},{5,4},{6,5},{7,6},{8,7},{9,8},{10,9},{11,1... | collective-permute-start | bytes 147464 | tf_op jit(solution)/shard_map/ppermute | solution.py:32
  291.1 6.5 %collective-permute-start = (f32[4,16,1]{2,1,0:T(8,128)S(1)}, f32[4,16,1]{2,1,0:T(8,128)S(1)}, u32[]{:S(2)}, u32[]{:S(2)}) collective-permute-start(f32[4,16,1]{2,1,0:T(8,128)S(1)} %bitcast.102), channel_id=1, source_target_pairs={{12,0},{24,12},{36,24},{48,36},{60,48},{72,60},{84,72},{96,84},{10... | collective-permute-start | bytes 776 | tf_op jit(solution)/shard_map/ppermute | solution.py:32
  295.4 8.5 %collective-permute-start.1 = (f32[4,16,1]{2,1,0:T(8,128)S(1)}, f32[4,16,1]{2,1,0:T(8,128)S(1)}, u32[]{:S(2)}, u32[]{:S(2)}) collective-permute-start(f32[4,16,1]{2,1,0:T(8,128)S(1)} %constant_dynamic-slice_fusion), channel_id=1, source_target_pairs={{0,12},{12,24},{24,36},{36,48},{48,60},{60,72},{72,84},{84,96},{96... | collective-permute-start | bytes 776 | tf_op jit(solution)/shard_map/ppermute | solution.py:29
where the time goes:
time: 313 us; the launch traced here: 311 us
  local copies, waits for them, and re-layouts  117 us (37%)
  other arithmetic  97.9 us (31%)
  blocking collectives  64.4 us (21%)
  starting transfers between devices  24.1 us (8%)
  waiting for transfers between devices  6.21 us (2%)
    all_gather x1, blocking collectives, body(): shard_piece = lax.all_gather(coarse_edges, 'slab', axis=2, tiled=True)  64.4 us
    and x1, other arithmetic, body(): at_start = jnp.take(earlier, jnp.take(starts, new_owner), axis=0)  35.6 us
    gather x1, local copies, waits for them, and re-layouts, body(): outgoing = jnp.where(send_live, jnp.take(fine_old, send_cols, axis=2), 0.0)  32 us
    gather x2, local copies, waits for them, and re-layouts, body(): new_strip = jnp.where(live_cols, jnp.take(incoming, recv_cols, axis=2), 0.0)  31.2 us
    unnamed x1, other arithmetic  21.8 us
    unnamed x11, local copies, waits for them, and re-layouts  18.9 us
    another operation x5, other arithmetic  18.6 us
    all_to_all x1, starting transfers between devices, body(): lax.all_to_all(outgoing, 'slab', split_axis=2, concat_axis=2, tiled=True)  10.3 us
  transfers between devices with their start and end apart: 5, of which 1 were waited for; matrix products, arithmetic and copies ran while one was open for 9% of the time, Pallas kernels for 0%

commit v1 on v0

v1 whole, which is shorter than its diff:
```python
import jax
import jax.numpy as jnp
from jax import lax
from jax.experimental import pallas as pl
from jax.experimental.pallas import tpu as pltpu
from jax.sharding import PartitionSpec as P

BX = 64
BOX_DEV = 24
MOST = 48
NBOX = 1536
PPD = 48
NPOS = 3072
SLABS = 64
TILES = MOST // 2
FIELDS = 4
ROWS = 16
BOX_ROWS = FIELDS * 8
MSG_ROWS = BOX_ROWS + 8

ANISOTROPY = 0.3
TIME_STEP = 0.1
COUPLING = 1.5
SOLUTE_ONE = 0.6
SOLUTE_TWO = -0.4
DIFF_HEAT = 2.0
DIFF_ONE = 0.5
DIFF_TWO = 0.25
LATENT = 0.5
REJECT_ONE = 0.5
REJECT_TWO = -0.3

SRC, FINE_L, FINE_R, OWN_L, OWN_R, SIB_L, SIB_R, MISC = range(8)


def lanes(shape=(8, 128)):
    return lax.broadcasted_iota(jnp.int32, shape, 1)


def pick(cond, a, b):
    return lax.select(cond, jnp.int32(a), jnp.int32(b))


def pack_kernel(owner, counts, pos, fine, coarse, out, starts, packed):
    me = lax.axis_index("slab")
    lane = lanes()
    low = lane < 64

    for tile in range(BOX_DEV // 2):
        for f in range(FIELDS):
            top = fine[f, 0:8, tile * 128 : tile * 128 + 128]
            bottom = fine[f, 8:16, tile * 128 : tile * 128 + 128]
            packed[2 * tile, f * 8 : f * 8 + 8] = jnp.where(low, top, pltpu.roll(bottom, 64, 1))
            packed[2 * tile + 1, f * 8 : f * 8 + 8] = jnp.where(low, pltpu.roll(top, 64, 1), bottom)

    inner = lane & 31
    group = lane >> 5
    even = (lane & 1) == 0
    firsts = [jnp.zeros((8, 128), jnp.float32) for _ in range(2)]
    lasts = [jnp.zeros((8, 128), jnp.float32) for _ in range(2)]
    for f in range(FIELDS):
        first = jnp.zeros((8, 128), jnp.float32)
        last = jnp.zeros((8, 128), jnp.float32)
        for tile in range(12):
            x = coarse[f, :, tile * 128 : tile * 128 + 128]
            if tile:
                x = pltpu.roll(x, 2 * tile, 1)
            first = jnp.where(inner == 2 * tile, x, first)
            last = jnp.where(inner == (31 + 2 * tile) % 32, x, last)

        def moved(x, shift):
            shift = (f * 32 + shift) % 128
            return pltpu.roll(x, shift, 1) if shift else x

        here = group == f
        first_even = jnp.where(even, moved(first, 0), moved(first, -63))
        first_odd = jnp.where(even, moved(first, -32), moved(first, -95))
        last_even = jnp.where(even, moved(last, -125), moved(last, -62))
        last_odd = jnp.where(even, moved(last, -31), moved(last, -94))
        firsts = [jnp.where(here, a, b) for a, b in zip((first_even, first_odd), firsts)]
        lasts = [jnp.where(here, a, b) for a, b in zip((last_even, last_odd), lasts)]

    block = pick((me & 1) == 0, me + 1, (me + 31) & 63)
    base = block * PPD
    first_box = jnp.int32(0)
    for step in (1024, 512, 256, 128, 64, 32, 16, 8, 4, 2, 1):
        trial = first_box + step
        value = pos[jnp.minimum(trial, NBOX) - 1]
        first_box = pick((trial <= NBOX) & (value < base), trial, first_box)

    def mark(i, words):
        word0, word1 = words
        k = first_box + i
        at = pos[jnp.minimum(k, NBOX - 1)] - base
        good = (k < NBOX) & (at <= PPD)
        bit = jnp.left_shift(jnp.int32(1), at & 31)
        word0 = word0 | pick(good & (at < 32), bit, 0)
        word1 = word1 | pick(good & (at >= 32), bit, 0)
        return word0, word1

    word0, word1 = lax.fori_loop(0, PPD + 1, mark, (jnp.int32(0), jnp.int32(0)), unroll=7)
    for core in range(2):
        joint = 2 * inner + core
        words = jnp.where(joint < 32, word0, word1)
        fine_here = (lax.shift_right_logical(words, joint & 31) & 1) == 1
        edge = jnp.where(fine_here, lasts[core], firsts[core])
        for b in range(core, SLABS, 2):
            out[b, BOX_ROWS:MSG_ROWS] = edge

    def find(i, r):
        return r + pick(owner[i] == me, i, 0)

    residue = lax.fori_loop(0, SLABS, find, jnp.int32(0), unroll=16)

    def fill(b, start):
        starts[b] = start
        k = start - 1 + ((residue - (start - 1)) & 63)
        slot = jnp.clip(k >> 6, 0, BOX_DEV - 1)
        out[b, 0:BOX_ROWS] = packed[slot]
        return start + counts[b]

    lax.fori_loop(0, SLABS, fill, jnp.int32(0), unroll=8)


def plan_kernel(owner, counts, pos, starts, plan):
    me = lax.axis_index("slab")
    mine = me & 1
    start = starts[me]
    plan[MISC * 64] = start
    plan[MISC * 64 + 1] = counts[me]

    def source(i, carry):
        plan[SRC * 64 + i] = owner[(start + i - 2) & 63]
        return carry

    lax.fori_loop(0, MOST + 4, source, 0, unroll=4)

    def code(at, joint, wanted):
        block = (at * 43691) >> 21
        joint = joint + at - block * PPD
        device = pick((block & 1) == 1, block - 1, (block + 33) & 63)
        keep = wanted & ((joint & 1) == mine)
        return pick(keep, device * 32 + (joint >> 1), -1)

    def ghosts(first, left_row, right_row, flags):
        def one(s, carry):
            k = jnp.minimum(first + s, NBOX - 1)
            at = pos[k]
            before = pos[jnp.maximum(k - 1, 0)]
            after = pos[jnp.minimum(k + 1, NBOX - 1)]
            fine_l = before == at - 1
            fine_r = after == at + 1
            if flags:
                plan[FINE_L * 64 + s] = pick(fine_l, 1, 0)
                plan[FINE_R * 64 + s] = pick(fine_r, 1, 0)
            has_l = jnp.logical_not(fine_l) & (k > 0)
            has_r = jnp.logical_not(fine_r) & (k < NBOX - 1)
            plan[left_row * 64 + s] = code(jnp.maximum(at - 1, 0), 1, has_l)
            plan[right_row * 64 + s] = code(jnp.minimum(at + 1, NPOS - 1), 0, has_r)
            return carry

        lax.fori_loop(0, MOST, one, 0, unroll=2)

    ghosts(start, OWN_L, OWN_R, True)
    ghosts(starts[me ^ 1], SIB_L, SIB_R, False)


def gather_edges(plan, inc, rows):
    lane = lanes()
    inner = lane & 31

    def one(m, carry):
        here = inner == m
        out = []
        for n, (row, half) in enumerate((row, half) for row in rows for half in range(2)):
            code = plan[row * 64 + half * TILES + m]
            x = inc[jnp.maximum(code, 0) >> 5, BOX_ROWS:MSG_ROWS]
            x = pltpu.roll(x, (m - (code & 31)) & 127, 1)
            out.append(jnp.where(here & (code >= 0), x, carry[n]))
        return tuple(out)

    zero = jnp.zeros((8, 128), jnp.float32)
    return lax.fori_loop(0, TILES, one, (zero,) * (2 * len(rows)), unroll=4)


def edge_kernel(plan, inc, low_rows, high_rows, sibling):
    low = lanes((1, 128)) < 64

    def one(t, carry):
        a = plan[SRC * 64 + 2 + 2 * t]
        b = plan[SRC * 64 + 3 + 2 * t]
        for f in range(FIELDS):
            row = f * 8
            low_rows[t, f : f + 1] = jnp.where(
                low, inc[a, row : row + 1], pltpu.roll(inc[b, row : row + 1], 64, 1)
            )
            row = f * 8 + 7
            high_rows[t, f : f + 1] = jnp.where(
                low, pltpu.roll(inc[a, row : row + 1], 64, 1), inc[b, row : row + 1]
            )
        return carry

    lax.fori_loop(0, TILES, one, 0, unroll=4)
    for n, edges in enumerate(gather_edges(plan, inc, (SIB_L, SIB_R))):
        sibling[n] = edges


def advance(center, west_cells, east_cells, south_cells, north_cells):
    laplace = [
        w + e + s + n - 4.0 * c
        for c, w, e, s, n in zip(center, west_cells, east_cells, south_cells, north_cells)
    ]
    phase = center[0]
    grad_x = 0.5 * (east_cells[0] - west_cells[0])
    grad_y = 0.5 * (north_cells[0] - south_cells[0])
    sq_x = grad_x * grad_x
    sq_y = grad_y * grad_y
    spread_sum = sq_x + sq_y + 1.0
    anisotropy = 1.0 + ANISOTROPY * (sq_x * sq_x - 6.0 * sq_x * sq_y + sq_y * sq_y) / (
        spread_sum * spread_sum
    )
    couple = center[1] + SOLUTE_ONE * center[2] + SOLUTE_TWO * center[3]
    wall_term = 1.0 - phase * phase
    phase_step = TIME_STEP * (
        anisotropy * anisotropy * laplace[0]
        + phase
        - phase * phase * phase
        - COUPLING * wall_term * wall_term * couple
    )
    return (
        phase + phase_step,
        center[1] + TIME_STEP * DIFF_HEAT * laplace[1] + LATENT * phase_step,
        center[2] + TIME_STEP * DIFF_ONE * laplace[2] + REJECT_ONE * center[2] * phase_step,
        center[3] + TIME_STEP * DIFF_TWO * laplace[3] + REJECT_TWO * center[3] * phase_step,
    )


def step_kernel(plan, inc, from_below, from_above, sibling, out, cen, edges):
    sub = lax.axis_index("sub")
    lane = lanes()
    low = lane < 64
    row8 = lax.broadcasted_iota(jnp.int32, (8, 128), 0)
    start = plan[MISC * 64]
    count = plan[MISC * 64 + 1]

    def unpack(t, carry):
        a = plan[SRC * 64 + 2 * t]
        b = plan[SRC * 64 + 1 + 2 * t]
        for f in range(FIELDS):
            x = inc[a, f * 8 : f * 8 + 8]
            y = inc[b, f * 8 : f * 8 + 8]
            cen[t, f, 0:8] = jnp.where(low, x, pltpu.roll(y, 64, 1))
            cen[t, f, 8:16] = jnp.where(low, pltpu.roll(x, 64, 1), y)
        return carry

    lax.fori_loop(0, TILES + 2, unpack, 0, unroll=2)

    own = gather_edges(plan, inc, (OWN_L, OWN_R))
    for n in range(4):
        whole = own[n] + sibling[n]
        edges[n, 0:8] = jnp.take_along_axis(whole, row8 >> 1, axis=0)
        edges[n, 8:16] = jnp.take_along_axis(whole, 4 + (row8 >> 1), axis=0)

    lane = lanes((ROWS, 128))
    row = lax.broadcasted_iota(jnp.int32, (ROWS, 128), 0)
    at_first = (lane & 31) == 0
    outer = (lane == 0) | (lane == 127)
    at_bottom = sub == 0
    at_top = sub == lax.axis_size("sub") - 1

    def one(t, carry):
        s = 2 * t
        half = pick(s >= TILES, 1, 0)
        m = s - half * TILES
        left = edges[half]
        right = edges[2 + half]
        ends = jnp.where(at_first, pltpu.roll(left, (128 - m) & 127, 1), pltpu.roll(right, 126 - m, 1))
        middle = jnp.where(at_first, pltpu.roll(left, 127 - m, 1), pltpu.roll(right, 127 - m, 1))
        fl0, fl1 = plan[FINE_L * 64 + s] == 1, plan[FINE_L * 64 + s + 1] == 1
        fr0, fr1 = plan[FINE_R * 64 + s] == 1, plan[FINE_R * 64 + s + 1] == 1
        k = start + s
        ghost_w = ((lane == 0) & jnp.logical_not(fl0)) | ((lane == 64) & jnp.logical_not(fl1))
        ghost_e = ((lane == 63) & jnp.logical_not(fr0)) | ((lane == 127) & jnp.logical_not(fr1))
        border = (
            ((lane == 0) & (k == 0))
            | ((lane == 63) & (k == NBOX - 1))
            | ((lane == 127) & (k + 1 == NBOX - 1))
        )
        live = jnp.where(lane < 64, s, s + 1) < count
        center, west, east, south, north = [], [], [], [], []
        for f in range(FIELDS):
            c = cen[t + 1, f]
            w = jnp.where(lane == 0, pltpu.roll(cen[t, f], 1, 1), pltpu.roll(c, 1, 1))
            e = jnp.where(lane == 127, pltpu.roll(cen[t + 2, f], 127, 1), pltpu.roll(c, 127, 1))
            g = jnp.where(
                outer,
                pltpu.roll(ends, 128 - 32 * f, 1) if f else ends,
                pltpu.roll(middle, (192 - 32 * f) % 128, 1) if f != 2 else middle,
            )
            g = jnp.where(border, c, g)
            below = jnp.where(at_bottom, c[0:1], from_below[t, f : f + 1])
            above = jnp.where(at_top, c[15:16], from_above[t, f : f + 1])
            center.append(c)
            west.append(jnp.where(ghost_w, g, w))
            east.append(jnp.where(ghost_e, g, e))
            south.append(jnp.where(row == 0, below, pltpu.roll(c, 1, 0)))
            north.append(jnp.where(row == ROWS - 1, above, pltpu.roll(c, ROWS - 1, 0)))
        stepped = advance(center, west, east, south, north)
        at = pl.ds(pl.multiple_of(t * 128, 128), 128)
        for f in range(FIELDS):
            out[f, :, at] = jnp.where(live, stepped[f], 0.0)
        return carry

    lax.fori_loop(0, TILES, one, 0)


SMEM = pl.BlockSpec(memory_space=pltpu.SMEM)
VMEM = pl.BlockSpec(memory_space=pltpu.VMEM)
PARAMS = pltpu.CompilerParams(vmem_limit_bytes=32 * 1024 * 1024)


def f32(*shape):
    return jax.ShapeDtypeStruct(shape, jnp.float32)


def i32(*shape):
    return jax.ShapeDtypeStruct(shape, jnp.int32)


def body(fine_old, coarse, box_pos, old_owner, new_counts):
    outgoing, starts = pl.pallas_call(
        pack_kernel,
        name="pack",
        out_shape=(f32(SLABS, MSG_ROWS, 128), i32(SLABS)),
        in_specs=[SMEM, SMEM, SMEM, VMEM, VMEM],
        out_specs=(VMEM, SMEM),
        scratch_shapes=[pltpu.VMEM((BOX_DEV, BOX_ROWS, 128), jnp.float32)],
        compiler_params=PARAMS,
    )(old_owner, new_counts, box_pos, fine_old, coarse)
    incoming = lax.all_to_all(outgoing, "slab", 0, 0, tiled=True)
    plan = pl.pallas_call(
        plan_kernel,
        name="plan",
        out_shape=i32(8 * 64),
        in_specs=[SMEM] * 4,
        out_specs=SMEM,
        compiler_params=PARAMS,
    )(old_owner, new_counts, box_pos, starts)
    low_rows, high_rows, sibling = pl.pallas_call(
        edge_kernel,
        name="edges",
        out_shape=(f32(TILES, FIELDS, 128), f32(TILES, FIELDS, 128), f32(4, 8, 128)),
        in_specs=[SMEM, VMEM],
        out_specs=(VMEM, VMEM, VMEM),
        compiler_params=PARAMS,
    )(plan, incoming)
    count = lax.axis_size("sub")
    up = [(i, i + 1) for i in range(count - 1)]
    sibling = lax.ppermute(sibling, "slab", [(i, i ^ 1) for i in range(SLABS)])
    from_below = lax.ppermute(high_rows, "sub", up)
    from_above = lax.ppermute(low_rows, "sub", [(b, a) for a, b in up])
    return pl.pallas_call(
        step_kernel,
        name="step",
        out_shape=f32(FIELDS, ROWS, MOST * BX),
        in_specs=[SMEM] + [VMEM] * 4,
        out_specs=VMEM,
        scratch_shapes=[
            pltpu.VMEM((TILES + 2, FIELDS, ROWS, 128), jnp.float32),
            pltpu.VMEM((4, ROWS, 128), jnp.float32),
        ],
        compiler_params=PARAMS,
    )(plan, incoming, from_below, from_above, sibling)


def solution(mesh):
    placed = (P(None, "sub", "slab"), P(None, "sub", "slab"), P(), P(), P())
    return jax.shard_map(
        body, mesh=mesh, in_specs=placed, out_specs=P(None, "sub", "slab"), check_vma=False
    )
```

time: 313 us -> 74.5 us (0.24)
  the two profiles are of different devices: /device:TPU:224 before, /device:TPU:192 now
where the time goes in v1:
time: 74.5 us; the launch traced here: 74 us
  waiting for transfers between devices  34.1 us (46%)
  starting transfers between devices  20 us (27%)
  Pallas kernels  15.8 us (21%)
  local copies, waits for them, and re-layouts  3.99 us (5%)
    all_to_all x1, waiting for transfers between devices, body(): incoming = lax.all_to_all(outgoing, 'slab', 0, 0, tiled=True)  30.8 us
    all_to_all x1, starting transfers between devices, body(): incoming = lax.all_to_all(outgoing, 'slab', 0, 0, tiled=True)  10.7 us
    pallas_call x1, Pallas kernels, body(): pl.pallas_call(step_kernel, name='step', out_shape=f32(FIELDS, ROWS, MOST...  7.35 us
    ppermute x1, starting transfers between devices, body(): from_below = lax.ppermute(high_rows, 'sub', up)  5.49 us
    unnamed x16, local copies, waits for them, and re-layouts  3.99 us
    pallas_call x1, Pallas kernels, body(): pl.pallas_call(plan_kernel, name='plan', out_shape=i32(8 * 64), in_specs=...  3.72 us
    pallas_call x1, Pallas kernels, body(): pl.pallas_call(pack_kernel, name='pack', out_shape=(f32(SLABS, MSG_ROWS,...  2.86 us
    ppermute x1, waiting for transfers between devices, body(): from_above = lax.ppermute(low_rows, 'sub', [(b, a) for a, b in up])  2.18 us
  transfers between devices with their start and end apart: 4, of which 3 were waited for; matrix products, arithmetic and copies ran while one was open for 0% of the time, Pallas kernels for 5%

profile of v1, /device:TPU:192, one launch (start us, length us, event | category | flops | bytes accessed | tf_op | source)
XLA Modules:
  0.0 74.0 jit_solution(12976081728866820993)
XLA Ops:
  0.0 0.0 copy-start
  0.0 1.0 %copy-done = f32[4,16,1536]{2,1,0:T(8,128)S(1)} copy-done((f32[4,16,1536]{2,1,0:T(8,128)S(1)}, f32[4,16,1536]{2,1,0:T(8,128)}, u32[]{:S(2)}) %copy-start) | copy-done | bytes 393240
  1.0 0.0 copy-start.1
  1.0 0.9 %copy-done.1 = f32[4,8,1536]{2,1,0:T(8,128)S(1)} copy-done((f32[4,8,1536]{2,1,0:T(8,128)S(1)}, f32[4,8,1536]{2,1,0:T(8,128)}, u32[]{:S(2)}) %copy-start.1) | copy-done | bytes 196632
  1.9 0.0 copy-start.2
  1.9 0.7 copy-done.2
  2.6 0.0 copy-start.4
  2.6 0.7 copy-done.4
  3.3 0.0 copy-start.6
  3.3 0.7 copy-done.6
  4.0 2.9 %pack.1 = (f32[64,40,128]{2,1,0:T(8,128)}, s32[64]{0:T(128)S(1)}) custom-call(s32[1536]{0:T(1024)S(1)} %copy-done.2, s32[64]{0:T(128)S(1)} %copy-done.6, s32[1536]{0:T(1024)S(1)} %copy-done.4, f32[4,16,1536]{2,1,0:T(8,128)S(1)} %copy-done, f32[4,8,1536]{2,1,0:T(8,128)S(1)} %copy-done.1), custom_call_target="tpu_custom_call" | custom-call | tf_op jit(solution)/shard_map/pack/pallas_call | solution.py:331
  6.8 0.0 copy-start.3
  6.9 0.0 copy-start.5
  6.9 0.0 copy-start.7
  6.9 10.7 %all-to-all-start = ((f32[64,40,128]{2,1,0:T(8,128)}), f32[64,40,128]{2,1,0:T(8,128)S(1)}, u32[]{:S(2)}, u32[]{:S(2)}) async-start(f32[64,40,128]{2,1,0:T(8,128)} %get-tuple-element.11), calls=%async_computation | async-start | bytes 2621440 | tf_op jit(solution)/shard_map/all_to_all | solution.py:340
  17.6 0.0 copy-done.3
  17.6 0.0 copy-done.5
  17.6 0.0 copy-done.7
  17.6 3.7 %plan.1 = s32[512]{0:T(512)S(1)} custom-call(s32[1536]{0:T(1024)S(1)} %copy-done.3, s32[64]{0:T(128)S(1)} %copy-done.7, s32[1536]{0:T(1024)S(1)} %copy-done.5, s32[64]{0:T(128)S(1)} %get-tuple-element.10.starts), custom_call_target="tpu_custom_call" | custom-call | tf_op jit(solution)/shard_map/plan/pallas_call | solution.py:341
  21.4 30.8 %all-to-all-done.inc = f32[64,40,128]{2,1,0:T(8,128)S(1)} async-done(((f32[64,40,128]{2,1,0:T(8,128)}), f32[64,40,128]{2,1,0:T(8,128)S(1)}, u32[]{:S(2)}, u32[]{:S(2)}) %all-to-all-start) | async-done | bytes 1310752 | tf_op jit(solution)/shard_map/all_to_all | solution.py:340
  52.1 1.9 %edges.1 = (f32[24,4,128]{2,1,0:T(4,128)S(1)}, f32[24,4,128]{2,1,0:T(4,128)S(1)}, f32[4,8,128]{2,1,0:T(8,128)S(1)}) custom-call(s32[512]{0:T(512)S(1)} %plan.1, f32[64,40,128]{2,1,0:T(8,128)S(1)} %all-to-all-done.inc), custom_call_target="tpu_custom_call" | custom-call | tf_op jit(solution)/shard_map/edges/pallas_call | solution.py:349
  54.0 5.5 %collective-permute-start = (f32[24,4,128]{2,1,0:T(4,128)S(1)}, f32[24,4,128]{2,1,0:T(4,128)S(1)}, u32[]{:S(2)}, u32[]{:S(2)}) collective-permute-start(f32[24,4,128]{2,1,0:T(4,128)S(1)} %get-tuple-element.12), channel_id=1, source_target_pairs={{0,1},{1,2},{2,3},{3,4},{4,5},{5,6},{6,7},{7,8},{8,9},{9,10},{10,1... | collective-permute-start | bytes 147464 | tf_op jit(solution)/shard_map/ppermute | solution.py:360
  59.5 1.9 %collective-permute-start.1 = (f32[24,4,128]{2,1,0:T(4,128)S(1)}, f32[24,4,128]{2,1,0:T(4,128)S(1)}, u32[]{:S(2)}, u32[]{:S(2)}) collective-permute-start(f32[24,4,128]{2,1,0:T(4,128)S(1)} %get-tuple-element.13), channel_id=1, source_target_pairs={{1,0},{2,1},{3,2},{4,3},{5,4},{6,5},{7,6},{8,7},{9,8},{10,9},{11,1... | collective-permute-start | bytes 147464 | tf_op jit(solution)/shard_map/ppermute | solution.py:361
  61.4 1.9 %collective-permute-start.2 = (f32[4,8,128]{2,1,0:T(8,128)S(1)}, f32[4,8,128]{2,1,0:T(8,128)S(1)}, u32[]{:S(2)}, u32[]{:S(2)}) collective-permute-start(f32[4,8,128]{2,1,0:T(8,128)S(1)} %get-tuple-element.14), channel_id=1, source_target_pairs={{0,12},{12,0},{24,36},{36,24},{48,60},{60,48},{72,84},{84,72},{96,... | collective-permute-start | bytes 49160 | tf_op jit(solution)/shard_map/ppermute | solution.py:359
  63.3 1.1 %collective-permute-done.2.sibling = f32[4,8,128]{2,1,0:T(8,128)S(1)} collective-permute-done((f32[4,8,128]{2,1,0:T(8,128)S(1)}, f32[4,8,128]{2,1,0:T(8,128)S(1)}, u32[]{:S(2)}, u32[]{:S(2)}) %collective-permute-start.2) | collective-permute-done | bytes 16416 | tf_op jit(solution)/shard_map/ppermute | solution.py:359
  64.5 0.0 collective-permute-done.from_below
  64.5 2.2 %collective-permute-done.1.from_above = f32[24,4,128]{2,1,0:T(4,128)S(1)} collective-permute-done((f32[24,4,128]{2,1,0:T(4,128)S(1)}, f32[24,4,128]{2,1,0:T(4,128)S(1)}, u32[]{:S(2)}, u32[]{:S(2)}) %collective-permute-start.1) | collective-permute-done | bytes 49184 | tf_op jit(solution)/shard_map/ppermute | solution.py:361
  66.7 7.4 %step.1 = f32[4,16,3072]{2,1,0:T(8,128)} custom-call(s32[512]{0:T(512)S(1)} %plan.1, f32[64,40,128]{2,1,0:T(8,128)S(1)} %all-to-all-done.inc, f32[24,4,128]{2,1,0:T(4,128)S(1)} %collective-permute-done.from_below, f32[24,4,128]{2,1,0:T(4,128)S(1)} %collective-permute-done.1.from_above, f32[4,8,128]{2,1,0:T(8,128)S(1)} %collective-permute-done.2.sibling), custom_call_target="tpu_custom_call" | custom-call | tf_op jit(solution)/shard_map/step/pallas_call | solution.py:362
Async XLA Ops:
  0.0 1.0 %copy-start = (f32[4,16,1536]{2,1,0:T(8,128)S(1)}, f32[4,16,1536]{2,1,0:T(8,128)}, u32[]{:S(2)}) copy-start(f32[4,16,1536]{2,1,0:T(8,128)} %fine.1) | copy-start | bytes 1179652
  1.0 0.9 %copy-start.1 = (f32[4,8,1536]{2,1,0:T(8,128)S(1)}, f32[4,8,1536]{2,1,0:T(8,128)}, u32[]{:S(2)}) copy-start(f32[4,8,1536]{2,1,0:T(8,128)} %coarse.1) | copy-start | bytes 589828
  1.9 0.7 copy-start.2
  2.6 0.7 copy-start.4
  3.3 0.7 copy-start.6
  6.8 10.8 %copy-start.3 = (s32[1536]{0:T(1024)S(1)}, s32[1536]{0:T(1024)}, u32[]{:S(2)}) copy-start(s32[1536]{0:T(1024)} %owner.3) | copy-start | bytes 18436
  6.9 10.8 %copy-start.5 = (s32[1536]{0:T(1024)S(1)}, s32[1536]{0:T(1024)}, u32[]{:S(2)}) copy-start(s32[1536]{0:T(1024)} %pos.3) | copy-start | bytes 18436
  6.9 10.8 %copy-start.7 = (s32[64]{0:T(128)S(1)}, s32[64]{0:T(128)}, u32[]{:S(2)}) copy-start(s32[64]{0:T(128)} %counts.3) | copy-start | bytes 772
  6.9 45.2 %all-to-all-start = ((f32[64,40,128]{2,1,0:T(8,128)}), f32[64,40,128]{2,1,0:T(8,128)S(1)}, u32[]{:S(2)}, u32[]{:S(2)}) async-start(f32[64,40,128]{2,1,0:T(8,128)} %get-tuple-element.11), calls=%async_computation | async-start | bytes 2621440 | tf_op jit(solution)/shard_map/all_to_all | solution.py:340
  54.0 10.5 %collective-permute-start = (f32[24,4,128]{2,1,0:T(4,128)S(1)}, f32[24,4,128]{2,1,0:T(4,128)S(1)}, u32[]{:S(2)}, u32[]{:S(2)}) collective-permute-start(f32[24,4,128]{2,1,0:T(4,128)S(1)} %get-tuple-element.12), channel_id=1, source_target_pairs={{0,1},{1,2},{2,3},{3,4},{4,5},{5,6},{6,7},{7,8},{8,9},{9,10},{10,1... | collective-permute-start | bytes 147464 | tf_op jit(solution)/shard_map/ppermute | solution.py:360
  59.5 7.2 %collective-permute-start.1 = (f32[24,4,128]{2,1,0:T(4,128)S(1)}, f32[24,4,128]{2,1,0:T(4,128)S(1)}, u32[]{:S(2)}, u32[]{:S(2)}) collective-permute-start(f32[24,4,128]{2,1,0:T(4,128)S(1)} %get-tuple-element.13), channel_id=1, source_target_pairs={{1,0},{2,1},{3,2},{4,3},{5,4},{6,5},{7,6},{8,7},{9,8},{10,9},{11,1... | collective-permute-start | bytes 147464 | tf_op jit(solution)/shard_map/ppermute | solution.py:361
  61.4 3.1 %collective-permute-start.2 = (f32[4,8,128]{2,1,0:T(8,128)S(1)}, f32[4,8,128]{2,1,0:T(8,128)S(1)}, u32[]{:S(2)}, u32[]{:S(2)}) collective-permute-start(f32[4,8,128]{2,1,0:T(8,128)S(1)} %get-tuple-element.14), channel_id=1, source_target_pairs={{0,12},{12,0},{24,36},{36,24},{48,60},{60,48},{72,84},{84,72},{96,... | collective-permute-start | bytes 49160 | tf_op jit(solution)/shard_map/ppermute | solution.py:359

commit v2 on v1

--- a/solution.py
+++ b/solution.py
@@ -13,6 +13,9 @@
 NPOS = 3072
 SLABS = 64
 TILES = MOST // 2
+QUARTER = MOST // 4
+GU = 12
+UU = 24
 FIELDS = 4
 ROWS = 16
 BOX_ROWS = FIELDS * 8
@@ -41,7 +44,19 @@
     return lax.select(cond, jnp.int32(a), jnp.int32(b))
 
 
-def pack_kernel(owner, counts, pos, fine, coarse, out, starts, packed):
+def pack_kernel(
+    owner_in, counts_in, pos_in, fine_in, coarse_in, out, starts, owner, counts, pos, fine, coarse, packed, sems
+):
+    copies = [
+        pltpu.make_async_copy(a, b, sems.at[n])
+        for n, (a, b) in enumerate(
+            ((pos_in, pos), (owner_in, owner), (counts_in, counts), (fine_in, fine), (coarse_in, coarse))
+        )
+    ]
+    for copy in copies:
+        copy.start()
+    for copy in copies:
+        copy.wait()
     me = lax.axis_index("slab")
     lane = lanes()
     low = lane < 64
@@ -98,7 +113,7 @@
         word1 = word1 | pick(good & (at >= 32), bit, 0)
         return word0, word1
 
-    word0, word1 = lax.fori_loop(0, PPD + 1, mark, (jnp.int32(0), jnp.int32(0)), unroll=7)
+    word0, word1 = lax.fori_loop(0, PPD + 1, mark, (jnp.int32(0), jnp.int32(0)), unroll=49)
     for core in range(2):
         joint = 2 * inner + core
         words = jnp.where(joint < 32, word0, word1)
@@ -110,7 +125,7 @@
     def find(i, r):
         return r + pick(owner[i] == me, i, 0)
 
-    residue = lax.fori_loop(0, SLABS, find, jnp.int32(0), unroll=16)
+    residue = lax.fori_loop(0, SLABS, find, jnp.int32(0), unroll=64)
 
     def fill(b, start):
         starts[b] = start
@@ -119,7 +134,7 @@
         out[b, 0:BOX_ROWS] = packed[slot]
         return start + counts[b]
 
-    lax.fori_loop(0, SLABS, fill, jnp.int32(0), unroll=8)
+    lax.fori_loop(0, SLABS, fill, jnp.int32(0), unroll=64)
 
 
 def plan_kernel(owner, counts, pos, starts, plan):
@@ -165,22 +180,23 @@
     ghosts(starts[me ^ 1], SIB_L, SIB_R, False)
 
 
-def gather_edges(plan, inc, rows):
+def gather_edges(plan, inc, left, right):
     lane = lanes()
     inner = lane & 31
 
     def one(m, carry):
-        here = inner == m
         out = []
-        for n, (row, half) in enumerate((row, half) for row in rows for half in range(2)):
-            code = plan[row * 64 + half * TILES + m]
-            x = inc[jnp.maximum(code, 0) >> 5, BOX_ROWS:MSG_ROWS]
-            x = pltpu.roll(x, (m - (code & 31)) & 127, 1)
-            out.append(jnp.where(here & (code >= 0), x, carry[n]))
+        for q, edges in enumerate(carry):
+            for row, to in ((left, m), (right, m + QUARTER)):
+                code = plan[row * 64 + q * QUARTER + m]
+                x = inc[jnp.maximum(code, 0) >> 5, BOX_ROWS:MSG_ROWS]
+                x = pltpu.roll(x, (to - (code & 31)) & 127, 1)
+                edges = jnp.where((inner == to) & (code >= 0), x, edges)
+            out.append(edges)
         return tuple(out)
 
     zero = jnp.zeros((8, 128), jnp.float32)
-    return lax.fori_loop(0, TILES, one, (zero,) * (2 * len(rows)), unroll=4)
+    return lax.fori_loop(0, QUARTER, one, (zero,) * 4, unroll=GU)
 
 
 def edge_kernel(plan, inc, low_rows, high_rows, sibling):
@@ -200,20 +216,15 @@
             )
         return carry
 
-    lax.fori_loop(0, TILES, one, 0, unroll=4)
-    for n, edges in enumerate(gather_edges(plan, inc, (SIB_L, SIB_R))):
+    lax.fori_loop(0, TILES, one, 0, unroll=24)
+    for n, edges in enumerate(gather_edges(plan, inc, SIB_L, SIB_R)):
         sibling[n] = edges
 
 
-def advance(center, west_cells, east_cells, south_cells, north_cells):
-    laplace = [
-        w + e + s + n - 4.0 * c
-        for c, w, e, s, n in zip(center, west_cells, east_cells, south_cells, north_cells)
-    ]
+def advance(center, across, sq_x, south_cells, north_cells):
+    laplace = [a + s + n - 4.0 * c for c, a, s, n in zip(center, across, south_cells, north_cells)]
     phase = center[0]
-    grad_x = 0.5 * (east_cells[0] - west_cells[0])
     grad_y = 0.5 * (north_cells[0] - south_cells[0])
-    sq_x = grad_x * grad_x
     sq_y = grad_y * grad_y
     spread_sum = sq_x + sq_y + 1.0
     anisotropy = 1.0 + ANISOTROPY * (sq_x * sq_x - 6.0 * sq_x * sq_y + sq_y * sq_y) / (
@@ -235,47 +246,48 @@
     )
 
 
-def step_kernel(plan, inc, from_below, from_above, sibling, out, cen, edges):
-    sub = lax.axis_index("sub")
+def middle_kernel(plan, inc, sibling, cen, across, slope, edges, outside):
     lane = lanes()
     low = lane < 64
     row8 = lax.broadcasted_iota(jnp.int32, (8, 128), 0)
     start = plan[MISC * 64]
-    count = plan[MISC * 64 + 1]
-
-    def unpack(t, carry):
-        a = plan[SRC * 64 + 2 * t]
-        b = plan[SRC * 64 + 1 + 2 * t]
+
+    def unpack(a, b, put):
         for f in range(FIELDS):
             x = inc[a, f * 8 : f * 8 + 8]
             y = inc[b, f * 8 : f * 8 + 8]
-            cen[t, f, 0:8] = jnp.where(low, x, pltpu.roll(y, 64, 1))
-            cen[t, f, 8:16] = jnp.where(low, pltpu.roll(x, 64, 1), y)
+            put(f, 0, jnp.where(low, x, pltpu.roll(y, 64, 1)))
+            put(f, 8, jnp.where(low, pltpu.roll(x, 64, 1), y))
+
+    def inside(t, carry):
+        def put(f, row, x):
+            cen[t, f, row : row + 8] = x
+
+        unpack(plan[SRC * 64 + 2 + 2 * t], plan[SRC * 64 + 3 + 2 * t], put)
         return carry
 
-    lax.fori_loop(0, TILES + 2, unpack, 0, unroll=2)
-
-    own = gather_edges(plan, inc, (OWN_L, OWN_R))
+    lax.fori_loop(0, TILES, inside, 0, unroll=UU)
+    for n, s in enumerate((0, MOST + 2)):
+
+        def put(f, row, x):
+            outside[n, f, row : row + 8] = x
+
+        unpack(plan[SRC * 64 + s], plan[SRC * 64 + s + 1], put)
+
+    own = gather_edges(plan, inc, OWN_L, OWN_R)
     for n in range(4):
         whole = own[n] + sibling[n]
         edges[n, 0:8] = jnp.take_along_axis(whole, row8 >> 1, axis=0)
         edges[n, 8:16] = jnp.take_along_axis(whole, 4 + (row8 >> 1), axis=0)
 
     lane = lanes((ROWS, 128))
-    row = lax.broadcasted_iota(jnp.int32, (ROWS, 128), 0)
-    at_first = (lane & 31) == 0
-    outer = (lane == 0) | (lane == 127)
-    at_bottom = sub == 0
-    at_top = sub == lax.axis_size("sub") - 1
-
-    def one(t, carry):
+    near = lanes()
+    where_from = jnp.where(near >= 64, 1, 0) + jnp.where((near & 63) >= 32, QUARTER, 0)
+
+    def one(t, before, after):
         s = 2 * t
-        half = pick(s >= TILES, 1, 0)
-        m = s - half * TILES
-        left = edges[half]
-        right = edges[2 + half]
-        ends = jnp.where(at_first, pltpu.roll(left, (128 - m) & 127, 1), pltpu.roll(right, 126 - m, 1))
-        middle = jnp.where(at_first, pltpu.roll(left, 127 - m, 1), pltpu.roll(right, 127 - m, 1))
+        q = (s * 43691) >> 19
+        m = s - q * QUARTER
         fl0, fl1 = plan[FINE_L * 64 + s] == 1, plan[FINE_L * 64 + s + 1] == 1
         fr0, fr1 = plan[FINE_R * 64 + s] == 1, plan[FINE_R * 64 + s + 1] == 1
         k = start + s
@@ -286,36 +298,71 @@
             | ((lane == 63) & (k == NBOX - 1))
             | ((lane == 127) & (k + 1 == NBOX - 1))
         )
-        live = jnp.where(lane < 64, s, s + 1) < count
-        center, west, east, south, north = [], [], [], [], []
-        for f in range(FIELDS):
-            c = cen[t + 1, f]
-            w = jnp.where(lane == 0, pltpu.roll(cen[t, f], 1, 1), pltpu.roll(c, 1, 1))
-            e = jnp.where(lane == 127, pltpu.roll(cen[t + 2, f], 127, 1), pltpu.roll(c, 127, 1))
-            g = jnp.where(
-                outer,
-                pltpu.roll(ends, 128 - 32 * f, 1) if f else ends,
-                pltpu.roll(middle, (192 - 32 * f) % 128, 1) if f != 2 else middle,
+        for f in range(FIELDS):
+            c = cen[t, f]
+            w = pltpu.roll(jnp.where(lane == 127, before[f], c), 1, 1)
+            e = pltpu.roll(jnp.where(lane == 0, after[f], c), 127, 1)
+            at = where_from + (m + 32 * f)
+            g = jnp.concatenate(
+                [jnp.take_along_axis(edges[q, h : h + 8], at, axis=1) for h in (0, 8)], axis=0
             )
             g = jnp.where(border, c, g)
+            w = jnp.where(ghost_w, g, w)
+            e = jnp.where(ghost_e, g, e)
+            across[t, f] = w + e
+            if f == 0:
+                grad = 0.5 * (e - w)
+                slope[t] = grad * grad
+
+    def between(t, carry):
+        one(t, cen.at[t - 1], cen.at[t + 1])
+        return carry
+
+    one(0, outside.at[0], cen.at[1])
+    lax.fori_loop(1, TILES - 1, between, 0, unroll=22)
+    one(TILES - 1, cen.at[TILES - 2], outside.at[1])
+
+
+def step_kernel(plan, cen, across, slope, from_below, from_above, out, held, sems):
+    sub = lax.axis_index("sub")
+    count = plan[MISC * 64 + 1]
+    lane = lanes((ROWS, 128))
+    row = lax.broadcasted_iota(jnp.int32, (ROWS, 128), 0)
+    at_bottom = sub == 0
+    at_top = sub == lax.axis_size("sub") - 1
+
+    def one(t, carry):
+        live = jnp.where(lane < 64, 2 * t, 2 * t + 1) < count
+        center, south, north = [], [], []
+        for f in range(FIELDS):
+            c = cen[t, f]
             below = jnp.where(at_bottom, c[0:1], from_below[t, f : f + 1])
             above = jnp.where(at_top, c[15:16], from_above[t, f : f + 1])
             center.append(c)
-            west.append(jnp.where(ghost_w, g, w))
-            east.append(jnp.where(ghost_e, g, e))
             south.append(jnp.where(row == 0, below, pltpu.roll(c, 1, 0)))
             north.append(jnp.where(row == ROWS - 1, above, pltpu.roll(c, ROWS - 1, 0)))
-        stepped = advance(center, west, east, south, north)
+        stepped = advance(center, [across[t, f] for f in range(FIELDS)], slope[t], south, north)
         at = pl.ds(pl.multiple_of(t * 128, 128), 128)
         for f in range(FIELDS):
-            out[f, :, at] = jnp.where(live, stepped[f], 0.0)
+            held[f, :, at] = jnp.where(live, stepped[f], 0.0)
         return carry
 
-    lax.fori_loop(0, TILES, one, 0)
-
-
+    copies = []
+    for part in range(PARTS):
+        each = TILES // PARTS
+        lax.fori_loop(part * each, (part + 1) * each, one, 0, unroll=UNROLL)
+        columns = pl.ds(part * each * 128, each * 128)
+        copies.append(pltpu.make_async_copy(held.at[:, :, columns], out.at[:, :, columns], sems.at[part]))
+        copies[-1].start()
+    for copy in copies:
+        copy.wait()
+
+
+PARTS = 4
+UNROLL = 6
 SMEM = pl.BlockSpec(memory_space=pltpu.SMEM)
 VMEM = pl.BlockSpec(memory_space=pltpu.VMEM)
+HBM = pl.BlockSpec(memory_space=pltpu.HBM)
 PARAMS = pltpu.CompilerParams(vmem_limit_bytes=32 * 1024 * 1024)
 
 
@@ -332,10 +379,18 @@
         pack_kernel,
         name="pack",
         out_shape=(f32(SLABS, MSG_ROWS, 128), i32(SLABS)),
-        in_specs=[SMEM, SMEM, SMEM, VMEM, VMEM],
+        in_specs=[HBM] * 5,
         out_specs=(VMEM, SMEM),
-        scratch_shapes=[pltpu.VMEM((BOX_DEV, BOX_ROWS, 128), jnp.float32)],
-        compiler_params=PARAMS,
+        scratch_shapes=[
+            pltpu.SMEM((NBOX,), jnp.int32),
+            pltpu.SMEM((SLABS,), jnp.int32),
+            pltpu.SMEM((NBOX,), jnp.int32),
+            pltpu.VMEM((FIELDS, ROWS, BOX_DEV * BX), jnp.float32),
+            pltpu.VMEM((FIELDS, ROWS // 2, PPD * BX // 2), jnp.float32),
+            pltpu.VMEM((BOX_DEV, BOX_ROWS, 128), jnp.float32),
+            pltpu.SemaphoreType.DMA((5,)),
+        ],
+        compiler_params=pltpu.CompilerParams(vmem_limit_bytes=62914560),
     )(old_owner, new_counts, box_pos, fine_old, coarse)
     incoming = lax.all_to_all(outgoing, "slab", 0, 0, tiled=True)
     plan = pl.pallas_call(
@@ -359,18 +414,32 @@
     sibling = lax.ppermute(sibling, "slab", [(i, i ^ 1) for i in range(SLABS)])
     from_below = lax.ppermute(high_rows, "sub", up)
     from_above = lax.ppermute(low_rows, "sub", [(b, a) for a, b in up])
+    cells = (TILES, FIELDS, ROWS, 128)
+    cen, across, slope = pl.pallas_call(
+        middle_kernel,
+        name="middle",
+        out_shape=(f32(*cells), f32(*cells), f32(TILES, ROWS, 128)),
+        in_specs=[SMEM, VMEM, VMEM],
+        out_specs=(VMEM, VMEM, VMEM),
+        scratch_shapes=[
+            pltpu.VMEM((4, ROWS, 128), jnp.float32),
+            pltpu.VMEM((2, FIELDS, ROWS, 128), jnp.float32),
+        ],
+        cost_estimate=pl.CostEstimate(flops=8_000_000, bytes_accessed=8_000_000, transcendentals=0),
+        compiler_params=PARAMS,
+    )(plan, incoming, sibling)
     return pl.pallas_call(
         step_kernel,
         name="step",
         out_shape=f32(FIELDS, ROWS, MOST * BX),
-        in_specs=[SMEM] + [VMEM] * 4,
-        out_specs=VMEM,
+        in_specs=[SMEM] + [VMEM] * 5,
+        out_specs=HBM,
         scratch_shapes=[
-            pltpu.VMEM((TILES + 2, FIELDS, ROWS, 128), jnp.float32),
-            pltpu.VMEM((4, ROWS, 128), jnp.float32),
+            pltpu.VMEM((FIELDS, ROWS, MOST * BX), jnp.float32),
+            pltpu.SemaphoreType.DMA((PARTS,)),
         ],
         compiler_params=PARAMS,
-    )(plan, incoming, from_below, from_above, sibling)
+    )(plan, cen, across, slope, from_below, from_above)
 
 
 def solution(mesh):

time: 74.5 us -> 64.6 us (0.87)
  Pallas kernels: 15.8 us -> 11.8 us
  local copies, waits for them, and re-layouts: 3.99 us -> 0.03 us
  waiting for transfers between devices: 34.1 us -> 32 us
    pallas_call x1, Pallas kernels: 7.35 us -> 1.91 us  [body(): pl.pallas_call(step_kernel, name='step', out_shape=f32(FIELDS, ROWS, MOST...]
    unnamed x16 -> x8, local copies, waits for them, and re-layouts: 3.99 us -> 0.03 us
    ppermute x1, waiting for transfers between devices: 2.18 us -> 0.08 us  [body(): from_above = lax.ppermute(low_rows, 'sub', [(b, a) for a, b in up])]
    pallas_call x0 -> x1, Pallas kernels: none -> 2.09 us  [body(): pl.pallas_call(middle_kernel, name='middle', out_shape=(f32(*cells), f32(...]
    pallas_call x1, Pallas kernels: 1.87 us -> 1.11 us  [body(): pl.pallas_call(edge_kernel, name='edges', out_shape=(f32(TILES, FIELDS, 1...]
  transfers between devices with their start and end apart: 4 -> 4, of which waited for: 3 -> 3; matrix products, arithmetic and copies ran while one was open for 0% -> 0% of each run, Pallas kernels for 5% -> 9%
where the time goes in v2:
time: 64.6 us; the launch traced here: 64 us
  waiting for transfers between devices  32 us (50%)
  starting transfers between devices  20 us (31%)
  Pallas kernels  11.8 us (18%)
    all_to_all x1, waiting for transfers between devices, body(): incoming = lax.all_to_all(outgoing, 'slab', 0, 0, tiled=True)  30.7 us
    all_to_all x1, starting transfers between devices, body(): incoming = lax.all_to_all(outgoing, 'slab', 0, 0, tiled=True)  10.7 us
    ppermute x1, starting transfers between devices, body(): from_below = lax.ppermute(high_rows, 'sub', up)  5.49 us
    pallas_call x1, Pallas kernels, body(): pl.pallas_call(plan_kernel, name='plan', out_shape=i32(8 * 64), in_specs=...  3.72 us
    pallas_call x1, Pallas kernels, body(): pl.pallas_call(pack_kernel, name='pack', out_shape=(f32(SLABS, MSG_ROWS,...  2.97 us
    pallas_call x1, Pallas kernels, body(): pl.pallas_call(middle_kernel, name='middle', out_shape=(f32(*cells), f32(...  2.09 us
    ppermute x1, starting transfers between devices, body(): from_above = lax.ppermute(low_rows, 'sub', [(b, a) for a, b in up])  1.92 us
    ppermute x1, starting transfers between devices, body(): sibling = lax.ppermute(sibling, 'slab', [(i, i ^ 1) for i in range(SLABS)])  1.92 us
  transfers between devices with their start and end apart: 4, of which 3 were waited for; matrix products, arithmetic and copies ran while one was open for 0% of the time, Pallas kernels for 9%

profile of v2, /device:TPU:192, one launch (start us, length us, event | category | flops | bytes accessed | tf_op | source)
XLA Modules:
  0.0 64.0 jit_solution(17192714070083409419)
XLA Ops:
  0.0 3.0 %pack.1 = (f32[64,40,128]{2,1,0:T(8,128)}, s32[64]{0:T(128)}) custom-call(s32[1536]{0:T(1024)} %owner.1, s32[64]{0:T(128)} %counts.1, s32[1536]{0:T(1024)} %pos.1, f32[4,16,1536]{2,1,0:T(8,128)} %fine_in.1, f32[4,8,1536]{2,1,0:T(8,128)} %coarse_in.1), custom_call_target="tpu_custom_call" | custom-call | tf_op jit(solution)/shard_map/pack/pallas_call | solution.py:378
  3.0 0.0 copy-start
  3.0 0.0 copy-start.1
  3.0 0.0 copy-start.2
  3.0 0.0 copy-start.3
  3.0 10.7 %all-to-all-start = ((f32[64,40,128]{2,1,0:T(8,128)}), f32[64,40,128]{2,1,0:T(8,128)S(1)}, u32[]{:S(2)}, u32[]{:S(2)}) async-start(f32[64,40,128]{2,1,0:T(8,128)} %get-tuple-element.14), calls=%async_computation | async-start | bytes 2621440 | tf_op jit(solution)/shard_map/all_to_all | solution.py:395
  13.8 0.0 copy-done
  13.8 0.0 copy-done.1
  13.8 0.0 copy-done.2
  13.8 0.0 copy-done.3
  13.8 3.7 %plan.1 = s32[512]{0:T(512)S(1)} custom-call(s32[1536]{0:T(1024)S(1)} %copy-done, s32[64]{0:T(128)S(1)} %copy-done.2, s32[1536]{0:T(1024)S(1)} %copy-done.1, s32[64]{0:T(128)S(1)} %copy-done.3), custom_call_target="tpu_custom_call" | custom-call | tf_op jit(solution)/shard_map/plan/pallas_call | solution.py:396
  17.5 30.7 %all-to-all-done.inc = f32[64,40,128]{2,1,0:T(8,128)S(1)} async-done(((f32[64,40,128]{2,1,0:T(8,128)}), f32[64,40,128]{2,1,0:T(8,128)S(1)}, u32[]{:S(2)}, u32[]{:S(2)}) %all-to-all-start) | async-done | bytes 1310752 | tf_op jit(solution)/shard_map/all_to_all | solution.py:395
  48.3 1.1 %edges.1 = (f32[24,4,128]{2,1,0:T(4,128)S(1)}, f32[24,4,128]{2,1,0:T(4,128)S(1)}, f32[4,8,128]{2,1,0:T(8,128)S(1)}) custom-call(s32[512]{0:T(512)S(1)} %plan.1, f32[64,40,128]{2,1,0:T(8,128)S(1)} %all-to-all-done.inc), custom_call_target="tpu_custom_call" | custom-call | tf_op jit(solution)/shard_map/edges/pallas_call | solution.py:404
  49.4 5.5 %collective-permute-start.1 = (f32[24,4,128]{2,1,0:T(4,128)S(1)}, f32[24,4,128]{2,1,0:T(4,128)S(1)}, u32[]{:S(2)}, u32[]{:S(2)}) collective-permute-start(f32[24,4,128]{2,1,0:T(4,128)S(1)} %get-tuple-element.19), channel_id=1, source_target_pairs={{0,1},{1,2},{2,3},{3,4},{4,5},{5,6},{6,7},{7,8},{8,9},{9,10},{10,1... | collective-permute-start | bytes 147464 | tf_op jit(solution)/shard_map/ppermute | solution.py:415
  54.9 1.9 %collective-permute-start.2 = (f32[24,4,128]{2,1,0:T(4,128)S(1)}, f32[24,4,128]{2,1,0:T(4,128)S(1)}, u32[]{:S(2)}, u32[]{:S(2)}) collective-permute-start(f32[24,4,128]{2,1,0:T(4,128)S(1)} %get-tuple-element.20), channel_id=1, source_target_pairs={{1,0},{2,1},{3,2},{4,3},{5,4},{6,5},{7,6},{8,7},{9,8},{10,9},{11,1... | collective-permute-start | bytes 147464 | tf_op jit(solution)/shard_map/ppermute | solution.py:416
  56.8 1.9 %collective-permute-start = (f32[4,8,128]{2,1,0:T(8,128)S(1)}, f32[4,8,128]{2,1,0:T(8,128)S(1)}, u32[]{:S(2)}, u32[]{:S(2)}) collective-permute-start(f32[4,8,128]{2,1,0:T(8,128)S(1)} %get-tuple-element.15), channel_id=1, source_target_pairs={{0,12},{12,0},{24,36},{36,24},{48,60},{60,48},{72,84},{84,72},{96,... | collective-permute-start | bytes 49160 | tf_op jit(solution)/shard_map/ppermute | solution.py:414
  58.7 1.1 %collective-permute-done.sibling = f32[4,8,128]{2,1,0:T(8,128)S(1)} collective-permute-done((f32[4,8,128]{2,1,0:T(8,128)S(1)}, f32[4,8,128]{2,1,0:T(8,128)S(1)}, u32[]{:S(2)}, u32[]{:S(2)}) %collective-permute-start) | collective-permute-done | bytes 16416 | tf_op jit(solution)/shard_map/ppermute | solution.py:414
  59.9 2.1 %middle.1 = (f32[24,4,16,128]{3,2,1,0:T(8,128)S(1)}, f32[24,4,16,128]{3,2,1,0:T(8,128)S(1)}, f32[24,16,128]{2,1,0:T(8,128)S(1)}) custom-call(s32[512]{0:T(512)S(1)} %plan.1, f32[64,40,128]{2,1,0:T(8,128)S(1)} %all-to-all-done.inc, f32[4,8,128]{2,1,0:T(8,128)S(1)} %collective-permute-done.sibling), custom_call_target="tpu_custom_call" | custom-call | flops 8000000 | bytes 8000000 | tf_op jit(solution)/shard_map/middle/pallas_call | solution.py:418
  62.0 0.0 collective-permute-done.1.from_below
  62.0 0.1 collective-permute-done.2.from_above
  62.1 1.9 %step.1 = f32[4,16,3072]{2,1,0:T(8,128)} custom-call(s32[512]{0:T(512)S(1)} %plan.1, f32[24,4,16,128]{3,2,1,0:T(8,128)S(1)} %get-tuple-element.16.cen, f32[24,4,16,128]{3,2,1,0:T(8,128)S(1)} %get-tuple-element.17.across, f32[24,16,128]{2,1,0:T(8,128)S(1)} %get-tuple-element.18.slope, f32[24,4,128]{2,1,0:T(4,128)S(1)} %collective-permute-done.1.from_below, ...), custom_call_target="tpu_custom_call" | custom-call | tf_op jit(solution)/shard_map/step/pallas_call | solution.py:431
Async XLA Ops:
  3.0 10.8 %copy-start = (s32[1536]{0:T(1024)S(1)}, s32[1536]{0:T(1024)}, u32[]{:S(2)}) copy-start(s32[1536]{0:T(1024)} %owner.1) | copy-start | bytes 18436
  3.0 10.8 %copy-start.1 = (s32[1536]{0:T(1024)S(1)}, s32[1536]{0:T(1024)}, u32[]{:S(2)}) copy-start(s32[1536]{0:T(1024)} %pos.1) | copy-start | bytes 18436
  3.0 10.8 %copy-start.2 = (s32[64]{0:T(128)S(1)}, s32[64]{0:T(128)}, u32[]{:S(2)}) copy-start(s32[64]{0:T(128)} %counts.1) | copy-start | bytes 772
  3.0 10.8 %copy-start.3 = (s32[64]{0:T(128)S(1)}, s32[64]{0:T(128)}, u32[]{:S(2)}) copy-start(s32[64]{0:T(128)} %get-tuple-element.13.starts) | copy-start | bytes 772
  3.0 45.2 %all-to-all-start = ((f32[64,40,128]{2,1,0:T(8,128)}), f32[64,40,128]{2,1,0:T(8,128)S(1)}, u32[]{:S(2)}, u32[]{:S(2)}) async-start(f32[64,40,128]{2,1,0:T(8,128)} %get-tuple-element.14), calls=%async_computation | async-start | bytes 2621440 | tf_op jit(solution)/shard_map/all_to_all | solution.py:395
  49.4 12.6 %collective-permute-start.1 = (f32[24,4,128]{2,1,0:T(4,128)S(1)}, f32[24,4,128]{2,1,0:T(4,128)S(1)}, u32[]{:S(2)}, u32[]{:S(2)}) collective-permute-start(f32[24,4,128]{2,1,0:T(4,128)S(1)} %get-tuple-element.19), channel_id=1, source_target_pairs={{0,1},{1,2},{2,3},{3,4},{4,5},{5,6},{6,7},{7,8},{8,9},{9,10},{10,1... | collective-permute-start | bytes 147464 | tf_op jit(solution)/shard_map/ppermute | solution.py:415
  54.9 7.2 %collective-permute-start.2 = (f32[24,4,128]{2,1,0:T(4,128)S(1)}, f32[24,4,128]{2,1,0:T(4,128)S(1)}, u32[]{:S(2)}, u32[]{:S(2)}) collective-permute-start(f32[24,4,128]{2,1,0:T(4,128)S(1)} %get-tuple-element.20), channel_id=1, source_target_pairs={{1,0},{2,1},{3,2},{4,3},{5,4},{6,5},{7,6},{8,7},{9,8},{10,9},{11,1... | collective-permute-start | bytes 147464 | tf_op jit(solution)/shard_map/ppermute | solution.py:416
  56.8 3.1 %collective-permute-start = (f32[4,8,128]{2,1,0:T(8,128)S(1)}, f32[4,8,128]{2,1,0:T(8,128)S(1)}, u32[]{:S(2)}, u32[]{:S(2)}) collective-permute-start(f32[4,8,128]{2,1,0:T(8,128)S(1)} %get-tuple-element.15), channel_id=1, source_target_pairs={{0,12},{12,0},{24,36},{36,24},{48,60},{60,48},{72,84},{84,72},{96,... | collective-permute-start | bytes 49160 | tf_op jit(solution)/shard_map/ppermute | solution.py:414

commit v3 on v2

--- a/solution.py
+++ b/solution.py
@@ -246,10 +246,27 @@
     )
 
 
-def middle_kernel(plan, inc, sibling, cen, across, slope, edges, outside):
+def whole_rows(coarse_rows, edges):
+    row = lax.broadcasted_iota(jnp.int32, (8, 128), 0) >> 1
+    for n, x in enumerate(coarse_rows):
+        edges[n, 0:8] = jnp.take_along_axis(x, row, axis=0)
+        edges[n, 8:16] = jnp.take_along_axis(x, 4 + row, axis=0)
+
+
+def ghost_source():
+    lane = lanes()
+    return jnp.where(lane >= 64, 1, 0) + jnp.where((lane & 63) >= 32, QUARTER, 0)
+
+
+def ghosts_of(edges, t, f, where_from):
+    q = (2 * t * 43691) >> 19
+    at = where_from + (2 * t - q * QUARTER + 32 * f)
+    return jnp.concatenate([jnp.take_along_axis(edges[q, h : h + 8], at, axis=1) for h in (0, 8)], axis=0)
+
+
+def middle_kernel(plan, inc, cen, across, slope, edges, outside):
     lane = lanes()
     low = lane < 64
-    row8 = lax.broadcasted_iota(jnp.int32, (8, 128), 0)
     start = plan[MISC * 64]
 
     def unpack(a, b, put):
@@ -274,20 +291,12 @@
 
         unpack(plan[SRC * 64 + s], plan[SRC * 64 + s + 1], put)
 
-    own = gather_edges(plan, inc, OWN_L, OWN_R)
-    for n in range(4):
-        whole = own[n] + sibling[n]
-        edges[n, 0:8] = jnp.take_along_axis(whole, row8 >> 1, axis=0)
-        edges[n, 8:16] = jnp.take_along_axis(whole, 4 + (row8 >> 1), axis=0)
-
+    whole_rows(gather_edges(plan, inc, OWN_L, OWN_R), edges)
     lane = lanes((ROWS, 128))
-    near = lanes()
-    where_from = jnp.where(near >= 64, 1, 0) + jnp.where((near & 63) >= 32, QUARTER, 0)
+    where_from = ghost_source()
 
     def one(t, before, after):
         s = 2 * t
-        q = (s * 43691) >> 19
-        m = s - q * QUARTER
         fl0, fl1 = plan[FINE_L * 64 + s] == 1, plan[FINE_L * 64 + s + 1] == 1
         fr0, fr1 = plan[FINE_R * 64 + s] == 1, plan[FINE_R * 64 + s + 1] == 1
         k = start + s
@@ -302,17 +311,13 @@
             c = cen[t, f]
             w = pltpu.roll(jnp.where(lane == 127, before[f], c), 1, 1)
             e = pltpu.roll(jnp.where(lane == 0, after[f], c), 127, 1)
-            at = where_from + (m + 32 * f)
-            g = jnp.concatenate(
-                [jnp.take_along_axis(edges[q, h : h + 8], at, axis=1) for h in (0, 8)], axis=0
-            )
+            g = ghosts_of(edges, t, f, where_from)
             g = jnp.where(border, c, g)
             w = jnp.where(ghost_w, g, w)
             e = jnp.where(ghost_e, g, e)
             across[t, f] = w + e
             if f == 0:
-                grad = 0.5 * (e - w)
-                slope[t] = grad * grad
+                slope[t] = e - w
 
     def between(t, carry):
         one(t, cen.at[t - 1], cen.at[t + 1])
@@ -323,25 +328,33 @@
     one(TILES - 1, cen.at[TILES - 2], outside.at[1])
 
 
-def step_kernel(plan, cen, across, slope, from_below, from_above, out, held, sems):
+def step_kernel(plan, cen, across, slope, sibling, from_below, from_above, out, held, edges, sems):
     sub = lax.axis_index("sub")
     count = plan[MISC * 64 + 1]
     lane = lanes((ROWS, 128))
     row = lax.broadcasted_iota(jnp.int32, (ROWS, 128), 0)
     at_bottom = sub == 0
     at_top = sub == lax.axis_size("sub") - 1
+    right = (lane & 63) >= 32
+    where_from = ghost_source()
+    whole_rows([sibling[n] for n in range(4)], edges)
 
     def one(t, carry):
         live = jnp.where(lane < 64, 2 * t, 2 * t + 1) < count
-        center, south, north = [], [], []
+        center, sides, south, north = [], [], [], []
         for f in range(FIELDS):
             c = cen[t, f]
             below = jnp.where(at_bottom, c[0:1], from_below[t, f : f + 1])
             above = jnp.where(at_top, c[15:16], from_above[t, f : f + 1])
+            g = ghosts_of(edges, t, f, where_from)
+            g = jnp.where(((lane + 1) & 63) < 2, g, 0.0)
+            if f == 0:
+                grad_x = 0.5 * (slope[t] + jnp.where(right, g, -g))
             center.append(c)
+            sides.append(across[t, f] + g)
             south.append(jnp.where(row == 0, below, pltpu.roll(c, 1, 0)))
             north.append(jnp.where(row == ROWS - 1, above, pltpu.roll(c, ROWS - 1, 0)))
-        stepped = advance(center, [across[t, f] for f in range(FIELDS)], slope[t], south, north)
+        stepped = advance(center, sides, grad_x * grad_x, south, north)
         at = pl.ds(pl.multiple_of(t * 128, 128), 128)
         for f in range(FIELDS):
             held[f, :, at] = jnp.where(live, stepped[f], 0.0)
@@ -419,7 +432,7 @@
         middle_kernel,
         name="middle",
         out_shape=(f32(*cells), f32(*cells), f32(TILES, ROWS, 128)),
-        in_specs=[SMEM, VMEM, VMEM],
+        in_specs=[SMEM, VMEM],
         out_specs=(VMEM, VMEM, VMEM),
         scratch_shapes=[
             pltpu.VMEM((4, ROWS, 128), jnp.float32),
@@ -427,19 +440,20 @@
         ],
         cost_estimate=pl.CostEstimate(flops=8_000_000, bytes_accessed=8_000_000, transcendentals=0),
         compiler_params=PARAMS,
-    )(plan, incoming, sibling)
+    )(plan, incoming)
     return pl.pallas_call(
         step_kernel,
         name="step",
         out_shape=f32(FIELDS, ROWS, MOST * BX),
-        in_specs=[SMEM] + [VMEM] * 5,
+        in_specs=[SMEM] + [VMEM] * 6,
         out_specs=HBM,
         scratch_shapes=[
             pltpu.VMEM((FIELDS, ROWS, MOST * BX), jnp.float32),
+            pltpu.VMEM((4, ROWS, 128), jnp.float32),
             pltpu.SemaphoreType.DMA((PARTS,)),
         ],
         compiler_params=PARAMS,
-    )(plan, cen, across, slope, from_below, from_above)
+    )(plan, cen, across, slope, sibling, from_below, from_above)
 
 
 def solution(mesh):

time: 64.6 us -> 64.5 us (level)
    ppermute x1, waiting for transfers between devices: 1.15 us -> 0.01 us  [body(): sibling = lax.ppermute(sibling, 'slab', [(i, i ^ 1) for i in range(SLABS)])]
    ppermute x1, waiting for transfers between devices: 0.08 us -> 1.22 us  [body(): from_above = lax.ppermute(low_rows, 'sub', [(b, a) for a, b in up])]
  transfers between devices with their start and end apart: 4 -> 4, of which waited for: 3 -> 2; matrix products, arithmetic and copies ran while one was open for 0% -> 0% of each run, Pallas kernels for 9% -> 9%
where the time goes in v3:
time: 64.5 us; the launch traced here: 64.2 us
  waiting for transfers between devices  32 us (50%)
  starting transfers between devices  20 us (31%)
  Pallas kernels  12 us (19%)
    all_to_all x1, waiting for transfers between devices, body(): incoming = lax.all_to_all(outgoing, 'slab', 0, 0, tiled=True)  30.7 us
    all_to_all x1, starting transfers between devices, body(): incoming = lax.all_to_all(outgoing, 'slab', 0, 0, tiled=True)  10.7 us
    ppermute x1, starting transfers between devices, body(): from_below = lax.ppermute(high_rows, 'sub', up)  5.49 us
    pallas_call x1, Pallas kernels, body(): pl.pallas_call(plan_kernel, name='plan', out_shape=i32(8 * 64), in_specs=...  3.72 us
    pallas_call x1, Pallas kernels, body(): pl.pallas_call(pack_kernel, name='pack', out_shape=(f32(SLABS, MSG_ROWS,...  2.97 us
    pallas_call x1, Pallas kernels, body(): pl.pallas_call(middle_kernel, name='middle', out_shape=(f32(*cells), f32(...  2.09 us
    pallas_call x1, Pallas kernels, body(): pl.pallas_call(step_kernel, name='step', out_shape=f32(FIELDS, ROWS, MOST...  2.09 us
    ppermute x1, starting transfers between devices, body(): from_above = lax.ppermute(low_rows, 'sub', [(b, a) for a, b in up])  1.92 us
  transfers between devices with their start and end apart: 4, of which 2 were waited for; matrix products, arithmetic and copies ran while one was open for 0% of the time, Pallas kernels for 9%

profile of v3, /device:TPU:192, one launch (start us, length us, event | category | flops | bytes accessed | tf_op | source)
XLA Modules:
  0.0 64.2 jit_solution(8940534647413572687)
XLA Ops:
  0.0 3.0 %pack.1 = (f32[64,40,128]{2,1,0:T(8,128)}, s32[64]{0:T(128)}) custom-call(s32[1536]{0:T(1024)} %owner.1, s32[64]{0:T(128)} %counts.1, s32[1536]{0:T(1024)} %pos.1, f32[4,16,1536]{2,1,0:T(8,128)} %fine_in.1, f32[4,8,1536]{2,1,0:T(8,128)} %coarse_in.1), custom_call_target="tpu_custom_call" | custom-call | tf_op jit(solution)/shard_map/pack/pallas_call | solution.py:391
  3.0 0.0 copy-start
  3.0 0.0 copy-start.1
  3.0 0.0 copy-start.2
  3.0 0.0 copy-start.3
  3.0 10.7 %all-to-all-start = ((f32[64,40,128]{2,1,0:T(8,128)}), f32[64,40,128]{2,1,0:T(8,128)S(1)}, u32[]{:S(2)}, u32[]{:S(2)}) async-start(f32[64,40,128]{2,1,0:T(8,128)} %get-tuple-element.14), calls=%async_computation | async-start | bytes 2621440 | tf_op jit(solution)/shard_map/all_to_all | solution.py:408
  13.8 0.0 copy-done
  13.8 0.0 copy-done.1
  13.8 0.0 copy-done.2
  13.8 0.0 copy-done.3
  13.8 3.7 %plan.1 = s32[512]{0:T(512)S(1)} custom-call(s32[1536]{0:T(1024)S(1)} %copy-done, s32[64]{0:T(128)S(1)} %copy-done.2, s32[1536]{0:T(1024)S(1)} %copy-done.1, s32[64]{0:T(128)S(1)} %copy-done.3), custom_call_target="tpu_custom_call" | custom-call | tf_op jit(solution)/shard_map/plan/pallas_call | solution.py:409
  17.5 30.7 %all-to-all-done.inc = f32[64,40,128]{2,1,0:T(8,128)S(1)} async-done(((f32[64,40,128]{2,1,0:T(8,128)}), f32[64,40,128]{2,1,0:T(8,128)S(1)}, u32[]{:S(2)}, u32[]{:S(2)}) %all-to-all-start) | async-done | bytes 1310752 | tf_op jit(solution)/shard_map/all_to_all | solution.py:408
  48.3 1.1 %edges.1 = (f32[24,4,128]{2,1,0:T(4,128)S(1)}, f32[24,4,128]{2,1,0:T(4,128)S(1)}, f32[4,8,128]{2,1,0:T(8,128)S(1)}) custom-call(s32[512]{0:T(512)S(1)} %plan.1, f32[64,40,128]{2,1,0:T(8,128)S(1)} %all-to-all-done.inc), custom_call_target="tpu_custom_call" | custom-call | tf_op jit(solution)/shard_map/edges/pallas_call | solution.py:417
  49.4 5.5 %collective-permute-start.1 = (f32[24,4,128]{2,1,0:T(4,128)S(1)}, f32[24,4,128]{2,1,0:T(4,128)S(1)}, u32[]{:S(2)}, u32[]{:S(2)}) collective-permute-start(f32[24,4,128]{2,1,0:T(4,128)S(1)} %get-tuple-element.19), channel_id=1, source_target_pairs={{0,1},{1,2},{2,3},{3,4},{4,5},{5,6},{6,7},{7,8},{8,9},{9,10},{10,1... | collective-permute-start | bytes 147464 | tf_op jit(solution)/shard_map/ppermute | solution.py:428
  54.9 1.9 %collective-permute-start.2 = (f32[24,4,128]{2,1,0:T(4,128)S(1)}, f32[24,4,128]{2,1,0:T(4,128)S(1)}, u32[]{:S(2)}, u32[]{:S(2)}) collective-permute-start(f32[24,4,128]{2,1,0:T(4,128)S(1)} %get-tuple-element.20), channel_id=1, source_target_pairs={{1,0},{2,1},{3,2},{4,3},{5,4},{6,5},{7,6},{8,7},{9,8},{10,9},{11,1... | collective-permute-start | bytes 147464 | tf_op jit(solution)/shard_map/ppermute | solution.py:429
  56.8 1.9 %collective-permute-start = (f32[4,8,128]{2,1,0:T(8,128)S(1)}, f32[4,8,128]{2,1,0:T(8,128)S(1)}, u32[]{:S(2)}, u32[]{:S(2)}) collective-permute-start(f32[4,8,128]{2,1,0:T(8,128)S(1)} %get-tuple-element.18), channel_id=1, source_target_pairs={{0,12},{12,0},{24,36},{36,24},{48,60},{60,48},{72,84},{84,72},{96,... | collective-permute-start | bytes 49160 | tf_op jit(solution)/shard_map/ppermute | solution.py:427
  58.7 2.1 %middle.1 = (f32[24,4,16,128]{3,2,1,0:T(8,128)S(1)}, f32[24,4,16,128]{3,2,1,0:T(8,128)S(1)}, f32[24,16,128]{2,1,0:T(8,128)S(1)}) custom-call(s32[512]{0:T(512)S(1)} %plan.1, f32[64,40,128]{2,1,0:T(8,128)S(1)} %all-to-all-done.inc), custom_call_target="tpu_custom_call" | custom-call | flops 8000000 | bytes 8000000 | tf_op jit(solution)/shard_map/middle/pallas_call | solution.py:431
  60.8 0.0 collective-permute-done.sibling
  60.8 0.0 collective-permute-done.1.from_below
  60.9 1.2 %collective-permute-done.2.from_above = f32[24,4,128]{2,1,0:T(4,128)S(1)} collective-permute-done((f32[24,4,128]{2,1,0:T(4,128)S(1)}, f32[24,4,128]{2,1,0:T(4,128)S(1)}, u32[]{:S(2)}, u32[]{:S(2)}) %collective-permute-start.2) | collective-permute-done | bytes 49184 | tf_op jit(solution)/shard_map/ppermute | solution.py:429
  62.1 2.1 %step.1 = f32[4,16,3072]{2,1,0:T(8,128)} custom-call(s32[512]{0:T(512)S(1)} %plan.1, f32[24,4,16,128]{3,2,1,0:T(8,128)S(1)} %get-tuple-element.15.cen, f32[24,4,16,128]{3,2,1,0:T(8,128)S(1)} %get-tuple-element.16.across, f32[24,16,128]{2,1,0:T(8,128)S(1)} %get-tuple-element.17.slope, f32[4,8,128]{2,1,0:T(8,128)S(1)} %collective-permute-done.sibling, ...), custom_call_target="tpu_custom_call" | custom-call | tf_op jit(solution)/shard_map/step/pallas_call | solution.py:444
Async XLA Ops:
  3.0 10.8 %copy-start = (s32[1536]{0:T(1024)S(1)}, s32[1536]{0:T(1024)}, u32[]{:S(2)}) copy-start(s32[1536]{0:T(1024)} %owner.1) | copy-start | bytes 18436
  3.0 10.8 %copy-start.1 = (s32[1536]{0:T(1024)S(1)}, s32[1536]{0:T(1024)}, u32[]{:S(2)}) copy-start(s32[1536]{0:T(1024)} %pos.1) | copy-start | bytes 18436
  3.0 10.8 %copy-start.2 = (s32[64]{0:T(128)S(1)}, s32[64]{0:T(128)}, u32[]{:S(2)}) copy-start(s32[64]{0:T(128)} %counts.1) | copy-start | bytes 772
  3.0 10.8 %copy-start.3 = (s32[64]{0:T(128)S(1)}, s32[64]{0:T(128)}, u32[]{:S(2)}) copy-start(s32[64]{0:T(128)} %get-tuple-element.13.starts) | copy-start | bytes 772
  3.0 45.2 %all-to-all-start = ((f32[64,40,128]{2,1,0:T(8,128)}), f32[64,40,128]{2,1,0:T(8,128)S(1)}, u32[]{:S(2)}, u32[]{:S(2)}) async-start(f32[64,40,128]{2,1,0:T(8,128)} %get-tuple-element.14), calls=%async_computation | async-start | bytes 2621440 | tf_op jit(solution)/shard_map/all_to_all | solution.py:408
  49.4 11.5 %collective-permute-start.1 = (f32[24,4,128]{2,1,0:T(4,128)S(1)}, f32[24,4,128]{2,1,0:T(4,128)S(1)}, u32[]{:S(2)}, u32[]{:S(2)}) collective-permute-start(f32[24,4,128]{2,1,0:T(4,128)S(1)} %get-tuple-element.19), channel_id=1, source_target_pairs={{0,1},{1,2},{2,3},{3,4},{4,5},{5,6},{6,7},{7,8},{8,9},{9,10},{10,1... | collective-permute-start | bytes 147464 | tf_op jit(solution)/shard_map/ppermute | solution.py:428
  54.9 7.2 %collective-permute-start.2 = (f32[24,4,128]{2,1,0:T(4,128)S(1)}, f32[24,4,128]{2,1,0:T(4,128)S(1)}, u32[]{:S(2)}, u32[]{:S(2)}) collective-permute-start(f32[24,4,128]{2,1,0:T(4,128)S(1)} %get-tuple-element.20), channel_id=1, source_target_pairs={{1,0},{2,1},{3,2},{4,3},{5,4},{6,5},{7,6},{8,7},{9,8},{10,9},{11,1... | collective-permute-start | bytes 147464 | tf_op jit(solution)/shard_map/ppermute | solution.py:429
  56.8 4.0 %collective-permute-start = (f32[4,8,128]{2,1,0:T(8,128)S(1)}, f32[4,8,128]{2,1,0:T(8,128)S(1)}, u32[]{:S(2)}, u32[]{:S(2)}) collective-permute-start(f32[4,8,128]{2,1,0:T(8,128)S(1)} %get-tuple-element.18), channel_id=1, source_target_pairs={{0,12},{12,0},{24,36},{36,24},{48,60},{60,48},{72,84},{84,72},{96,... | collective-permute-start | bytes 49160 | tf_op jit(solution)/shard_map/ppermute | solution.py:427

commit v4 on v3

--- a/solution.py
+++ b/solution.py
@@ -199,21 +199,20 @@
     return lax.fori_loop(0, QUARTER, one, (zero,) * 4, unroll=GU)
 
 
-def edge_kernel(plan, inc, low_rows, high_rows, sibling):
+def edge_kernel(plan, inc, first_rows, second_rows, sibling):
     low = lanes((1, 128)) < 64
+    odd = (lax.axis_index("sub") & 1) == 1
 
     def one(t, carry):
         a = plan[SRC * 64 + 2 + 2 * t]
         b = plan[SRC * 64 + 3 + 2 * t]
         for f in range(FIELDS):
             row = f * 8
-            low_rows[t, f : f + 1] = jnp.where(
-                low, inc[a, row : row + 1], pltpu.roll(inc[b, row : row + 1], 64, 1)
-            )
+            bottom = jnp.where(low, inc[a, row : row + 1], pltpu.roll(inc[b, row : row + 1], 64, 1))
             row = f * 8 + 7
-            high_rows[t, f : f + 1] = jnp.where(
-                low, pltpu.roll(inc[a, row : row + 1], 64, 1), inc[b, row : row + 1]
-            )
+            top = jnp.where(low, pltpu.roll(inc[a, row : row + 1], 64, 1), inc[b, row : row + 1])
+            first_rows[t, f : f + 1] = jnp.where(odd, top, bottom)
+            second_rows[t, f : f + 1] = jnp.where(odd, bottom, top)
         return carry
 
     lax.fori_loop(0, TILES, one, 0, unroll=24)
@@ -328,11 +327,12 @@
     one(TILES - 1, cen.at[TILES - 2], outside.at[1])
 
 
-def step_kernel(plan, cen, across, slope, sibling, from_below, from_above, out, held, edges, sems):
+def step_kernel(plan, cen, across, slope, sibling, first_rows, second_rows, out, held, edges, sems):
     sub = lax.axis_index("sub")
     count = plan[MISC * 64 + 1]
     lane = lanes((ROWS, 128))
     row = lax.broadcasted_iota(jnp.int32, (ROWS, 128), 0)
+    odd = (sub & 1) == 1
     at_bottom = sub == 0
     at_top = sub == lax.axis_size("sub") - 1
     right = (lane & 63) >= 32
@@ -344,8 +344,9 @@
         center, sides, south, north = [], [], [], []
         for f in range(FIELDS):
             c = cen[t, f]
-            below = jnp.where(at_bottom, c[0:1], from_below[t, f : f + 1])
-            above = jnp.where(at_top, c[15:16], from_above[t, f : f + 1])
+            one_side, other_side = first_rows[t, f : f + 1], second_rows[t, f : f + 1]
+            below = jnp.where(at_bottom, c[0:1], jnp.where(odd, other_side, one_side))
+            above = jnp.where(at_top, c[15:16], jnp.where(odd, one_side, other_side))
             g = ghosts_of(edges, t, f, where_from)
             g = jnp.where(((lane + 1) & 63) < 2, g, 0.0)
             if f == 0:
@@ -414,7 +415,7 @@
         out_specs=SMEM,
         compiler_params=PARAMS,
     )(old_owner, new_counts, box_pos, starts)
-    low_rows, high_rows, sibling = pl.pallas_call(
+    first_rows, second_rows, sibling = pl.pallas_call(
         edge_kernel,
         name="edges",
         out_shape=(f32(TILES, FIELDS, 128), f32(TILES, FIELDS, 128), f32(4, 8, 128)),
@@ -423,10 +424,11 @@
         compiler_params=PARAMS,
     )(plan, incoming)
     count = lax.axis_size("sub")
-    up = [(i, i + 1) for i in range(count - 1)]
+    pairs = [(i, i + 1) for i in range(count - 1)]
+    pairs = [pairs[start::2] + [(b, a) for a, b in pairs[start::2]] for start in (1, 0)]
+    first_rows = lax.ppermute(first_rows, "sub", pairs[0])
+    second_rows = lax.ppermute(second_rows, "sub", pairs[1])
     sibling = lax.ppermute(sibling, "slab", [(i, i ^ 1) for i in range(SLABS)])
-    from_below = lax.ppermute(high_rows, "sub", up)
-    from_above = lax.ppermute(low_rows, "sub", [(b, a) for a, b in up])
     cells = (TILES, FIELDS, ROWS, 128)
     cen, across, slope = pl.pallas_call(
         middle_kernel,
@@ -453,7 +455,7 @@
             pltpu.SemaphoreType.DMA((PARTS,)),
         ],
         compiler_params=PARAMS,
-    )(plan, cen, across, slope, sibling, from_below, from_above)
+    )(plan, cen, across, slope, sibling, first_rows, second_rows)
 
 
 def solution(mesh):

time: 64.5 us -> 66.3 us (1.028)
  the two profiles are of different devices: /device:TPU:192 before, /device:TPU:129 now
where the time goes in v4:
time: 66.3 us; the launch traced here: 66 us
  waiting for transfers between devices  29.8 us (45%)
  starting transfers between devices  24 us (36%)
  Pallas kernels  12 us (18%)
    all_to_all x1, waiting for transfers between devices, body(): incoming = lax.all_to_all(outgoing, 'slab', 0, 0, tiled=True)  29.8 us
    all_to_all x1, starting transfers between devices, body(): incoming = lax.all_to_all(outgoing, 'slab', 0, 0, tiled=True)  10.9 us
    ppermute x1, starting transfers between devices, body(): second_rows = lax.ppermute(second_rows, 'sub', pairs[1])  7.29 us
    ppermute x1, starting transfers between devices, body(): sibling = lax.ppermute(sibling, 'slab', [(i, i ^ 1) for i in range(SLABS)])  3.82 us
    pallas_call x1, Pallas kernels, body(): pl.pallas_call(plan_kernel, name='plan', out_shape=i32(8 * 64), in_specs=...  3.72 us
    pallas_call x1, Pallas kernels, body(): pl.pallas_call(pack_kernel, name='pack', out_shape=(f32(SLABS, MSG_ROWS,...  2.97 us
    pallas_call x1, Pallas kernels, body(): pl.pallas_call(step_kernel, name='step', out_shape=f32(FIELDS, ROWS, MOST...  2.13 us
    pallas_call x1, Pallas kernels, body(): pl.pallas_call(middle_kernel, name='middle', out_shape=(f32(*cells), f32(...  2.09 us
  transfers between devices with their start and end apart: 4, of which 1 were waited for; matrix products, arithmetic and copies ran while one was open for 0% of the time, Pallas kernels for 9%

profile of v4, /device:TPU:129, one launch (start us, length us, event | category | flops | bytes accessed | tf_op | source)
XLA Modules:
  0.0 66.0 jit_solution(15336942778167788212)
XLA Ops:
  0.0 3.0 %pack.1 = (f32[64,40,128]{2,1,0:T(8,128)}, s32[64]{0:T(128)}) custom-call(s32[1536]{0:T(1024)} %owner.1, s32[64]{0:T(128)} %counts.1, s32[1536]{0:T(1024)} %pos.1, f32[4,16,1536]{2,1,0:T(8,128)} %fine_in.1, f32[4,8,1536]{2,1,0:T(8,128)} %coarse_in.1), custom_call_target="tpu_custom_call" | custom-call | tf_op jit(solution)/shard_map/pack/pallas_call | solution.py:392
  3.0 0.0 copy-start
  3.0 0.0 copy-start.1
  3.0 0.0 copy-start.2
  3.0 0.0 copy-start.3
  3.0 10.9 %all-to-all-start = ((f32[64,40,128]{2,1,0:T(8,128)}), f32[64,40,128]{2,1,0:T(8,128)S(1)}, u32[]{:S(2)}, u32[]{:S(2)}) async-start(f32[64,40,128]{2,1,0:T(8,128)} %get-tuple-element.14), calls=%async_computation | async-start | bytes 2621440 | tf_op jit(solution)/shard_map/all_to_all | solution.py:409
  14.0 0.0 copy-done
  14.0 0.0 copy-done.1
  14.0 0.0 copy-done.2
  14.0 0.0 copy-done.3
  14.0 3.7 %plan.1 = s32[512]{0:T(512)S(1)} custom-call(s32[1536]{0:T(1024)S(1)} %copy-done, s32[64]{0:T(128)S(1)} %copy-done.2, s32[1536]{0:T(1024)S(1)} %copy-done.1, s32[64]{0:T(128)S(1)} %copy-done.3), custom_call_target="tpu_custom_call" | custom-call | tf_op jit(solution)/shard_map/plan/pallas_call | solution.py:410
  17.7 29.8 %all-to-all-done.inc = f32[64,40,128]{2,1,0:T(8,128)S(1)} async-done(((f32[64,40,128]{2,1,0:T(8,128)}), f32[64,40,128]{2,1,0:T(8,128)S(1)}, u32[]{:S(2)}, u32[]{:S(2)}) %all-to-all-start) | async-done | bytes 1310752 | tf_op jit(solution)/shard_map/all_to_all | solution.py:409
  47.6 1.1 %edges.1 = (f32[24,4,128]{2,1,0:T(4,128)S(1)}, f32[24,4,128]{2,1,0:T(4,128)S(1)}, f32[4,8,128]{2,1,0:T(8,128)S(1)}) custom-call(s32[512]{0:T(512)S(1)} %plan.1, f32[64,40,128]{2,1,0:T(8,128)S(1)} %all-to-all-done.inc), custom_call_target="tpu_custom_call" | custom-call | tf_op jit(solution)/shard_map/edges/pallas_call | solution.py:418
  48.7 1.9 %collective-permute-start.1 = (f32[24,4,128]{2,1,0:T(4,128)S(1)}, f32[24,4,128]{2,1,0:T(4,128)S(1)}, u32[]{:S(2)}, u32[]{:S(2)}) collective-permute-start(f32[24,4,128]{2,1,0:T(4,128)S(1)} %get-tuple-element.19), channel_id=1, source_target_pairs={{1,2},{3,4},{5,6},{7,8},{9,10},{2,1},{4,3},{6,5},{8,7},{10,9},{13,... | collective-permute-start | bytes 147464 | tf_op jit(solution)/shard_map/ppermute | solution.py:429
  50.6 7.3 %collective-permute-start.2 = (f32[24,4,128]{2,1,0:T(4,128)S(1)}, f32[24,4,128]{2,1,0:T(4,128)S(1)}, u32[]{:S(2)}, u32[]{:S(2)}) collective-permute-start(f32[24,4,128]{2,1,0:T(4,128)S(1)} %get-tuple-element.20), channel_id=1, source_target_pairs={{0,1},{2,3},{4,5},{6,7},{8,9},{10,11},{1,0},{3,2},{5,4},{7,6},{9,8... | collective-permute-start | bytes 147464 | tf_op jit(solution)/shard_map/ppermute | solution.py:430
  57.9 3.8 %collective-permute-start = (f32[4,8,128]{2,1,0:T(8,128)S(1)}, f32[4,8,128]{2,1,0:T(8,128)S(1)}, u32[]{:S(2)}, u32[]{:S(2)}) collective-permute-start(f32[4,8,128]{2,1,0:T(8,128)S(1)} %get-tuple-element.18), channel_id=1, source_target_pairs={{0,12},{12,0},{24,36},{36,24},{48,60},{60,48},{72,84},{84,72},{96,... | collective-permute-start | bytes 49160 | tf_op jit(solution)/shard_map/ppermute | solution.py:431
  61.8 2.1 %middle.1 = (f32[24,4,16,128]{3,2,1,0:T(8,128)S(1)}, f32[24,4,16,128]{3,2,1,0:T(8,128)S(1)}, f32[24,16,128]{2,1,0:T(8,128)S(1)}) custom-call(s32[512]{0:T(512)S(1)} %plan.1, f32[64,40,128]{2,1,0:T(8,128)S(1)} %all-to-all-done.inc), custom_call_target="tpu_custom_call" | custom-call | flops 8000000 | bytes 8000000 | tf_op jit(solution)/shard_map/middle/pallas_call | solution.py:433
  63.9 0.0 collective-permute-done.sibling
  63.9 0.0 collective-permute-done.1.first_rows
  63.9 0.0 collective-permute-done.2.second_rows
  63.9 2.1 %step.1 = f32[4,16,3072]{2,1,0:T(8,128)} custom-call(s32[512]{0:T(512)S(1)} %plan.1, f32[24,4,16,128]{3,2,1,0:T(8,128)S(1)} %get-tuple-element.15.cen, f32[24,4,16,128]{3,2,1,0:T(8,128)S(1)} %get-tuple-element.16.across, f32[24,16,128]{2,1,0:T(8,128)S(1)} %get-tuple-element.17.slope, f32[4,8,128]{2,1,0:T(8,128)S(1)} %collective-permute-done.sibling, ...), custom_call_target="tpu_custom_call" | custom-call | tf_op jit(solution)/shard_map/step/pallas_call | solution.py:446
Async XLA Ops:
  3.0 11.0 %copy-start = (s32[1536]{0:T(1024)S(1)}, s32[1536]{0:T(1024)}, u32[]{:S(2)}) copy-start(s32[1536]{0:T(1024)} %owner.1) | copy-start | bytes 18436
  3.0 11.0 %copy-start.1 = (s32[1536]{0:T(1024)S(1)}, s32[1536]{0:T(1024)}, u32[]{:S(2)}) copy-start(s32[1536]{0:T(1024)} %pos.1) | copy-start | bytes 18436
  3.0 11.0 %copy-start.2 = (s32[64]{0:T(128)S(1)}, s32[64]{0:T(128)}, u32[]{:S(2)}) copy-start(s32[64]{0:T(128)} %counts.1) | copy-start | bytes 772
  3.0 11.0 %copy-start.3 = (s32[64]{0:T(128)S(1)}, s32[64]{0:T(128)}, u32[]{:S(2)}) copy-start(s32[64]{0:T(128)} %get-tuple-element.13.starts) | copy-start | bytes 772
  3.0 44.5 %all-to-all-start = ((f32[64,40,128]{2,1,0:T(8,128)}), f32[64,40,128]{2,1,0:T(8,128)S(1)}, u32[]{:S(2)}, u32[]{:S(2)}) async-start(f32[64,40,128]{2,1,0:T(8,128)} %get-tuple-element.14), calls=%async_computation | async-start | bytes 2621440 | tf_op jit(solution)/shard_map/all_to_all | solution.py:409
  48.7 15.2 %collective-permute-start.1 = (f32[24,4,128]{2,1,0:T(4,128)S(1)}, f32[24,4,128]{2,1,0:T(4,128)S(1)}, u32[]{:S(2)}, u32[]{:S(2)}) collective-permute-start(f32[24,4,128]{2,1,0:T(4,128)S(1)} %get-tuple-element.19), channel_id=1, source_target_pairs={{1,2},{3,4},{5,6},{7,8},{9,10},{2,1},{4,3},{6,5},{8,7},{10,9},{13,... | collective-permute-start | bytes 147464 | tf_op jit(solution)/shard_map/ppermute | solution.py:429
  50.6 13.3 %collective-permute-start.2 = (f32[24,4,128]{2,1,0:T(4,128)S(1)}, f32[24,4,128]{2,1,0:T(4,128)S(1)}, u32[]{:S(2)}, u32[]{:S(2)}) collective-permute-start(f32[24,4,128]{2,1,0:T(4,128)S(1)} %get-tuple-element.20), channel_id=1, source_target_pairs={{0,1},{2,3},{4,5},{6,7},{8,9},{10,11},{1,0},{3,2},{5,4},{7,6},{9,8... | collective-permute-start | bytes 147464 | tf_op jit(solution)/shard_map/ppermute | solution.py:430
  57.9 5.9 %collective-permute-start = (f32[4,8,128]{2,1,0:T(8,128)S(1)}, f32[4,8,128]{2,1,0:T(8,128)S(1)}, u32[]{:S(2)}, u32[]{:S(2)}) collective-permute-start(f32[4,8,128]{2,1,0:T(8,128)S(1)} %get-tuple-element.18), channel_id=1, source_target_pairs={{0,12},{12,0},{24,36},{36,24},{48,60},{60,48},{72,84},{84,72},{96,... | collective-permute-start | bytes 49160 | tf_op jit(solution)/shard_map/ppermute | solution.py:431

commit v5 on v4

--- a/solution.py
+++ b/solution.py
@@ -211,8 +211,8 @@
             bottom = jnp.where(low, inc[a, row : row + 1], pltpu.roll(inc[b, row : row + 1], 64, 1))
             row = f * 8 + 7
             top = jnp.where(low, pltpu.roll(inc[a, row : row + 1], 64, 1), inc[b, row : row + 1])
-            first_rows[t, f : f + 1] = jnp.where(odd, top, bottom)
-            second_rows[t, f : f + 1] = jnp.where(odd, bottom, top)
+            first_rows[t, f : f + 1] = jnp.where(odd, bottom, top)
+            second_rows[t, f : f + 1] = jnp.where(odd, top, bottom)
         return carry
 
     lax.fori_loop(0, TILES, one, 0, unroll=24)
@@ -345,8 +345,8 @@
         for f in range(FIELDS):
             c = cen[t, f]
             one_side, other_side = first_rows[t, f : f + 1], second_rows[t, f : f + 1]
-            below = jnp.where(at_bottom, c[0:1], jnp.where(odd, other_side, one_side))
-            above = jnp.where(at_top, c[15:16], jnp.where(odd, one_side, other_side))
+            below = jnp.where(at_bottom, c[0:1], jnp.where(odd, one_side, other_side))
+            above = jnp.where(at_top, c[15:16], jnp.where(odd, other_side, one_side))
             g = ghosts_of(edges, t, f, where_from)
             g = jnp.where(((lane + 1) & 63) < 2, g, 0.0)
             if f == 0:
@@ -425,7 +425,7 @@
     )(plan, incoming)
     count = lax.axis_size("sub")
     pairs = [(i, i + 1) for i in range(count - 1)]
-    pairs = [pairs[start::2] + [(b, a) for a, b in pairs[start::2]] for start in (1, 0)]
+    pairs = [pairs[start::2] + [(b, a) for a, b in pairs[start::2]] for start in (0, 1)]
     first_rows = lax.ppermute(first_rows, "sub", pairs[0])
     second_rows = lax.ppermute(second_rows, "sub", pairs[1])
     sibling = lax.ppermute(sibling, "slab", [(i, i ^ 1) for i in range(SLABS)])

time: 66.3 us -> 66.3 us (level)
  the two profiles are of different devices: /device:TPU:129 before, /device:TPU:192 now
where the time goes in v5:
time: 66.3 us; the launch traced here: 65.4 us
  waiting for transfers between devices  30.7 us (46%)
  starting transfers between devices  22.4 us (34%)
  Pallas kernels  12 us (18%)
    all_to_all x1, waiting for transfers between devices, body(): incoming = lax.all_to_all(outgoing, 'slab', 0, 0, tiled=True)  30.7 us
    all_to_all x1, starting transfers between devices, body(): incoming = lax.all_to_all(outgoing, 'slab', 0, 0, tiled=True)  10.7 us
    ppermute x1, starting transfers between devices, body(): second_rows = lax.ppermute(second_rows, 'sub', pairs[1])  7.85 us
    pallas_call x1, Pallas kernels, body(): pl.pallas_call(plan_kernel, name='plan', out_shape=i32(8 * 64), in_specs=...  3.72 us
    pallas_call x1, Pallas kernels, body(): pl.pallas_call(pack_kernel, name='pack', out_shape=(f32(SLABS, MSG_ROWS,...  2.97 us
    pallas_call x1, Pallas kernels, body(): pl.pallas_call(step_kernel, name='step', out_shape=f32(FIELDS, ROWS, MOST...  2.13 us
    pallas_call x1, Pallas kernels, body(): pl.pallas_call(middle_kernel, name='middle', out_shape=(f32(*cells), f32(...  2.09 us
    ppermute x1, starting transfers between devices, body(): first_rows = lax.ppermute(first_rows, 'sub', pairs[0])  1.92 us
  transfers between devices with their start and end apart: 4, of which 1 were waited for; matrix products, arithmetic and copies ran while one was open for 0% of the time, Pallas kernels for 9%

profile of v5, /device:TPU:192, one launch (start us, length us, event | category | flops | bytes accessed | tf_op | source)
XLA Modules:
  0.0 65.4 jit_solution(17328072957425572620)
XLA Ops:
  0.0 3.0 %pack.1 = (f32[64,40,128]{2,1,0:T(8,128)}, s32[64]{0:T(128)}) custom-call(s32[1536]{0:T(1024)} %owner.1, s32[64]{0:T(128)} %counts.1, s32[1536]{0:T(1024)} %pos.1, f32[4,16,1536]{2,1,0:T(8,128)} %fine_in.1, f32[4,8,1536]{2,1,0:T(8,128)} %coarse_in.1), custom_call_target="tpu_custom_call" | custom-call | tf_op jit(solution)/shard_map/pack/pallas_call | solution.py:392
  3.0 0.0 copy-start
  3.0 0.0 copy-start.1
  3.0 0.0 copy-start.2
  3.0 0.0 copy-start.3
  3.0 10.7 %all-to-all-start = ((f32[64,40,128]{2,1,0:T(8,128)}), f32[64,40,128]{2,1,0:T(8,128)S(1)}, u32[]{:S(2)}, u32[]{:S(2)}) async-start(f32[64,40,128]{2,1,0:T(8,128)} %get-tuple-element.14), calls=%async_computation | async-start | bytes 2621440 | tf_op jit(solution)/shard_map/all_to_all | solution.py:409
  13.8 0.0 copy-done
  13.8 0.0 copy-done.1
  13.8 0.0 copy-done.2
  13.8 0.0 copy-done.3
  13.8 3.7 %plan.1 = s32[512]{0:T(512)S(1)} custom-call(s32[1536]{0:T(1024)S(1)} %copy-done, s32[64]{0:T(128)S(1)} %copy-done.2, s32[1536]{0:T(1024)S(1)} %copy-done.1, s32[64]{0:T(128)S(1)} %copy-done.3), custom_call_target="tpu_custom_call" | custom-call | tf_op jit(solution)/shard_map/plan/pallas_call | solution.py:410
  17.5 30.7 %all-to-all-done.inc = f32[64,40,128]{2,1,0:T(8,128)S(1)} async-done(((f32[64,40,128]{2,1,0:T(8,128)}), f32[64,40,128]{2,1,0:T(8,128)S(1)}, u32[]{:S(2)}, u32[]{:S(2)}) %all-to-all-start) | async-done | bytes 1310752 | tf_op jit(solution)/shard_map/all_to_all | solution.py:409
  48.3 1.1 %edges.1 = (f32[24,4,128]{2,1,0:T(4,128)S(1)}, f32[24,4,128]{2,1,0:T(4,128)S(1)}, f32[4,8,128]{2,1,0:T(8,128)S(1)}) custom-call(s32[512]{0:T(512)S(1)} %plan.1, f32[64,40,128]{2,1,0:T(8,128)S(1)} %all-to-all-done.inc), custom_call_target="tpu_custom_call" | custom-call | tf_op jit(solution)/shard_map/edges/pallas_call | solution.py:418
  49.4 1.9 %collective-permute-start.1 = (f32[24,4,128]{2,1,0:T(4,128)S(1)}, f32[24,4,128]{2,1,0:T(4,128)S(1)}, u32[]{:S(2)}, u32[]{:S(2)}) collective-permute-start(f32[24,4,128]{2,1,0:T(4,128)S(1)} %get-tuple-element.19), channel_id=1, source_target_pairs={{0,1},{2,3},{4,5},{6,7},{8,9},{10,11},{1,0},{3,2},{5,4},{7,6},{9,8... | collective-permute-start | bytes 147464 | tf_op jit(solution)/shard_map/ppermute | solution.py:429
  51.3 7.9 %collective-permute-start.2 = (f32[24,4,128]{2,1,0:T(4,128)S(1)}, f32[24,4,128]{2,1,0:T(4,128)S(1)}, u32[]{:S(2)}, u32[]{:S(2)}) collective-permute-start(f32[24,4,128]{2,1,0:T(4,128)S(1)} %get-tuple-element.20), channel_id=1, source_target_pairs={{1,2},{3,4},{5,6},{7,8},{9,10},{2,1},{4,3},{6,5},{8,7},{10,9},{13,... | collective-permute-start | bytes 147464 | tf_op jit(solution)/shard_map/ppermute | solution.py:430
  59.2 1.9 %collective-permute-start = (f32[4,8,128]{2,1,0:T(8,128)S(1)}, f32[4,8,128]{2,1,0:T(8,128)S(1)}, u32[]{:S(2)}, u32[]{:S(2)}) collective-permute-start(f32[4,8,128]{2,1,0:T(8,128)S(1)} %get-tuple-element.18), channel_id=1, source_target_pairs={{0,12},{12,0},{24,36},{36,24},{48,60},{60,48},{72,84},{84,72},{96,... | collective-permute-start | bytes 49160 | tf_op jit(solution)/shard_map/ppermute | solution.py:431
  61.1 2.1 %middle.1 = (f32[24,4,16,128]{3,2,1,0:T(8,128)S(1)}, f32[24,4,16,128]{3,2,1,0:T(8,128)S(1)}, f32[24,16,128]{2,1,0:T(8,128)S(1)}) custom-call(s32[512]{0:T(512)S(1)} %plan.1, f32[64,40,128]{2,1,0:T(8,128)S(1)} %all-to-all-done.inc), custom_call_target="tpu_custom_call" | custom-call | flops 8000000 | bytes 8000000 | tf_op jit(solution)/shard_map/middle/pallas_call | solution.py:433
  63.2 0.0 collective-permute-done.sibling
  63.2 0.0 collective-permute-done.1.first_rows
  63.2 0.0 collective-permute-done.2.second_rows
  63.2 2.1 %step.1 = f32[4,16,3072]{2,1,0:T(8,128)} custom-call(s32[512]{0:T(512)S(1)} %plan.1, f32[24,4,16,128]{3,2,1,0:T(8,128)S(1)} %get-tuple-element.15.cen, f32[24,4,16,128]{3,2,1,0:T(8,128)S(1)} %get-tuple-element.16.across, f32[24,16,128]{2,1,0:T(8,128)S(1)} %get-tuple-element.17.slope, f32[4,8,128]{2,1,0:T(8,128)S(1)} %collective-permute-done.sibling, ...), custom_call_target="tpu_custom_call" | custom-call | tf_op jit(solution)/shard_map/step/pallas_call | solution.py:446
Async XLA Ops:
  3.0 10.8 %copy-start = (s32[1536]{0:T(1024)S(1)}, s32[1536]{0:T(1024)}, u32[]{:S(2)}) copy-start(s32[1536]{0:T(1024)} %owner.1) | copy-start | bytes 18436
  3.0 10.8 %copy-start.1 = (s32[1536]{0:T(1024)S(1)}, s32[1536]{0:T(1024)}, u32[]{:S(2)}) copy-start(s32[1536]{0:T(1024)} %pos.1) | copy-start | bytes 18436
  3.0 10.8 %copy-start.2 = (s32[64]{0:T(128)S(1)}, s32[64]{0:T(128)}, u32[]{:S(2)}) copy-start(s32[64]{0:T(128)} %counts.1) | copy-start | bytes 772
  3.0 10.8 %copy-start.3 = (s32[64]{0:T(128)S(1)}, s32[64]{0:T(128)}, u32[]{:S(2)}) copy-start(s32[64]{0:T(128)} %get-tuple-element.13.starts) | copy-start | bytes 772
  3.0 45.2 %all-to-all-start = ((f32[64,40,128]{2,1,0:T(8,128)}), f32[64,40,128]{2,1,0:T(8,128)S(1)}, u32[]{:S(2)}, u32[]{:S(2)}) async-start(f32[64,40,128]{2,1,0:T(8,128)} %get-tuple-element.14), calls=%async_computation | async-start | bytes 2621440 | tf_op jit(solution)/shard_map/all_to_all | solution.py:409
  49.4 13.8 %collective-permute-start.1 = (f32[24,4,128]{2,1,0:T(4,128)S(1)}, f32[24,4,128]{2,1,0:T(4,128)S(1)}, u32[]{:S(2)}, u32[]{:S(2)}) collective-permute-start(f32[24,4,128]{2,1,0:T(4,128)S(1)} %get-tuple-element.19), channel_id=1, source_target_pairs={{0,1},{2,3},{4,5},{6,7},{8,9},{10,11},{1,0},{3,2},{5,4},{7,6},{9,8... | collective-permute-start | bytes 147464 | tf_op jit(solution)/shard_map/ppermute | solution.py:429
  51.3 11.9 %collective-permute-start.2 = (f32[24,4,128]{2,1,0:T(4,128)S(1)}, f32[24,4,128]{2,1,0:T(4,128)S(1)}, u32[]{:S(2)}, u32[]{:S(2)}) collective-permute-start(f32[24,4,128]{2,1,0:T(4,128)S(1)} %get-tuple-element.20), channel_id=1, source_target_pairs={{1,2},{3,4},{5,6},{7,8},{9,10},{2,1},{4,3},{6,5},{8,7},{10,9},{13,... | collective-permute-start | bytes 147464 | tf_op jit(solution)/shard_map/ppermute | solution.py:430
  59.2 4.0 %collective-permute-start = (f32[4,8,128]{2,1,0:T(8,128)S(1)}, f32[4,8,128]{2,1,0:T(8,128)S(1)}, u32[]{:S(2)}, u32[]{:S(2)}) collective-permute-start(f32[4,8,128]{2,1,0:T(8,128)S(1)} %get-tuple-element.18), channel_id=1, source_target_pairs={{0,12},{12,0},{24,36},{36,24},{48,60},{60,48},{72,84},{84,72},{96,... | collective-permute-start | bytes 49160 | tf_op jit(solution)/shard_map/ppermute | solution.py:431

commit v6 on v3

--- a/solution.py
+++ b/solution.py
@@ -134,7 +134,7 @@
         out[b, 0:BOX_ROWS] = packed[slot]
         return start + counts[b]
 
-    lax.fori_loop(0, SLABS, fill, jnp.int32(0), unroll=64)
+    lax.fori_loop(0, SLABS, fill, jnp.int32(0), unroll=32)
 
 
 def plan_kernel(owner, counts, pos, starts, plan):
@@ -200,20 +200,15 @@
 
 
 def edge_kernel(plan, inc, low_rows, high_rows, sibling):
-    low = lanes((1, 128)) < 64
+    low = lanes((FIELDS, 128)) < 64
 
     def one(t, carry):
         a = plan[SRC * 64 + 2 + 2 * t]
         b = plan[SRC * 64 + 3 + 2 * t]
-        for f in range(FIELDS):
-            row = f * 8
-            low_rows[t, f : f + 1] = jnp.where(
-                low, inc[a, row : row + 1], pltpu.roll(inc[b, row : row + 1], 64, 1)
-            )
-            row = f * 8 + 7
-            high_rows[t, f : f + 1] = jnp.where(
-                low, pltpu.roll(inc[a, row : row + 1], 64, 1), inc[b, row : row + 1]
-            )
+        bottoms = [inc[s, pl.ds(0, FIELDS, stride=8)] for s in (a, b)]
+        tops = [inc[s, pl.ds(7, FIELDS, stride=8)] for s in (a, b)]
+        low_rows[t] = jnp.where(low, bottoms[0], pltpu.roll(bottoms[1], 64, 1))
+        high_rows[t] = jnp.where(low, pltpu.roll(tops[0], 64, 1), tops[1])
         return carry
 
     lax.fori_loop(0, TILES, one, 0, unroll=24)
@@ -425,8 +420,8 @@
     count = lax.axis_size("sub")
     up = [(i, i + 1) for i in range(count - 1)]
     sibling = lax.ppermute(sibling, "slab", [(i, i ^ 1) for i in range(SLABS)])
+    from_above = lax.ppermute(low_rows, "sub", [(b, a) for a, b in up])
     from_below = lax.ppermute(high_rows, "sub", up)
-    from_above = lax.ppermute(low_rows, "sub", [(b, a) for a, b in up])
     cells = (TILES, FIELDS, ROWS, 128)
     cen, across, slope = pl.pallas_call(
         middle_kernel,

time: 64.5 us -> 64.4 us (level)
  no operation moved by 1% of the time
where the time goes in v6:
time: 64.4 us; the launch traced here: 64.1 us
  waiting for transfers between devices  32 us (50%)
  starting transfers between devices  20 us (31%)
  Pallas kernels  11.9 us (18%)
    all_to_all x1, waiting for transfers between devices, body(): incoming = lax.all_to_all(outgoing, 'slab', 0, 0, tiled=True)  30.7 us
    all_to_all x1, starting transfers between devices, body(): incoming = lax.all_to_all(outgoing, 'slab', 0, 0, tiled=True)  10.7 us
    ppermute x1, starting transfers between devices, body(): from_below = lax.ppermute(high_rows, 'sub', up)  5.49 us
    pallas_call x1, Pallas kernels, body(): pl.pallas_call(plan_kernel, name='plan', out_shape=i32(8 * 64), in_specs=...  3.72 us
    pallas_call x1, Pallas kernels, body(): pl.pallas_call(pack_kernel, name='pack', out_shape=(f32(SLABS, MSG_ROWS,...  3.01 us
    pallas_call x1, Pallas kernels, body(): pl.pallas_call(middle_kernel, name='middle', out_shape=(f32(*cells), f32(...  2.09 us
    pallas_call x1, Pallas kernels, body(): pl.pallas_call(step_kernel, name='step', out_shape=f32(FIELDS, ROWS, MOST...  2.09 us
    ppermute x1, starting transfers between devices, body(): from_above = lax.ppermute(low_rows, 'sub', [(b, a) for a, b in up])  1.92 us
  transfers between devices with their start and end apart: 4, of which 2 were waited for; matrix products, arithmetic and copies ran while one was open for 0% of the time, Pallas kernels for 9%

profile of v6, /device:TPU:192, one launch (start us, length us, event | category | flops | bytes accessed | tf_op | source)
XLA Modules:
  0.0 64.1 jit_solution(3826225791305295438)
XLA Ops:
  0.0 3.0 %pack.1 = (f32[64,40,128]{2,1,0:T(8,128)}, s32[64]{0:T(128)}) custom-call(s32[1536]{0:T(1024)} %owner.1, s32[64]{0:T(128)} %counts.1, s32[1536]{0:T(1024)} %pos.1, f32[4,16,1536]{2,1,0:T(8,128)} %fine_in.1, f32[4,8,1536]{2,1,0:T(8,128)} %coarse_in.1), custom_call_target="tpu_custom_call" | custom-call | tf_op jit(solution)/shard_map/pack/pallas_call | solution.py:386
  3.0 0.0 copy-start
  3.0 0.0 copy-start.1
  3.0 0.0 copy-start.2
  3.1 0.0 copy-start.3
  3.1 10.7 %all-to-all-start = ((f32[64,40,128]{2,1,0:T(8,128)}), f32[64,40,128]{2,1,0:T(8,128)S(1)}, u32[]{:S(2)}, u32[]{:S(2)}) async-start(f32[64,40,128]{2,1,0:T(8,128)} %get-tuple-element.14), calls=%async_computation | async-start | bytes 2621440 | tf_op jit(solution)/shard_map/all_to_all | solution.py:403
  13.8 0.0 copy-done
  13.8 0.0 copy-done.1
  13.8 0.0 copy-done.2
  13.8 0.0 copy-done.3
  13.8 3.7 %plan.1 = s32[512]{0:T(512)S(1)} custom-call(s32[1536]{0:T(1024)S(1)} %copy-done, s32[64]{0:T(128)S(1)} %copy-done.2, s32[1536]{0:T(1024)S(1)} %copy-done.1, s32[64]{0:T(128)S(1)} %copy-done.3), custom_call_target="tpu_custom_call" | custom-call | tf_op jit(solution)/shard_map/plan/pallas_call | solution.py:404
  17.6 30.7 %all-to-all-done.inc = f32[64,40,128]{2,1,0:T(8,128)S(1)} async-done(((f32[64,40,128]{2,1,0:T(8,128)}), f32[64,40,128]{2,1,0:T(8,128)S(1)}, u32[]{:S(2)}, u32[]{:S(2)}) %all-to-all-start) | async-done | bytes 1310752 | tf_op jit(solution)/shard_map/all_to_all | solution.py:403
  48.3 1.0 %edges.1 = (f32[24,4,128]{2,1,0:T(4,128)S(1)}, f32[24,4,128]{2,1,0:T(4,128)S(1)}, f32[4,8,128]{2,1,0:T(8,128)S(1)}) custom-call(s32[512]{0:T(512)S(1)} %plan.1, f32[64,40,128]{2,1,0:T(8,128)S(1)} %all-to-all-done.inc), custom_call_target="tpu_custom_call" | custom-call | tf_op jit(solution)/shard_map/edges/pallas_call | solution.py:412
  49.3 5.5 %collective-permute-start.1 = (f32[24,4,128]{2,1,0:T(4,128)S(1)}, f32[24,4,128]{2,1,0:T(4,128)S(1)}, u32[]{:S(2)}, u32[]{:S(2)}) collective-permute-start(f32[24,4,128]{2,1,0:T(4,128)S(1)} %get-tuple-element.19), channel_id=1, source_target_pairs={{0,1},{1,2},{2,3},{3,4},{4,5},{5,6},{6,7},{7,8},{8,9},{9,10},{10,1... | collective-permute-start | bytes 147464 | tf_op jit(solution)/shard_map/ppermute | solution.py:424
  54.8 1.9 %collective-permute-start.2 = (f32[24,4,128]{2,1,0:T(4,128)S(1)}, f32[24,4,128]{2,1,0:T(4,128)S(1)}, u32[]{:S(2)}, u32[]{:S(2)}) collective-permute-start(f32[24,4,128]{2,1,0:T(4,128)S(1)} %get-tuple-element.20), channel_id=1, source_target_pairs={{1,0},{2,1},{3,2},{4,3},{5,4},{6,5},{7,6},{8,7},{9,8},{10,9},{11,1... | collective-permute-start | bytes 147464 | tf_op jit(solution)/shard_map/ppermute | solution.py:423
  56.8 1.9 %collective-permute-start = (f32[4,8,128]{2,1,0:T(8,128)S(1)}, f32[4,8,128]{2,1,0:T(8,128)S(1)}, u32[]{:S(2)}, u32[]{:S(2)}) collective-permute-start(f32[4,8,128]{2,1,0:T(8,128)S(1)} %get-tuple-element.18), channel_id=1, source_target_pairs={{0,12},{12,0},{24,36},{36,24},{48,60},{60,48},{72,84},{84,72},{96,... | collective-permute-start | bytes 49160 | tf_op jit(solution)/shard_map/ppermute | solution.py:422
  58.7 2.1 %middle.1 = (f32[24,4,16,128]{3,2,1,0:T(8,128)S(1)}, f32[24,4,16,128]{3,2,1,0:T(8,128)S(1)}, f32[24,16,128]{2,1,0:T(8,128)S(1)}) custom-call(s32[512]{0:T(512)S(1)} %plan.1, f32[64,40,128]{2,1,0:T(8,128)S(1)} %all-to-all-done.inc), custom_call_target="tpu_custom_call" | custom-call | flops 8000000 | bytes 8000000 | tf_op jit(solution)/shard_map/middle/pallas_call | solution.py:426
  60.8 0.0 collective-permute-done.sibling
  60.8 0.0 collective-permute-done.1.from_below
  60.8 1.2 %collective-permute-done.2.from_above = f32[24,4,128]{2,1,0:T(4,128)S(1)} collective-permute-done((f32[24,4,128]{2,1,0:T(4,128)S(1)}, f32[24,4,128]{2,1,0:T(4,128)S(1)}, u32[]{:S(2)}, u32[]{:S(2)}) %collective-permute-start.2) | collective-permute-done | bytes 49184 | tf_op jit(solution)/shard_map/ppermute | solution.py:423
  62.0 2.1 %step.1 = f32[4,16,3072]{2,1,0:T(8,128)} custom-call(s32[512]{0:T(512)S(1)} %plan.1, f32[24,4,16,128]{3,2,1,0:T(8,128)S(1)} %get-tuple-element.15.cen, f32[24,4,16,128]{3,2,1,0:T(8,128)S(1)} %get-tuple-element.16.across, f32[24,16,128]{2,1,0:T(8,128)S(1)} %get-tuple-element.17.slope, f32[4,8,128]{2,1,0:T(8,128)S(1)} %collective-permute-done.sibling, ...), custom_call_target="tpu_custom_call" | custom-call | tf_op jit(solution)/shard_map/step/pallas_call | solution.py:439
Async XLA Ops:
  3.0 10.8 %copy-start = (s32[1536]{0:T(1024)S(1)}, s32[1536]{0:T(1024)}, u32[]{:S(2)}) copy-start(s32[1536]{0:T(1024)} %owner.1) | copy-start | bytes 18436
  3.0 10.8 %copy-start.1 = (s32[1536]{0:T(1024)S(1)}, s32[1536]{0:T(1024)}, u32[]{:S(2)}) copy-start(s32[1536]{0:T(1024)} %pos.1) | copy-start | bytes 18436
  3.0 10.8 %copy-start.2 = (s32[64]{0:T(128)S(1)}, s32[64]{0:T(128)}, u32[]{:S(2)}) copy-start(s32[64]{0:T(128)} %counts.1) | copy-start | bytes 772
  3.1 10.8 %copy-start.3 = (s32[64]{0:T(128)S(1)}, s32[64]{0:T(128)}, u32[]{:S(2)}) copy-start(s32[64]{0:T(128)} %get-tuple-element.13.starts) | copy-start | bytes 772
  3.1 45.2 %all-to-all-start = ((f32[64,40,128]{2,1,0:T(8,128)}), f32[64,40,128]{2,1,0:T(8,128)S(1)}, u32[]{:S(2)}, u32[]{:S(2)}) async-start(f32[64,40,128]{2,1,0:T(8,128)} %get-tuple-element.14), calls=%async_computation | async-start | bytes 2621440 | tf_op jit(solution)/shard_map/all_to_all | solution.py:403
  49.3 11.5 %collective-permute-start.1 = (f32[24,4,128]{2,1,0:T(4,128)S(1)}, f32[24,4,128]{2,1,0:T(4,128)S(1)}, u32[]{:S(2)}, u32[]{:S(2)}) collective-permute-start(f32[24,4,128]{2,1,0:T(4,128)S(1)} %get-tuple-element.19), channel_id=1, source_target_pairs={{0,1},{1,2},{2,3},{3,4},{4,5},{5,6},{6,7},{7,8},{8,9},{9,10},{10,1... | collective-permute-start | bytes 147464 | tf_op jit(solution)/shard_map/ppermute | solution.py:424
  54.8 7.2 %collective-permute-start.2 = (f32[24,4,128]{2,1,0:T(4,128)S(1)}, f32[24,4,128]{2,1,0:T(4,128)S(1)}, u32[]{:S(2)}, u32[]{:S(2)}) collective-permute-start(f32[24,4,128]{2,1,0:T(4,128)S(1)} %get-tuple-element.20), channel_id=1, source_target_pairs={{1,0},{2,1},{3,2},{4,3},{5,4},{6,5},{7,6},{8,7},{9,8},{10,9},{11,1... | collective-permute-start | bytes 147464 | tf_op jit(solution)/shard_map/ppermute | solution.py:423
  56.8 4.0 %collective-permute-start = (f32[4,8,128]{2,1,0:T(8,128)S(1)}, f32[4,8,128]{2,1,0:T(8,128)S(1)}, u32[]{:S(2)}, u32[]{:S(2)}) collective-permute-start(f32[4,8,128]{2,1,0:T(8,128)S(1)} %get-tuple-element.18), channel_id=1, source_target_pairs={{0,12},{12,0},{24,36},{36,24},{48,60},{60,48},{72,84},{84,72},{96,... | collective-permute-start | bytes 49160 | tf_op jit(solution)/shard_map/ppermute | solution.py:422

commit v7 on v6

--- a/solution.py
+++ b/solution.py
@@ -323,7 +323,7 @@
     one(TILES - 1, cen.at[TILES - 2], outside.at[1])
 
 
-def step_kernel(plan, cen, across, slope, sibling, from_below, from_above, out, held, edges, sems):
+def step_kernel(plan, cen, across, slope, sibling, from_above, from_below, out, held, edges, sems):
     sub = lax.axis_index("sub")
     count = plan[MISC * 64 + 1]
     lane = lanes((ROWS, 128))
@@ -448,7 +448,7 @@
             pltpu.SemaphoreType.DMA((PARTS,)),
         ],
         compiler_params=PARAMS,
-    )(plan, cen, across, slope, sibling, from_below, from_above)
+    )(plan, cen, across, slope, sibling, from_above, from_below)
 
 
 def solution(mesh):

time: 64.4 us -> 66.2 us (1.028)
  the two profiles are of different devices: /device:TPU:192 before, /device:TPU:1 now
where the time goes in v7:
time: 66.2 us; the launch traced here: 65.9 us
  waiting for transfers between devices  30 us (45%)
  starting transfers between devices  23.8 us (36%)
  Pallas kernels  11.9 us (18%)
    all_to_all x1, waiting for transfers between devices, body(): incoming = lax.all_to_all(outgoing, 'slab', 0, 0, tiled=True)  30 us
    all_to_all x1, starting transfers between devices, body(): incoming = lax.all_to_all(outgoing, 'slab', 0, 0, tiled=True)  14.8 us
    ppermute x1, starting transfers between devices, body(): from_below = lax.ppermute(high_rows, 'sub', up)  3.99 us
    ppermute x1, starting transfers between devices, body(): sibling = lax.ppermute(sibling, 'slab', [(i, i ^ 1) for i in range(SLABS)])  3.78 us
    pallas_call x1, Pallas kernels, body(): pl.pallas_call(plan_kernel, name='plan', out_shape=i32(8 * 64), in_specs=...  3.72 us
    pallas_call x1, Pallas kernels, body(): pl.pallas_call(pack_kernel, name='pack', out_shape=(f32(SLABS, MSG_ROWS,...  3.01 us
    pallas_call x1, Pallas kernels, body(): pl.pallas_call(middle_kernel, name='middle', out_shape=(f32(*cells), f32(...  2.1 us
    pallas_call x1, Pallas kernels, body(): pl.pallas_call(step_kernel, name='step', out_shape=f32(FIELDS, ROWS, MOST...  2.09 us
  transfers between devices with their start and end apart: 4, of which 1 were waited for; matrix products, arithmetic and copies ran while one was open for 0% of the time, Pallas kernels for 9%

profile of v7, /device:TPU:1, one launch (start us, length us, event | category | flops | bytes accessed | tf_op | source)
XLA Modules:
  0.0 65.9 jit_solution(1563501589495498246)
XLA Ops:
  0.0 3.0 %pack.1 = (f32[64,40,128]{2,1,0:T(8,128)}, s32[64]{0:T(128)}) custom-call(s32[1536]{0:T(1024)} %owner.1, s32[64]{0:T(128)} %counts.1, s32[1536]{0:T(1024)} %pos.1, f32[4,16,1536]{2,1,0:T(8,128)} %fine_in.1, f32[4,8,1536]{2,1,0:T(8,128)} %coarse_in.1), custom_call_target="tpu_custom_call" | custom-call | tf_op jit(solution)/shard_map/pack/pallas_call | solution.py:386
  3.0 0.0 copy-start
  3.0 0.0 copy-start.1
  3.0 0.0 copy-start.2
  3.1 0.0 copy-start.3
  3.1 14.8 %all-to-all-start = ((f32[64,40,128]{2,1,0:T(8,128)}), f32[64,40,128]{2,1,0:T(8,128)S(1)}, u32[]{:S(2)}, u32[]{:S(2)}) async-start(f32[64,40,128]{2,1,0:T(8,128)} %get-tuple-element.14), calls=%async_computation | async-start | bytes 2621440 | tf_op jit(solution)/shard_map/all_to_all | solution.py:403
  17.8 0.0 copy-done
  17.8 0.0 copy-done.1
  17.9 0.0 copy-done.2
  17.9 0.0 copy-done.3
  17.9 3.7 %plan.1 = s32[512]{0:T(512)S(1)} custom-call(s32[1536]{0:T(1024)S(1)} %copy-done, s32[64]{0:T(128)S(1)} %copy-done.2, s32[1536]{0:T(1024)S(1)} %copy-done.1, s32[64]{0:T(128)S(1)} %copy-done.3), custom_call_target="tpu_custom_call" | custom-call | tf_op jit(solution)/shard_map/plan/pallas_call | solution.py:404
  21.6 30.0 %all-to-all-done.inc = f32[64,40,128]{2,1,0:T(8,128)S(1)} async-done(((f32[64,40,128]{2,1,0:T(8,128)}), f32[64,40,128]{2,1,0:T(8,128)S(1)}, u32[]{:S(2)}, u32[]{:S(2)}) %all-to-all-start) | async-done | bytes 1310752 | tf_op jit(solution)/shard_map/all_to_all | solution.py:403
  51.6 1.0 %edges.1 = (f32[24,4,128]{2,1,0:T(4,128)S(1)}, f32[24,4,128]{2,1,0:T(4,128)S(1)}, f32[4,8,128]{2,1,0:T(8,128)S(1)}) custom-call(s32[512]{0:T(512)S(1)} %plan.1, f32[64,40,128]{2,1,0:T(8,128)S(1)} %all-to-all-done.inc), custom_call_target="tpu_custom_call" | custom-call | tf_op jit(solution)/shard_map/edges/pallas_call | solution.py:412
  52.6 1.3 %collective-permute-start.1 = (f32[24,4,128]{2,1,0:T(4,128)S(1)}, f32[24,4,128]{2,1,0:T(4,128)S(1)}, u32[]{:S(2)}, u32[]{:S(2)}) collective-permute-start(f32[24,4,128]{2,1,0:T(4,128)S(1)} %get-tuple-element.19), channel_id=1, source_target_pairs={{1,0},{2,1},{3,2},{4,3},{5,4},{6,5},{7,6},{8,7},{9,8},{10,9},{11,1... | collective-permute-start | bytes 147464 | tf_op jit(solution)/shard_map/ppermute | solution.py:423
  53.9 4.0 %collective-permute-start.2 = (f32[24,4,128]{2,1,0:T(4,128)S(1)}, f32[24,4,128]{2,1,0:T(4,128)S(1)}, u32[]{:S(2)}, u32[]{:S(2)}) collective-permute-start(f32[24,4,128]{2,1,0:T(4,128)S(1)} %get-tuple-element.20), channel_id=1, source_target_pairs={{0,1},{1,2},{2,3},{3,4},{4,5},{5,6},{6,7},{7,8},{8,9},{9,10},{10,1... | collective-permute-start | bytes 147464 | tf_op jit(solution)/shard_map/ppermute | solution.py:424
  57.9 3.8 %collective-permute-start = (f32[4,8,128]{2,1,0:T(8,128)S(1)}, f32[4,8,128]{2,1,0:T(8,128)S(1)}, u32[]{:S(2)}, u32[]{:S(2)}) collective-permute-start(f32[4,8,128]{2,1,0:T(8,128)S(1)} %get-tuple-element.18), channel_id=1, source_target_pairs={{0,12},{12,0},{24,36},{36,24},{48,60},{60,48},{72,84},{84,72},{96,... | collective-permute-start | bytes 49160 | tf_op jit(solution)/shard_map/ppermute | solution.py:422
  61.7 2.1 %middle.1 = (f32[24,4,16,128]{3,2,1,0:T(8,128)S(1)}, f32[24,4,16,128]{3,2,1,0:T(8,128)S(1)}, f32[24,16,128]{2,1,0:T(8,128)S(1)}) custom-call(s32[512]{0:T(512)S(1)} %plan.1, f32[64,40,128]{2,1,0:T(8,128)S(1)} %all-to-all-done.inc), custom_call_target="tpu_custom_call" | custom-call | flops 8000000 | bytes 8000000 | tf_op jit(solution)/shard_map/middle/pallas_call | solution.py:426
  63.8 0.0 collective-permute-done.sibling
  63.8 0.0 collective-permute-done.1.from_above
  63.8 0.0 collective-permute-done.2.from_below
  63.8 2.1 %step.1 = f32[4,16,3072]{2,1,0:T(8,128)} custom-call(s32[512]{0:T(512)S(1)} %plan.1, f32[24,4,16,128]{3,2,1,0:T(8,128)S(1)} %get-tuple-element.15.cen, f32[24,4,16,128]{3,2,1,0:T(8,128)S(1)} %get-tuple-element.16.across, f32[24,16,128]{2,1,0:T(8,128)S(1)} %get-tuple-element.17.slope, f32[4,8,128]{2,1,0:T(8,128)S(1)} %collective-permute-done.sibling, ...), custom_call_target="tpu_custom_call" | custom-call | tf_op jit(solution)/shard_map/step/pallas_call | solution.py:439
Async XLA Ops:
  3.0 14.8 %copy-start = (s32[1536]{0:T(1024)S(1)}, s32[1536]{0:T(1024)}, u32[]{:S(2)}) copy-start(s32[1536]{0:T(1024)} %owner.1) | copy-start | bytes 18436
  3.0 14.8 %copy-start.1 = (s32[1536]{0:T(1024)S(1)}, s32[1536]{0:T(1024)}, u32[]{:S(2)}) copy-start(s32[1536]{0:T(1024)} %pos.1) | copy-start | bytes 18436
  3.0 14.8 %copy-start.2 = (s32[64]{0:T(128)S(1)}, s32[64]{0:T(128)}, u32[]{:S(2)}) copy-start(s32[64]{0:T(128)} %counts.1) | copy-start | bytes 772
  3.1 14.8 %copy-start.3 = (s32[64]{0:T(128)S(1)}, s32[64]{0:T(128)}, u32[]{:S(2)}) copy-start(s32[64]{0:T(128)} %get-tuple-element.13.starts) | copy-start | bytes 772
  3.1 48.5 %all-to-all-start = ((f32[64,40,128]{2,1,0:T(8,128)}), f32[64,40,128]{2,1,0:T(8,128)S(1)}, u32[]{:S(2)}, u32[]{:S(2)}) async-start(f32[64,40,128]{2,1,0:T(8,128)} %get-tuple-element.14), calls=%async_computation | async-start | bytes 2621440 | tf_op jit(solution)/shard_map/all_to_all | solution.py:403
  52.6 11.2 %collective-permute-start.1 = (f32[24,4,128]{2,1,0:T(4,128)S(1)}, f32[24,4,128]{2,1,0:T(4,128)S(1)}, u32[]{:S(2)}, u32[]{:S(2)}) collective-permute-start(f32[24,4,128]{2,1,0:T(4,128)S(1)} %get-tuple-element.19), channel_id=1, source_target_pairs={{1,0},{2,1},{3,2},{4,3},{5,4},{6,5},{7,6},{8,7},{9,8},{10,9},{11,1... | collective-permute-start | bytes 147464 | tf_op jit(solution)/shard_map/ppermute | solution.py:423
  53.9 9.9 %collective-permute-start.2 = (f32[24,4,128]{2,1,0:T(4,128)S(1)}, f32[24,4,128]{2,1,0:T(4,128)S(1)}, u32[]{:S(2)}, u32[]{:S(2)}) collective-permute-start(f32[24,4,128]{2,1,0:T(4,128)S(1)} %get-tuple-element.20), channel_id=1, source_target_pairs={{0,1},{1,2},{2,3},{3,4},{4,5},{5,6},{6,7},{7,8},{8,9},{9,10},{10,1... | collective-permute-start | bytes 147464 | tf_op jit(solution)/shard_map/ppermute | solution.py:424
  57.9 5.9 %collective-permute-start = (f32[4,8,128]{2,1,0:T(8,128)S(1)}, f32[4,8,128]{2,1,0:T(8,128)S(1)}, u32[]{:S(2)}, u32[]{:S(2)}) collective-permute-start(f32[4,8,128]{2,1,0:T(8,128)S(1)} %get-tuple-element.18), channel_id=1, source_target_pairs={{0,12},{12,0},{24,36},{36,24},{48,60},{60,48},{72,84},{84,72},{96,... | collective-permute-start | bytes 49160 | tf_op jit(solution)/shard_map/ppermute | solution.py:422

commit v8 on v7

--- a/solution.py
+++ b/solution.py
@@ -259,7 +259,7 @@
     return jnp.concatenate([jnp.take_along_axis(edges[q, h : h + 8], at, axis=1) for h in (0, 8)], axis=0)
 
 
-def middle_kernel(plan, inc, cen, across, slope, edges, outside):
+def middle_kernel(plan, inc, cen, across, slope, alive, edges, outside):
     lane = lanes()
     low = lane < 64
     start = plan[MISC * 64]
@@ -289,6 +289,9 @@
     whole_rows(gather_edges(plan, inc, OWN_L, OWN_R), edges)
     lane = lanes((ROWS, 128))
     where_from = ghost_source()
+    count = plan[MISC * 64 + 1]
+    slot = lax.broadcasted_iota(jnp.int32, (TILES, 128), 0) * 2 + (lanes((TILES, 128)) >> 6)
+    alive[...] = jnp.where(slot < count, 1.0, 0.0)
 
     def one(t, before, after):
         s = 2 * t
@@ -323,9 +326,8 @@
     one(TILES - 1, cen.at[TILES - 2], outside.at[1])
 
 
-def step_kernel(plan, cen, across, slope, sibling, from_above, from_below, out, held, edges, sems):
+def step_kernel(cen, across, slope, alive, sibling, from_below, from_above, out, held, edges, sems):
     sub = lax.axis_index("sub")
-    count = plan[MISC * 64 + 1]
     lane = lanes((ROWS, 128))
     row = lax.broadcasted_iota(jnp.int32, (ROWS, 128), 0)
     at_bottom = sub == 0
@@ -335,7 +337,7 @@
     whole_rows([sibling[n] for n in range(4)], edges)
 
     def one(t, carry):
-        live = jnp.where(lane < 64, 2 * t, 2 * t + 1) < count
+        live = jnp.broadcast_to(alive[pl.ds(t, 1)], (ROWS, 128)) == 1.0
         center, sides, south, north = [], [], [], []
         for f in range(FIELDS):
             c = cen[t, f]
@@ -423,12 +425,12 @@
     from_above = lax.ppermute(low_rows, "sub", [(b, a) for a, b in up])
     from_below = lax.ppermute(high_rows, "sub", up)
     cells = (TILES, FIELDS, ROWS, 128)
-    cen, across, slope = pl.pallas_call(
+    cen, across, slope, alive = pl.pallas_call(
         middle_kernel,
         name="middle",
-        out_shape=(f32(*cells), f32(*cells), f32(TILES, ROWS, 128)),
+        out_shape=(f32(*cells), f32(*cells), f32(TILES, ROWS, 128), f32(TILES, 128)),
         in_specs=[SMEM, VMEM],
-        out_specs=(VMEM, VMEM, VMEM),
+        out_specs=(VMEM, VMEM, VMEM, VMEM),
         scratch_shapes=[
             pltpu.VMEM((4, ROWS, 128), jnp.float32),
             pltpu.VMEM((2, FIELDS, ROWS, 128), jnp.float32),
@@ -440,7 +442,7 @@
         step_kernel,
         name="step",
         out_shape=f32(FIELDS, ROWS, MOST * BX),
-        in_specs=[SMEM] + [VMEM] * 6,
+        in_specs=[VMEM] * 7,
         out_specs=HBM,
         scratch_shapes=[
             pltpu.VMEM((FIELDS, ROWS, MOST * BX), jnp.float32),
@@ -448,7 +450,7 @@
             pltpu.SemaphoreType.DMA((PARTS,)),
         ],
         compiler_params=PARAMS,
-    )(plan, cen, across, slope, sibling, from_above, from_below)
+    )(cen, across, slope, alive, sibling, from_below, from_above)
 
 
 def solution(mesh):

time: 66.2 us -> 63.8 us (0.964)
  the two profiles are of different devices: /device:TPU:1 before, /device:TPU:192 now
where the time goes in v8:
time: 63.8 us; the launch traced here: 63.5 us
  waiting for transfers between devices  32 us (50%)
  starting transfers between devices  20 us (31%)
  Pallas kernels  11.3 us (18%)
    all_to_all x1, waiting for transfers between devices, body(): incoming = lax.all_to_all(outgoing, 'slab', 0, 0, tiled=True)  30.7 us
    all_to_all x1, starting transfers between devices, body(): incoming = lax.all_to_all(outgoing, 'slab', 0, 0, tiled=True)  10.7 us
    ppermute x1, starting transfers between devices, body(): from_below = lax.ppermute(high_rows, 'sub', up)  5.49 us
    pallas_call x1, Pallas kernels, body(): pl.pallas_call(plan_kernel, name='plan', out_shape=i32(8 * 64), in_specs=...  3.72 us
    pallas_call x1, Pallas kernels, body(): pl.pallas_call(pack_kernel, name='pack', out_shape=(f32(SLABS, MSG_ROWS,...  3.01 us
    pallas_call x1, Pallas kernels, body(): pl.pallas_call(middle_kernel, name='middle', out_shape=(f32(*cells), f32(...  2.09 us
    ppermute x1, starting transfers between devices, body(): from_above = lax.ppermute(low_rows, 'sub', [(b, a) for a, b in up])  1.92 us
    ppermute x1, starting transfers between devices, body(): sibling = lax.ppermute(sibling, 'slab', [(i, i ^ 1) for i in range(SLABS)])  1.92 us
  transfers between devices with their start and end apart: 4, of which 2 were waited for; matrix products, arithmetic and copies ran while one was open for 0% of the time, Pallas kernels for 9%

profile of v8, /device:TPU:192, one launch (start us, length us, event | category | flops | bytes accessed | tf_op | source)
XLA Modules:
  0.0 63.5 jit_solution(3529744950395308080)
XLA Ops:
  0.0 3.0 %pack.1 = (f32[64,40,128]{2,1,0:T(8,128)}, s32[64]{0:T(128)}) custom-call(s32[1536]{0:T(1024)} %owner.1, s32[64]{0:T(128)} %counts.1, s32[1536]{0:T(1024)} %pos.1, f32[4,16,1536]{2,1,0:T(8,128)} %fine_in.1, f32[4,8,1536]{2,1,0:T(8,128)} %coarse_in.1), custom_call_target="tpu_custom_call" | custom-call | tf_op jit(solution)/shard_map/pack/pallas_call | solution.py:388
  3.0 0.0 copy-start
  3.0 0.0 copy-start.1
  3.0 0.0 copy-start.2
  3.1 0.0 copy-start.3
  3.1 10.7 %all-to-all-start = ((f32[64,40,128]{2,1,0:T(8,128)}), f32[64,40,128]{2,1,0:T(8,128)S(1)}, u32[]{:S(2)}, u32[]{:S(2)}) async-start(f32[64,40,128]{2,1,0:T(8,128)} %get-tuple-element.15), calls=%async_computation | async-start | bytes 2621440 | tf_op jit(solution)/shard_map/all_to_all | solution.py:405
  13.8 0.0 copy-done
  13.8 0.0 copy-done.1
  13.8 0.0 copy-done.2
  13.8 0.0 copy-done.3
  13.8 3.7 %plan.1 = s32[512]{0:T(512)S(1)} custom-call(s32[1536]{0:T(1024)S(1)} %copy-done, s32[64]{0:T(128)S(1)} %copy-done.2, s32[1536]{0:T(1024)S(1)} %copy-done.1, s32[64]{0:T(128)S(1)} %copy-done.3), custom_call_target="tpu_custom_call" | custom-call | tf_op jit(solution)/shard_map/plan/pallas_call | solution.py:406
  17.6 30.7 %all-to-all-done.inc = f32[64,40,128]{2,1,0:T(8,128)S(1)} async-done(((f32[64,40,128]{2,1,0:T(8,128)}), f32[64,40,128]{2,1,0:T(8,128)S(1)}, u32[]{:S(2)}, u32[]{:S(2)}) %all-to-all-start) | async-done | bytes 1310752 | tf_op jit(solution)/shard_map/all_to_all | solution.py:405
  48.3 1.0 %edges.1 = (f32[24,4,128]{2,1,0:T(4,128)S(1)}, f32[24,4,128]{2,1,0:T(4,128)S(1)}, f32[4,8,128]{2,1,0:T(8,128)S(1)}) custom-call(s32[512]{0:T(512)S(1)} %plan.1, f32[64,40,128]{2,1,0:T(8,128)S(1)} %all-to-all-done.inc), custom_call_target="tpu_custom_call" | custom-call | tf_op jit(solution)/shard_map/edges/pallas_call | solution.py:414
  49.3 5.5 %collective-permute-start.1 = (f32[24,4,128]{2,1,0:T(4,128)S(1)}, f32[24,4,128]{2,1,0:T(4,128)S(1)}, u32[]{:S(2)}, u32[]{:S(2)}) collective-permute-start(f32[24,4,128]{2,1,0:T(4,128)S(1)} %get-tuple-element.21), channel_id=1, source_target_pairs={{0,1},{1,2},{2,3},{3,4},{4,5},{5,6},{6,7},{7,8},{8,9},{9,10},{10,1... | collective-permute-start | bytes 147464 | tf_op jit(solution)/shard_map/ppermute | solution.py:426
  54.8 1.9 %collective-permute-start.2 = (f32[24,4,128]{2,1,0:T(4,128)S(1)}, f32[24,4,128]{2,1,0:T(4,128)S(1)}, u32[]{:S(2)}, u32[]{:S(2)}) collective-permute-start(f32[24,4,128]{2,1,0:T(4,128)S(1)} %get-tuple-element.22), channel_id=1, source_target_pairs={{1,0},{2,1},{3,2},{4,3},{5,4},{6,5},{7,6},{8,7},{9,8},{10,9},{11,1... | collective-permute-start | bytes 147464 | tf_op jit(solution)/shard_map/ppermute | solution.py:425
  56.8 1.9 %collective-permute-start = (f32[4,8,128]{2,1,0:T(8,128)S(1)}, f32[4,8,128]{2,1,0:T(8,128)S(1)}, u32[]{:S(2)}, u32[]{:S(2)}) collective-permute-start(f32[4,8,128]{2,1,0:T(8,128)S(1)} %get-tuple-element.20), channel_id=1, source_target_pairs={{0,12},{12,0},{24,36},{36,24},{48,60},{60,48},{72,84},{84,72},{96,... | collective-permute-start | bytes 49160 | tf_op jit(solution)/shard_map/ppermute | solution.py:424
  58.7 2.1 %middle.1 = (f32[24,4,16,128]{3,2,1,0:T(8,128)S(1)}, f32[24,4,16,128]{3,2,1,0:T(8,128)S(1)}, f32[24,16,128]{2,1,0:T(8,128)S(1)}, f32[24,128]{1,0:T(8,128)S(1)}) custom-call(s32[512]{0:T(512)S(1)} %plan.1, f32[64,40,128]{2,1,0:T(8,128)S(1)} %all-to-all-done.inc), custom_call_target="tpu_custom_call" | custom-call | flops 8000000 | bytes 8000000 | tf_op jit(solution)/shard_map/middle/pallas_call | solution.py:428
  60.8 0.0 collective-permute-done.sibling
  60.8 0.0 collective-permute-done.1.from_below
  60.8 1.2 %collective-permute-done.2.from_above = f32[24,4,128]{2,1,0:T(4,128)S(1)} collective-permute-done((f32[24,4,128]{2,1,0:T(4,128)S(1)}, f32[24,4,128]{2,1,0:T(4,128)S(1)}, u32[]{:S(2)}, u32[]{:S(2)}) %collective-permute-start.2) | collective-permute-done | bytes 49184 | tf_op jit(solution)/shard_map/ppermute | solution.py:425
  62.0 1.5 %step.1 = f32[4,16,3072]{2,1,0:T(8,128)} custom-call(f32[24,4,16,128]{3,2,1,0:T(8,128)S(1)} %get-tuple-element.16.cen, f32[24,4,16,128]{3,2,1,0:T(8,128)S(1)} %get-tuple-element.17.across, f32[24,16,128]{2,1,0:T(8,128)S(1)} %get-tuple-element.18.slope, f32[24,128]{1,0:T(8,128)S(1)} %get-tuple-element.19.alive, ...), custom_call_target="tpu_custom_call" | custom-call | tf_op jit(solution)/shard_map/step/pallas_call | solution.py:441
Async XLA Ops:
  3.0 10.8 %copy-start = (s32[1536]{0:T(1024)S(1)}, s32[1536]{0:T(1024)}, u32[]{:S(2)}) copy-start(s32[1536]{0:T(1024)} %owner.1) | copy-start | bytes 18436
  3.0 10.8 %copy-start.1 = (s32[1536]{0:T(1024)S(1)}, s32[1536]{0:T(1024)}, u32[]{:S(2)}) copy-start(s32[1536]{0:T(1024)} %pos.1) | copy-start | bytes 18436
  3.0 10.8 %copy-start.2 = (s32[64]{0:T(128)S(1)}, s32[64]{0:T(128)}, u32[]{:S(2)}) copy-start(s32[64]{0:T(128)} %counts.1) | copy-start | bytes 772
  3.1 10.8 %copy-start.3 = (s32[64]{0:T(128)S(1)}, s32[64]{0:T(128)}, u32[]{:S(2)}) copy-start(s32[64]{0:T(128)} %get-tuple-element.14.starts) | copy-start | bytes 772
  3.1 45.2 %all-to-all-start = ((f32[64,40,128]{2,1,0:T(8,128)}), f32[64,40,128]{2,1,0:T(8,128)S(1)}, u32[]{:S(2)}, u32[]{:S(2)}) async-start(f32[64,40,128]{2,1,0:T(8,128)} %get-tuple-element.15), calls=%async_computation | async-start | bytes 2621440 | tf_op jit(solution)/shard_map/all_to_all | solution.py:405
  49.3 11.5 %collective-permute-start.1 = (f32[24,4,128]{2,1,0:T(4,128)S(1)}, f32[24,4,128]{2,1,0:T(4,128)S(1)}, u32[]{:S(2)}, u32[]{:S(2)}) collective-permute-start(f32[24,4,128]{2,1,0:T(4,128)S(1)} %get-tuple-element.21), channel_id=1, source_target_pairs={{0,1},{1,2},{2,3},{3,4},{4,5},{5,6},{6,7},{7,8},{8,9},{9,10},{10,1... | collective-permute-start | bytes 147464 | tf_op jit(solution)/shard_map/ppermute | solution.py:426
  54.8 7.2 %collective-permute-start.2 = (f32[24,4,128]{2,1,0:T(4,128)S(1)}, f32[24,4,128]{2,1,0:T(4,128)S(1)}, u32[]{:S(2)}, u32[]{:S(2)}) collective-permute-start(f32[24,4,128]{2,1,0:T(4,128)S(1)} %get-tuple-element.22), channel_id=1, source_target_pairs={{1,0},{2,1},{3,2},{4,3},{5,4},{6,5},{7,6},{8,7},{9,8},{10,9},{11,1... | collective-permute-start | bytes 147464 | tf_op jit(solution)/shard_map/ppermute | solution.py:425
  56.8 4.0 %collective-permute-start = (f32[4,8,128]{2,1,0:T(8,128)S(1)}, f32[4,8,128]{2,1,0:T(8,128)S(1)}, u32[]{:S(2)}, u32[]{:S(2)}) collective-permute-start(f32[4,8,128]{2,1,0:T(8,128)S(1)} %get-tuple-element.20), channel_id=1, source_target_pairs={{0,12},{12,0},{24,36},{36,24},{48,60},{60,48},{72,84},{84,72},{96,... | collective-permute-start | bytes 49160 | tf_op jit(solution)/shard_map/ppermute | solution.py:424

commit v9 on v8

--- a/solution.py
+++ b/solution.py
@@ -105,12 +105,11 @@
 
     def mark(i, words):
         word0, word1 = words
-        k = first_box + i
-        at = pos[jnp.minimum(k, NBOX - 1)] - base
-        good = (k < NBOX) & (at <= PPD)
+        at = pos[jnp.minimum(first_box + i, NBOX - 1)] - base
         bit = jnp.left_shift(jnp.int32(1), at & 31)
-        word0 = word0 | pick(good & (at < 32), bit, 0)
-        word1 = word1 | pick(good & (at >= 32), bit, 0)
+        word = at >> 5
+        word0 = word0 | pick(word == 0, bit, 0)
+        word1 = word1 | pick(word == 1, bit, 0)
         return word0, word1
 
     word0, word1 = lax.fori_loop(0, PPD + 1, mark, (jnp.int32(0), jnp.int32(0)), unroll=49)
@@ -199,7 +198,7 @@
     return lax.fori_loop(0, QUARTER, one, (zero,) * 4, unroll=GU)
 
 
-def edge_kernel(plan, inc, low_rows, high_rows, sibling):
+def edge_kernel(plan, inc, low_rows, high_rows):
     low = lanes((FIELDS, 128)) < 64
 
     def one(t, carry):
@@ -212,6 +211,9 @@
         return carry
 
     lax.fori_loop(0, TILES, one, 0, unroll=24)
+
+
+def sibling_kernel(plan, inc, sibling):
     for n, edges in enumerate(gather_edges(plan, inc, SIB_L, SIB_R)):
         sibling[n] = edges
 
@@ -411,12 +413,20 @@
         out_specs=SMEM,
         compiler_params=PARAMS,
     )(old_owner, new_counts, box_pos, starts)
-    low_rows, high_rows, sibling = pl.pallas_call(
+    low_rows, high_rows = pl.pallas_call(
         edge_kernel,
         name="edges",
-        out_shape=(f32(TILES, FIELDS, 128), f32(TILES, FIELDS, 128), f32(4, 8, 128)),
-        in_specs=[SMEM, VMEM],
-        out_specs=(VMEM, VMEM, VMEM),
+        out_shape=(f32(TILES, FIELDS, 128), f32(TILES, FIELDS, 128)),
+        in_specs=[VMEM, VMEM],
+        out_specs=(VMEM, VMEM),
+        compiler_params=PARAMS,
+    )(plan, incoming)
+    sibling = pl.pallas_call(
+        sibling_kernel,
+        name="sibling",
+        out_shape=f32(4, 8, 128),
+        in_specs=[VMEM, VMEM],
+        out_specs=VMEM,
         compiler_params=PARAMS,
     )(plan, incoming)
     count = lax.axis_size("sub")

time: 63.8 us -> 63 us (0.987)
    pallas_call x1, Pallas kernels: 1.02 us -> 0.23 us  [body(): pl.pallas_call(edge_kernel, name='edges', out_shape=(f32(TILES, FIELDS, 1...]
  transfers between devices with their start and end apart: 4 -> 4, of which waited for: 2 -> 2; matrix products, arithmetic and copies ran while one was open for 0% -> 0% of each run, Pallas kernels for 9% -> 10%
where the time goes in v9:
time: 63 us; the launch traced here: 62.7 us
  waiting for transfers between devices  31.4 us (50%)
  starting transfers between devices  20 us (32%)
  Pallas kernels  11 us (17%)
    all_to_all x1, waiting for transfers between devices, body(): incoming = lax.all_to_all(outgoing, 'slab', 0, 0, tiled=True)  30.7 us
    all_to_all x1, starting transfers between devices, body(): incoming = lax.all_to_all(outgoing, 'slab', 0, 0, tiled=True)  10.7 us
    ppermute x1, starting transfers between devices, body(): from_below = lax.ppermute(high_rows, 'sub', up)  5.49 us
    pallas_call x1, Pallas kernels, body(): pl.pallas_call(plan_kernel, name='plan', out_shape=i32(8 * 64), in_specs=...  3.72 us
    pallas_call x1, Pallas kernels, body(): pl.pallas_call(pack_kernel, name='pack', out_shape=(f32(SLABS, MSG_ROWS,...  2.94 us
    pallas_call x1, Pallas kernels, body(): pl.pallas_call(middle_kernel, name='middle', out_shape=(f32(*cells), f32(...  2.09 us
    ppermute x1, starting transfers between devices, body(): sibling = lax.ppermute(sibling, 'slab', [(i, i ^ 1) for i in range(SLABS)])  1.92 us
    ppermute x1, starting transfers between devices, body(): from_above = lax.ppermute(low_rows, 'sub', [(b, a) for a, b in up])  1.92 us
  transfers between devices with their start and end apart: 4, of which 2 were waited for; matrix products, arithmetic and copies ran while one was open for 0% of the time, Pallas kernels for 10%

profile of v9, /device:TPU:192, one launch (start us, length us, event | category | flops | bytes accessed | tf_op | source)
XLA Modules:
  0.0 62.7 jit_solution(9519852383512880648)
XLA Ops:
  0.0 2.9 %pack.1 = (f32[64,40,128]{2,1,0:T(8,128)}, s32[64]{0:T(128)}) custom-call(s32[1536]{0:T(1024)} %owner.1, s32[64]{0:T(128)} %counts.1, s32[1536]{0:T(1024)} %pos.1, f32[4,16,1536]{2,1,0:T(8,128)} %fine_in.1, f32[4,8,1536]{2,1,0:T(8,128)} %coarse_in.1), custom_call_target="tpu_custom_call" | custom-call | tf_op jit(solution)/shard_map/pack/pallas_call | solution.py:390
  3.0 0.0 copy-start
  3.0 0.0 copy-start.1
  3.0 0.0 copy-start.2
  3.0 0.0 copy-start.3
  3.0 10.7 %all-to-all-start = ((f32[64,40,128]{2,1,0:T(8,128)}), f32[64,40,128]{2,1,0:T(8,128)S(1)}, u32[]{:S(2)}, u32[]{:S(2)}) async-start(f32[64,40,128]{2,1,0:T(8,128)} %get-tuple-element.14), calls=%async_computation | async-start | bytes 2621440 | tf_op jit(solution)/shard_map/all_to_all | solution.py:407
  13.7 0.0 copy-done
  13.7 0.0 copy-done.1
  13.7 0.0 copy-done.2
  13.8 0.0 copy-done.3
  13.8 3.7 %plan.1 = s32[512]{0:T(512)S(1)} custom-call(s32[1536]{0:T(1024)S(1)} %copy-done, s32[64]{0:T(128)S(1)} %copy-done.2, s32[1536]{0:T(1024)S(1)} %copy-done.1, s32[64]{0:T(128)S(1)} %copy-done.3), custom_call_target="tpu_custom_call" | custom-call | tf_op jit(solution)/shard_map/plan/pallas_call | solution.py:408
  17.5 30.7 %all-to-all-done.inc = f32[64,40,128]{2,1,0:T(8,128)S(1)} async-done(((f32[64,40,128]{2,1,0:T(8,128)}), f32[64,40,128]{2,1,0:T(8,128)S(1)}, u32[]{:S(2)}, u32[]{:S(2)}) %all-to-all-start) | async-done | bytes 1310752 | tf_op jit(solution)/shard_map/all_to_all | solution.py:407
  48.2 0.2 edges.1
  48.5 5.5 %collective-permute-start.1 = (f32[24,4,128]{2,1,0:T(4,128)S(1)}, f32[24,4,128]{2,1,0:T(4,128)S(1)}, u32[]{:S(2)}, u32[]{:S(2)}) collective-permute-start(f32[24,4,128]{2,1,0:T(4,128)S(1)} %get-tuple-element.19), channel_id=1, source_target_pairs={{0,1},{1,2},{2,3},{3,4},{4,5},{5,6},{6,7},{7,8},{8,9},{9,10},{10,1... | collective-permute-start | bytes 147464 | tf_op jit(solution)/shard_map/ppermute | solution.py:436
  54.0 1.9 %collective-permute-start.2 = (f32[24,4,128]{2,1,0:T(4,128)S(1)}, f32[24,4,128]{2,1,0:T(4,128)S(1)}, u32[]{:S(2)}, u32[]{:S(2)}) collective-permute-start(f32[24,4,128]{2,1,0:T(4,128)S(1)} %get-tuple-element.20), channel_id=1, source_target_pairs={{1,0},{2,1},{3,2},{4,3},{5,4},{6,5},{7,6},{8,7},{9,8},{10,9},{11,1... | collective-permute-start | bytes 147464 | tf_op jit(solution)/shard_map/ppermute | solution.py:435
  55.9 0.5 sibling.1
  56.4 1.9 %collective-permute-start = (f32[4,8,128]{2,1,0:T(8,128)S(1)}, f32[4,8,128]{2,1,0:T(8,128)S(1)}, u32[]{:S(2)}, u32[]{:S(2)}) collective-permute-start(f32[4,8,128]{2,1,0:T(8,128)S(1)} %sibling.1), channel_id=1, source_target_pairs={{0,12},{12,0},{24,36},{36,24},{48,60},{60,48},{72,84},{84,72},{96,... | collective-permute-start | bytes 49160 | tf_op jit(solution)/shard_map/ppermute | solution.py:434
  58.3 2.1 %middle.1 = (f32[24,4,16,128]{3,2,1,0:T(8,128)S(1)}, f32[24,4,16,128]{3,2,1,0:T(8,128)S(1)}, f32[24,16,128]{2,1,0:T(8,128)S(1)}, f32[24,128]{1,0:T(8,128)S(1)}) custom-call(s32[512]{0:T(512)S(1)} %plan.1, f32[64,40,128]{2,1,0:T(8,128)S(1)} %all-to-all-done.inc), custom_call_target="tpu_custom_call" | custom-call | flops 8000000 | bytes 8000000 | tf_op jit(solution)/shard_map/middle/pallas_call | solution.py:438
  60.4 0.0 collective-permute-done.sibling
  60.5 0.0 collective-permute-done.1.from_below
  60.5 0.7 %collective-permute-done.2.from_above = f32[24,4,128]{2,1,0:T(4,128)S(1)} collective-permute-done((f32[24,4,128]{2,1,0:T(4,128)S(1)}, f32[24,4,128]{2,1,0:T(4,128)S(1)}, u32[]{:S(2)}, u32[]{:S(2)}) %collective-permute-start.2) | collective-permute-done | bytes 49184 | tf_op jit(solution)/shard_map/ppermute | solution.py:435
  61.2 1.5 %step.1 = f32[4,16,3072]{2,1,0:T(8,128)} custom-call(f32[24,4,16,128]{3,2,1,0:T(8,128)S(1)} %get-tuple-element.15.cen, f32[24,4,16,128]{3,2,1,0:T(8,128)S(1)} %get-tuple-element.16.across, f32[24,16,128]{2,1,0:T(8,128)S(1)} %get-tuple-element.17.slope, f32[24,128]{1,0:T(8,128)S(1)} %get-tuple-element.18.alive, ...), custom_call_target="tpu_custom_call" | custom-call | tf_op jit(solution)/shard_map/step/pallas_call | solution.py:451
Async XLA Ops:
  3.0 10.8 %copy-start = (s32[1536]{0:T(1024)S(1)}, s32[1536]{0:T(1024)}, u32[]{:S(2)}) copy-start(s32[1536]{0:T(1024)} %owner.1) | copy-start | bytes 18436
  3.0 10.8 %copy-start.1 = (s32[1536]{0:T(1024)S(1)}, s32[1536]{0:T(1024)}, u32[]{:S(2)}) copy-start(s32[1536]{0:T(1024)} %pos.1) | copy-start | bytes 18436
  3.0 10.8 %copy-start.2 = (s32[64]{0:T(128)S(1)}, s32[64]{0:T(128)}, u32[]{:S(2)}) copy-start(s32[64]{0:T(128)} %counts.1) | copy-start | bytes 772
  3.0 10.8 %copy-start.3 = (s32[64]{0:T(128)S(1)}, s32[64]{0:T(128)}, u32[]{:S(2)}) copy-start(s32[64]{0:T(128)} %get-tuple-element.13.starts) | copy-start | bytes 772
  3.0 45.2 %all-to-all-start = ((f32[64,40,128]{2,1,0:T(8,128)}), f32[64,40,128]{2,1,0:T(8,128)S(1)}, u32[]{:S(2)}, u32[]{:S(2)}) async-start(f32[64,40,128]{2,1,0:T(8,128)} %get-tuple-element.14), calls=%async_computation | async-start | bytes 2621440 | tf_op jit(solution)/shard_map/all_to_all | solution.py:407
  48.5 12.0 %collective-permute-start.1 = (f32[24,4,128]{2,1,0:T(4,128)S(1)}, f32[24,4,128]{2,1,0:T(4,128)S(1)}, u32[]{:S(2)}, u32[]{:S(2)}) collective-permute-start(f32[24,4,128]{2,1,0:T(4,128)S(1)} %get-tuple-element.19), channel_id=1, source_target_pairs={{0,1},{1,2},{2,3},{3,4},{4,5},{5,6},{6,7},{7,8},{8,9},{9,10},{10,1... | collective-permute-start | bytes 147464 | tf_op jit(solution)/shard_map/ppermute | solution.py:436
  54.0 7.2 %collective-permute-start.2 = (f32[24,4,128]{2,1,0:T(4,128)S(1)}, f32[24,4,128]{2,1,0:T(4,128)S(1)}, u32[]{:S(2)}, u32[]{:S(2)}) collective-permute-start(f32[24,4,128]{2,1,0:T(4,128)S(1)} %get-tuple-element.20), channel_id=1, source_target_pairs={{1,0},{2,1},{3,2},{4,3},{5,4},{6,5},{7,6},{8,7},{9,8},{10,9},{11,1... | collective-permute-start | bytes 147464 | tf_op jit(solution)/shard_map/ppermute | solution.py:435
  56.4 4.0 %collective-permute-start = (f32[4,8,128]{2,1,0:T(8,128)S(1)}, f32[4,8,128]{2,1,0:T(8,128)S(1)}, u32[]{:S(2)}, u32[]{:S(2)}) collective-permute-start(f32[4,8,128]{2,1,0:T(8,128)S(1)} %sibling.1), channel_id=1, source_target_pairs={{0,12},{12,0},{24,36},{36,24},{48,60},{60,48},{72,84},{84,72},{96,... | collective-permute-start | bytes 49160 | tf_op jit(solution)/shard_map/ppermute | solution.py:434

commit v10 on v9

--- a/solution.py
+++ b/solution.py
@@ -45,7 +45,7 @@
 
 
 def pack_kernel(
-    owner_in, counts_in, pos_in, fine_in, coarse_in, out, starts, owner, counts, pos, fine, coarse, packed, sems
+    owner_in, counts_in, pos_in, fine_in, coarse_in, out, owner, counts, pos, fine, coarse, packed, sems
 ):
     copies = [
         pltpu.make_async_copy(a, b, sems.at[n])
@@ -127,7 +127,6 @@
     residue = lax.fori_loop(0, SLABS, find, jnp.int32(0), unroll=64)
 
     def fill(b, start):
-        starts[b] = start
         k = start - 1 + ((residue - (start - 1)) & 63)
         slot = jnp.clip(k >> 6, 0, BOX_DEV - 1)
         out[b, 0:BOX_ROWS] = packed[slot]
@@ -136,10 +135,16 @@
     lax.fori_loop(0, SLABS, fill, jnp.int32(0), unroll=32)
 
 
-def plan_kernel(owner, counts, pos, starts, plan):
+def plan_kernel(owner, counts, pos, plan):
     me = lax.axis_index("slab")
     mine = me & 1
-    start = starts[me]
+
+    def total(b, sums):
+        start, other = sums
+        n = counts[b]
+        return start + pick(b < me, n, 0), other + pick(b < (me ^ 1), n, 0)
+
+    start, other = lax.fori_loop(0, SLABS, total, (jnp.int32(0), jnp.int32(0)), unroll=16)
     plan[MISC * 64] = start
     plan[MISC * 64 + 1] = counts[me]
 
@@ -176,7 +181,7 @@
         lax.fori_loop(0, MOST, one, 0, unroll=2)
 
     ghosts(start, OWN_L, OWN_R, True)
-    ghosts(starts[me ^ 1], SIB_L, SIB_R, False)
+    ghosts(other, SIB_L, SIB_R, False)
 
 
 def gather_edges(plan, inc, left, right):
@@ -387,12 +392,12 @@
 
 
 def body(fine_old, coarse, box_pos, old_owner, new_counts):
-    outgoing, starts = pl.pallas_call(
+    outgoing = pl.pallas_call(
         pack_kernel,
         name="pack",
-        out_shape=(f32(SLABS, MSG_ROWS, 128), i32(SLABS)),
+        out_shape=f32(SLABS, MSG_ROWS, 128),
         in_specs=[HBM] * 5,
-        out_specs=(VMEM, SMEM),
+        out_specs=VMEM,
         scratch_shapes=[
             pltpu.SMEM((NBOX,), jnp.int32),
             pltpu.SMEM((SLABS,), jnp.int32),
@@ -409,10 +414,10 @@
         plan_kernel,
         name="plan",
         out_shape=i32(8 * 64),
-        in_specs=[SMEM] * 4,
+        in_specs=[SMEM] * 3,
         out_specs=SMEM,
         compiler_params=PARAMS,
-    )(old_owner, new_counts, box_pos, starts)
+    )(old_owner, new_counts, box_pos)
     low_rows, high_rows = pl.pallas_call(
         edge_kernel,
         name="edges",

time: 63 us -> 62.9 us (level)
  no operation moved by 1% of the time
where the time goes in v10:
time: 62.9 us; the launch traced here: 62.6 us
  waiting for transfers between devices  31.3 us (50%)
  starting transfers between devices  20 us (32%)
  Pallas kernels  11.1 us (18%)
    all_to_all x1, waiting for transfers between devices, body(): incoming = lax.all_to_all(outgoing, 'slab', 0, 0, tiled=True)  30.6 us
    all_to_all x1, starting transfers between devices, body(): incoming = lax.all_to_all(outgoing, 'slab', 0, 0, tiled=True)  10.7 us
    ppermute x1, starting transfers between devices, body(): from_below = lax.ppermute(high_rows, 'sub', up)  5.49 us
    pallas_call x1, Pallas kernels, body(): pl.pallas_call(plan_kernel, name='plan', out_shape=i32(8 * 64), in_specs=...  3.87 us
    pallas_call x1, Pallas kernels, body(): pl.pallas_call(pack_kernel, name='pack', out_shape=f32(SLABS, MSG_ROWS, 1...  2.89 us
    pallas_call x1, Pallas kernels, body(): pl.pallas_call(middle_kernel, name='middle', out_shape=(f32(*cells), f32(...  2.09 us
    ppermute x1, starting transfers between devices, body(): sibling = lax.ppermute(sibling, 'slab', [(i, i ^ 1) for i in range(SLABS)])  1.92 us
    ppermute x1, starting transfers between devices, body(): from_above = lax.ppermute(low_rows, 'sub', [(b, a) for a, b in up])  1.92 us
  transfers between devices with their start and end apart: 4, of which 2 were waited for; matrix products, arithmetic and copies ran while one was open for 0% of the time, Pallas kernels for 10%

profile of v10, /device:TPU:192, one launch (start us, length us, event | category | flops | bytes accessed | tf_op | source)
XLA Modules:
  0.0 62.6 jit_solution(8589708540695638866)
XLA Ops:
  0.0 2.9 %pack.1 = f32[64,40,128]{2,1,0:T(8,128)} custom-call(s32[1536]{0:T(1024)} %owner_in.1, s32[64]{0:T(128)} %counts_in.1, s32[1536]{0:T(1024)} %pos_in.1, f32[4,16,1536]{2,1,0:T(8,128)} %fine_in.1, f32[4,8,1536]{2,1,0:T(8,128)} %coarse_in.1), custom_call_target="tpu_custom_call" | custom-call | tf_op jit(solution)/shard_map/pack/pallas_call | solution.py:395
  2.9 0.0 copy-start
  2.9 0.0 copy-start.1
  2.9 0.0 copy-start.2
  2.9 10.7 %all-to-all-start = ((f32[64,40,128]{2,1,0:T(8,128)}), f32[64,40,128]{2,1,0:T(8,128)S(1)}, u32[]{:S(2)}, u32[]{:S(2)}) async-start(f32[64,40,128]{2,1,0:T(8,128)} %pack.1), calls=%async_computation | async-start | bytes 2621440 | tf_op jit(solution)/shard_map/all_to_all | solution.py:412
  13.7 0.0 copy-done
  13.7 0.0 copy-done.1
  13.7 0.0 copy-done.2
  13.7 3.9 %plan.1 = s32[512]{0:T(512)S(1)} custom-call(s32[1536]{0:T(1024)S(1)} %copy-done, s32[64]{0:T(128)S(1)} %copy-done.2, s32[1536]{0:T(1024)S(1)} %copy-done.1), custom_call_target="tpu_custom_call" | custom-call | tf_op jit(solution)/shard_map/plan/pallas_call | solution.py:413
  17.6 30.6 %all-to-all-done.inc = f32[64,40,128]{2,1,0:T(8,128)S(1)} async-done(((f32[64,40,128]{2,1,0:T(8,128)}), f32[64,40,128]{2,1,0:T(8,128)S(1)}, u32[]{:S(2)}, u32[]{:S(2)}) %all-to-all-start) | async-done | bytes 1310752 | tf_op jit(solution)/shard_map/all_to_all | solution.py:412
  48.2 0.2 edges.1
  48.4 5.5 %collective-permute-start.1 = (f32[24,4,128]{2,1,0:T(4,128)S(1)}, f32[24,4,128]{2,1,0:T(4,128)S(1)}, u32[]{:S(2)}, u32[]{:S(2)}) collective-permute-start(f32[24,4,128]{2,1,0:T(4,128)S(1)} %get-tuple-element.15), channel_id=1, source_target_pairs={{0,1},{1,2},{2,3},{3,4},{4,5},{5,6},{6,7},{7,8},{8,9},{9,10},{10,1... | collective-permute-start | bytes 147464 | tf_op jit(solution)/shard_map/ppermute | solution.py:441
  53.9 1.9 %collective-permute-start.2 = (f32[24,4,128]{2,1,0:T(4,128)S(1)}, f32[24,4,128]{2,1,0:T(4,128)S(1)}, u32[]{:S(2)}, u32[]{:S(2)}) collective-permute-start(f32[24,4,128]{2,1,0:T(4,128)S(1)} %get-tuple-element.16), channel_id=1, source_target_pairs={{1,0},{2,1},{3,2},{4,3},{5,4},{6,5},{7,6},{8,7},{9,8},{10,9},{11,1... | collective-permute-start | bytes 147464 | tf_op jit(solution)/shard_map/ppermute | solution.py:440
  55.8 0.5 sibling.1
  56.4 1.9 %collective-permute-start = (f32[4,8,128]{2,1,0:T(8,128)S(1)}, f32[4,8,128]{2,1,0:T(8,128)S(1)}, u32[]{:S(2)}, u32[]{:S(2)}) collective-permute-start(f32[4,8,128]{2,1,0:T(8,128)S(1)} %sibling.1), channel_id=1, source_target_pairs={{0,12},{12,0},{24,36},{36,24},{48,60},{60,48},{72,84},{84,72},{96,... | collective-permute-start | bytes 49160 | tf_op jit(solution)/shard_map/ppermute | solution.py:439
  58.3 2.1 %middle.1 = (f32[24,4,16,128]{3,2,1,0:T(8,128)S(1)}, f32[24,4,16,128]{3,2,1,0:T(8,128)S(1)}, f32[24,16,128]{2,1,0:T(8,128)S(1)}, f32[24,128]{1,0:T(8,128)S(1)}) custom-call(s32[512]{0:T(512)S(1)} %plan.1, f32[64,40,128]{2,1,0:T(8,128)S(1)} %all-to-all-done.inc), custom_call_target="tpu_custom_call" | custom-call | flops 8000000 | bytes 8000000 | tf_op jit(solution)/shard_map/middle/pallas_call | solution.py:443
  60.4 0.0 collective-permute-done.sibling
  60.4 0.0 collective-permute-done.1.from_below
  60.4 0.7 %collective-permute-done.2.from_above = f32[24,4,128]{2,1,0:T(4,128)S(1)} collective-permute-done((f32[24,4,128]{2,1,0:T(4,128)S(1)}, f32[24,4,128]{2,1,0:T(4,128)S(1)}, u32[]{:S(2)}, u32[]{:S(2)}) %collective-permute-start.2) | collective-permute-done | bytes 49184 | tf_op jit(solution)/shard_map/ppermute | solution.py:440
  61.1 1.5 %step.1 = f32[4,16,3072]{2,1,0:T(8,128)} custom-call(f32[24,4,16,128]{3,2,1,0:T(8,128)S(1)} %get-tuple-element.11.cen, f32[24,4,16,128]{3,2,1,0:T(8,128)S(1)} %get-tuple-element.12.across, f32[24,16,128]{2,1,0:T(8,128)S(1)} %get-tuple-element.13.slope, f32[24,128]{1,0:T(8,128)S(1)} %get-tuple-element.14.alive, ...), custom_call_target="tpu_custom_call" | custom-call | tf_op jit(solution)/shard_map/step/pallas_call | solution.py:456
Async XLA Ops:
  2.9 10.8 %copy-start = (s32[1536]{0:T(1024)S(1)}, s32[1536]{0:T(1024)}, u32[]{:S(2)}) copy-start(s32[1536]{0:T(1024)} %owner_in.1) | copy-start | bytes 18436
  2.9 10.8 %copy-start.1 = (s32[1536]{0:T(1024)S(1)}, s32[1536]{0:T(1024)}, u32[]{:S(2)}) copy-start(s32[1536]{0:T(1024)} %pos_in.1) | copy-start | bytes 18436
  2.9 10.8 %copy-start.2 = (s32[64]{0:T(128)S(1)}, s32[64]{0:T(128)}, u32[]{:S(2)}) copy-start(s32[64]{0:T(128)} %counts_in.1) | copy-start | bytes 772
  2.9 45.2 %all-to-all-start = ((f32[64,40,128]{2,1,0:T(8,128)}), f32[64,40,128]{2,1,0:T(8,128)S(1)}, u32[]{:S(2)}, u32[]{:S(2)}) async-start(f32[64,40,128]{2,1,0:T(8,128)} %pack.1), calls=%async_computation | async-start | bytes 2621440 | tf_op jit(solution)/shard_map/all_to_all | solution.py:412
  48.4 12.0 %collective-permute-start.1 = (f32[24,4,128]{2,1,0:T(4,128)S(1)}, f32[24,4,128]{2,1,0:T(4,128)S(1)}, u32[]{:S(2)}, u32[]{:S(2)}) collective-permute-start(f32[24,4,128]{2,1,0:T(4,128)S(1)} %get-tuple-element.15), channel_id=1, source_target_pairs={{0,1},{1,2},{2,3},{3,4},{4,5},{5,6},{6,7},{7,8},{8,9},{9,10},{10,1... | collective-permute-start | bytes 147464 | tf_op jit(solution)/shard_map/ppermute | solution.py:441
  53.9 7.2 %collective-permute-start.2 = (f32[24,4,128]{2,1,0:T(4,128)S(1)}, f32[24,4,128]{2,1,0:T(4,128)S(1)}, u32[]{:S(2)}, u32[]{:S(2)}) collective-permute-start(f32[24,4,128]{2,1,0:T(4,128)S(1)} %get-tuple-element.16), channel_id=1, source_target_pairs={{1,0},{2,1},{3,2},{4,3},{5,4},{6,5},{7,6},{8,7},{9,8},{10,9},{11,1... | collective-permute-start | bytes 147464 | tf_op jit(solution)/shard_map/ppermute | solution.py:440
  56.4 4.0 %collective-permute-start = (f32[4,8,128]{2,1,0:T(8,128)S(1)}, f32[4,8,128]{2,1,0:T(8,128)S(1)}, u32[]{:S(2)}, u32[]{:S(2)}) collective-permute-start(f32[4,8,128]{2,1,0:T(8,128)S(1)} %sibling.1), channel_id=1, source_target_pairs={{0,12},{12,0},{24,36},{36,24},{48,60},{60,48},{72,84},{84,72},{96,... | collective-permute-start | bytes 49160 | tf_op jit(solution)/shard_map/ppermute | solution.py:439
